TPU v7x, 1024 devices: a whole 4x4x32 slice. The times are simulated.
1024 devices in a mesh: tile: 32 (over z_lo, core), spec: 32 (over y, z_hi, x).
Axes of the slice: x: 4, y: 4, z: 32 (z_hi: 2, z_lo: 16; z = z_hi * 16 + z_lo), core: 2. Of those that a mesh axis runs over, the one named last changes fastest.
Arguments:
- object_field: float32 [2, 8192, 512], P(None, 'tile'), may hold values from -5 to 5
- probe_modes: float32 [32, 2, 256, 256], P('spec'), may hold values from -5 to 5
- amplitude: float32 [128, 256, 256], P('tile'), may hold values from 1 to 8
- positions: int32 [128, 2], P('tile'), may hold values from 0 to 256, as said below
Outputs:
- updated_object: float32 [2, 8192, 512], P(None, ('tile', 'spec'))
Inputs may be any that keep to these rules, and one draw needn't show every extreme that they name: positions[j, 0] lies in 0 to 255 and positions[j, 1] in 0 to 256; both ends of both ranges occur.
All inputs are finite; a program needn't handle non-finite values.
Results may differ from a plain program's by a relative error of at most 0.00005.
Values sent between devices are 32-bit elements; how exact they have to be, the bound alone decides.
No kernel may reach another device: no remote copies, remote signals or barrier semaphores. Data moves between devices by JAX's collectives and lax.ppermute only.
A program may use at most 32 MiB of HBM per device.

v0:
```python
import math

import jax
import jax.numpy as jnp
from jax import lax
from jax.sharding import PartitionSpec as P


def passed_along(value, axis, steps):
    count = lax.axis_size(axis)
    pairs = [(source, (source + steps) % count) for source in range(count)]
    return lax.ppermute(value, axis, pairs)


def tables(side, direction):
    freq_idx = lax.broadcasted_iota(jnp.int32, (side, side), 0)
    sample_idx = lax.broadcasted_iota(jnp.int32, (side, side), 1)
    phase = (freq_idx * sample_idx % side).astype(jnp.float32)
    angle = phase * (2.0 * math.pi / side)
    factor = 1.0 / math.sqrt(side)
    return (jnp.cos(angle) * factor, direction * jnp.sin(angle) * factor)


def transform(real_part, imag_part, table_re, table_im):
    exact = lax.Precision.HIGHEST
    left_re = jnp.einsum("kn,bnj->bkj", table_re, real_part, precision=exact) - jnp.einsum(
        "kn,bnj->bkj", table_im, imag_part, precision=exact
    )
    left_im = jnp.einsum("kn,bnj->bkj", table_re, imag_part, precision=exact) + jnp.einsum(
        "kn,bnj->bkj", table_im, real_part, precision=exact
    )
    out_re = jnp.einsum("bkn,nj->bkj", left_re, table_re, precision=exact) - jnp.einsum(
        "bkn,nj->bkj", left_im, table_im, precision=exact
    )
    out_im = jnp.einsum("bkn,nj->bkj", left_re, table_im, precision=exact) + jnp.einsum(
        "bkn,nj->bkj", left_im, table_re, precision=exact
    )
    return (out_re, out_im)


def body(object_field, probe_modes, amplitude, positions):
    strip_rows = object_field.shape[1]
    probe_side = probe_modes.shape[2]
    patterns = positions.shape[0]
    mode_count = lax.axis_size("spec")
    below_strip = passed_along(object_field, "tile", -1)
    extended = jnp.concatenate([object_field, below_strip], 1)
    probe_re = probe_modes[0, 0]
    probe_im = probe_modes[0, 1]

    def window(position):
        return lax.dynamic_slice(
            extended, (0, position[0], position[1]), (2, probe_side, probe_side)
        )

    patches = jax.vmap(window)(positions)
    exit_re = probe_re * patches[:, 0] - probe_im * patches[:, 1]
    exit_im = probe_re * patches[:, 1] + probe_im * patches[:, 0]
    forward_re, forward_im = tables(probe_side, -1.0)
    far_re, far_im = transform(exit_re, exit_im, forward_re, forward_im)
    intensity = far_re * far_re + far_im * far_im
    floor_term = 0.05 * mode_count
    summed = lax.psum(intensity, "spec")
    scaling = amplitude / jnp.sqrt(summed + floor_term)
    inverse_re, inverse_im = tables(probe_side, 1.0)
    revised_re, revised_im = transform(far_re * scaling, far_im * scaling, inverse_re, inverse_im)
    delta_re = revised_re - exit_re
    delta_im = revised_im - exit_im
    contrib_re = probe_re * delta_re + probe_im * delta_im
    contrib_im = probe_re * delta_im - probe_im * delta_re

    def accumulate(pattern, gradient):
        row_start = positions[pattern, 0]
        col_start = positions[pattern, 1]
        addition = jnp.stack([contrib_re[pattern], contrib_im[pattern]])
        current = lax.dynamic_slice(
            gradient, (0, row_start, col_start), (2, probe_side, probe_side)
        )
        return lax.dynamic_update_slice(gradient, current + addition, (0, row_start, col_start))

    gradient = lax.fori_loop(0, patterns, accumulate, jnp.zeros(extended.shape, jnp.float32))
    upper_part = gradient[:, :strip_rows]
    lower_part = gradient[:, strip_rows:]
    arrived = passed_along(lower_part, "tile", 1)
    total_gradient = lax.psum_scatter(upper_part + arrived, "spec", scatter_dimension=1, tiled=True)
    own_rows = strip_rows // mode_count
    own_share = lax.dynamic_slice_in_dim(
        object_field, lax.axis_index("spec") * own_rows, own_rows, 1
    )
    return own_share + 0.5 * total_gradient / mode_count


def solution(mesh):
    placed = (
        P(None, "tile", None),
        P("spec", None, None, None),
        P("tile", None, None),
        P("tile", None),
    )
    return jax.shard_map(
        body, mesh=mesh, in_specs=placed, out_specs=P(None, ("tile", "spec"), None), check_vma=False
    )
```

profile of v0, /device:TPU:32, one launch (start us, length us, event | category | flops | bytes accessed | tf_op | source)
XLA Modules:
  0.0 1561.5 jit_solution(16923591692176318535)
XLA Ops:
  6.5 1.9 collective-permute-start
  10.6 10.5 collective-permute-done
  22.8 11.7 while.15
  23.5 2.3 bitcast_dynamic-update-slice_fusion.2
  26.4 2.3 bitcast_dynamic-update-slice_fusion.2
  29.3 2.3 bitcast_dynamic-update-slice_fusion.2
  32.3 2.3 bitcast_dynamic-update-slice_fusion.2
  36.3 2.6 fusion.33
  38.9 2.6 fusion.37
  41.6 2.6 fusion.5
  44.2 2.7 fusion.35
  46.9 3.1 fusion.22
  50.0 2.6 fusion.4
  52.7 2.7 convolution_subtract_fusion.2
  55.4 4.1 multiply_add_fusion.1
  59.8 903.4 %all-reduce.2.cloned.1.call-done = f32[4,256,256]{2,1,0:T(8,128)} async-done(((f32[4,256,256]{2,1,0:T(8,128)}), f32[4,256,256]{2,1,0:T(8,128)}) %all-reduce.2.cloned.1.call-update) | async-done | bytes 1048592 | tf_op jit(solution)/shard_map/psum | solution.py:63
  964.9 2.7 fusion.12
  967.6 2.7 fusion.8
  970.3 2.7 fusion.3
  973.0 2.7 fusion.17
  975.7 2.9 fusion.29
  978.6 2.7 fusion.2
  981.3 2.8 fusion
  984.1 4.3 multiply_subtract_fusion
  989.1 57.3 %while.14 = (s32[]{:T(128)}, f32[2,512,512]{2,1,0:T(8,128)S(1)}, s32[4,2]{0,1:T(2,128)S(1)}, f32[4,256,256]{2,1,0:T(8,128)}, f32[4,256,256]{2,1,0:T(8,128)}, /*index=5*/s32[]{:T(128)}, s32[]{:T(128)}, s32[]{:T(128)}) while((s32[]{:T(128)}, f32[2,512,512]{2,1,0:T(8,128)S(1)}, s32[4,2]{0,1:T(2,128)S(1)}, f32[4,256,256]{2,1,0:T(8,128)}, ...), condition=%wide.region_2.3_spmd, body=%wide.region_1.2_spmd.sunk | while | flops 262152 | bytes 3670205 | solution.py:81
  994.8 8.7 dynamic_update_slice.8
  1009.3 9.3 dynamic_update_slice.8
  1024.3 7.8 dynamic_update_slice.8
  1037.8 8.6 dynamic_update_slice.8
  1046.5 1.9 collective-permute-start.1
  1048.4 14.2 collective-permute-done.1
  1063.8 489.1 %reduce-scatter.2.cloned.1.call-done = f32[2,8,512]{2,1,0:T(8,128)} async-done(((f32[2,256,512]{2,1,0:T(8,128)}), f32[2,8,512]{2,1,0:T(8,128)}) %reduce-scatter.2.cloned.1.call-update) | async-done | bytes 32784 | tf_op jit(solution)/shard_map/reduce_scatter | solution.py:85
  (47 shorter events, 21.3 us)
Async XLA Ops:
  6.5 956.7 %all-reduce.2.cloned.1.call-start = ((), (), s32[]{:S(2)}) async-start(), calls=%async_computation.1 | async-start | bytes 2097152 | tf_op jit(solution)/shard_map/psum | solution.py:63
  6.5 14.5 collective-permute-start
  10.6 24.0 %copy-start.1 = (f32[256,256]{1,0:T(8,128)}, f32[256,256]{1,0:T(8,128)S(1)}, u32[]{:S(2)}) copy-start(f32[256,256]{1,0:T(8,128)S(1)} %get-tuple-element.137) | copy-start | bytes 786436
  59.5 1493.4 %reduce-scatter.2.cloned.1.call-start = ((), (), s32[]{:S(2)}) async-start(), calls=%async_computation.2 | async-start | bytes 1081344 | tf_op jit(solution)/shard_map/reduce_scatter | solution.py:85
  964.9 2.7 copy-start
  981.3 2.8 copy-start.2
  988.4 0.7 copy-start.3
  1046.5 16.1 %collective-permute-start.1 = (f32[2,256,512]{2,1,0:T(8,128)S(1)}, f32[2,256,512]{2,1,0:T(8,128)S(1)}, u32[]{:S(2)}, u32[]{:S(2)}) collective-permute-start(f32[2,256,512]{2,1,0:T(8,128)S(1)} %slice.33), channel_id=1, source_target_pairs={{0,32},{32,64},{64,96},{96,128},{128,160},{160,192},{192,224},{224... | collective-permute-start | bytes 3145736 | tf_op jit(solution)/shard_map/ppermute | solution.py:12
Sparse Core Ops, SparseCore 0:
  59.7 903.5 all-reduce.1
  1063.9 488.9 reduce-scatter.1
where the time goes:
time: 1570 us; the launch traced here: 1560 us
  waiting for transfers between devices  1420 us (90%)
  local copies, waits for them, and re-layouts  55.8 us (4%)
  matrix products  46.6 us (3%)
    psum x1, waiting for transfers between devices, body(): summed = lax.psum(intensity, 'spec')  903 us
    reduce_scatter x1, waiting for transfers between devices, body(): lax.psum_scatter(upper_part + arrived, 'spec', scatter_dimension=1, tiled...  489 us
    dynamic_update_slice x4, local copies, waits for them, and re-layouts, accumulate(): lax.dynamic_update_slice(gradient, current + addition, (0, row_start, col...  34.4 us
  transfers between devices with their start and end apart: 4, of which 4 were waited for; matrix products, arithmetic and copies ran while one was open for 0% of the time, Pallas kernels for 0%

commit v1 on v0

v1 whole, which is shorter than its diff:
```python
import math

import jax
import jax.numpy as jnp
import ml_dtypes
import numpy as np
from jax import lax
from jax.experimental import pallas as pl
from jax.experimental.pallas import tpu as pltpu
from jax.sharding import Mesh, PartitionSpec as P

AXES = ("zlo", "core", "y", "zhi", "x")
SIZES = (16, 2, 4, 2, 4)
PLANE = ("y", "x")
SIDE = 256
PLANE_SIZE = 16
SPAN = SIDE + 8


def pairs_of(move):
    count = math.prod(SIZES)
    pairs = []
    for source in range(count):
        place = np.unravel_index(source, SIZES)
        target = np.ravel_multi_index(move(*(int(v) for v in place)), SIZES)
        pairs.append((source, int(target)))
    return pairs


def along_ring(steps):
    def move(zlo, core, y, zhi, x):
        chip, core = divmod(((zhi * 16 + zlo) * 2 + core + steps) % 64, 2)
        return chip % 16, core, y, chip // 16, x

    return move


def other_half(zlo, core, y, zhi, x):
    return zlo, core, y, 1 - zhi, x


def moved(value, move):
    return lax.ppermute(value, AXES, pairs_of(move))


def tables():
    index = np.arange(SIDE)
    angle = (np.outer(index, index) % SIDE) * (2.0 * math.pi / SIDE)
    cos, sin = np.cos(angle) / 16.0, np.sin(angle) / 16.0
    forward = np.block([[cos, sin], [-sin, cos]])
    out = []
    for table in (forward, forward.T):
        high = table.astype(np.float32).astype(ml_dtypes.bfloat16)
        low = (table - high.astype(np.float64)).astype(np.float32)
        out += [high, low.astype(ml_dtypes.bfloat16)]
    return out


def halves(value):
    high = value.astype(jnp.bfloat16)
    return high, (value - high.astype(jnp.float32)).astype(jnp.bfloat16)


def product(a_high, a_low, b_high, b_low):
    dot = lambda a, b: jnp.dot(a, b, preferred_element_type=jnp.float32)
    return dot(a_high, b_high) + (dot(a_high, b_low) + dot(a_low, b_high))


def transform(real, imag, left, right):
    high, low = halves(jnp.concatenate([real, imag], 0))
    part = product(left[0][...], left[1][...], high, low)
    high, low = halves(jnp.concatenate([part[:SIDE], part[SIDE:]], 1))
    out = product(high, low, right[0][...], right[1][...])
    return out[:, :SIDE], out[:, SIDE:]


def forward_kernel(pos, own, halo, probe, fh, fl, ih, il, far, intensity, ext):
    ext[:, :SIDE] = own[...]
    ext[:, SIDE:] = halo[...]

    def pattern(p, carry):
        row, col = pos[p, 0], pos[p, 1]
        base = pl.multiple_of(row // 8 * 8, 8)
        left = lax.rem(512 - col, 512)
        up = lax.rem(SPAN - (row - base), SPAN)

        def window(part):
            rows = pltpu.roll(ext[part, pl.ds(base, SPAN), :], left, 1)[:, :SIDE]
            return pltpu.roll(rows, up, 0)[:SIDE]

        patch_re, patch_im = window(0), window(1)
        probe_re, probe_im = probe[0], probe[1]
        exit_re = probe_re * patch_re - probe_im * patch_im
        exit_im = probe_re * patch_im + probe_im * patch_re
        far_re, far_im = transform(exit_re, exit_im, (fh, fl), (ih, il))
        far[p, 0] = far_re
        far[p, 1] = far_im
        strength = far_re * far_re + far_im * far_im
        intensity[:, p] = strength.reshape(PLANE_SIZE, SIDE // PLANE_SIZE, SIDE)
        return carry

    lax.fori_loop(0, pos.shape[0], pattern, 0)


def inverse_kernel(pos, change, far, probe, fh, fl, ih, il, out, grad):
    grad[...] = jnp.zeros_like(grad)

    def pattern(p, carry):
        row, col = pos[p, 0], pos[p, 1]
        factor = change[:, p].reshape(SIDE, SIDE)
        diff_re, diff_im = transform(far[p, 0] * factor, far[p, 1] * factor, (ih, il), (fh, fl))
        probe_re, probe_im = probe[0], probe[1]
        add_re = probe_re * diff_re + probe_im * diff_im
        add_im = probe_re * diff_im - probe_im * diff_re
        base = pl.multiple_of(row // 8 * 8, 8)
        below = jnp.zeros((SPAN - SIDE, SIDE), jnp.float32)
        beside = jnp.zeros((SPAN, SIDE), jnp.float32)
        for part, add in ((0, add_re), (1, add_im)):
            placed = pltpu.roll(jnp.concatenate([add, below], 0), row - base, 0)
            placed = pltpu.roll(jnp.concatenate([placed, beside], 1), col, 1)
            grad[part, pl.ds(base, SPAN), :] += placed
        return carry

    lax.fori_loop(0, pos.shape[0], pattern, 0)
    for d in range(PLANE_SIZE):
        for lower in range(2):
            for half in range(2):
                start = lower * SIDE + (d // 4) * 64 + half * 32 + (d % 4) * 8
                out[d, lower, :, half] = grad[:, start : start + 8, :]


VMEM = pl.BlockSpec(memory_space=pltpu.VMEM)
SMEM = pl.BlockSpec(memory_space=pltpu.SMEM)
PARAMS = pltpu.CompilerParams(vmem_limit_bytes=40 * 1024 * 1024)


def forward(positions, own, halo, probe, table):
    count = positions.shape[0]
    return pl.pallas_call(
        forward_kernel,
        out_shape=(
            jax.ShapeDtypeStruct((count, 2, SIDE, SIDE), jnp.float32),
            jax.ShapeDtypeStruct((PLANE_SIZE, count, SIDE // PLANE_SIZE, SIDE), jnp.float32),
        ),
        in_specs=[SMEM] + [VMEM] * 7,
        out_specs=(VMEM, VMEM),
        scratch_shapes=[pltpu.VMEM((2, 512, 512), jnp.float32)],
        compiler_params=PARAMS,
        name="forward",
    )(positions, own, halo, probe, *table)


def inverse(positions, change, far, probe, table):
    return pl.pallas_call(
        inverse_kernel,
        out_shape=jax.ShapeDtypeStruct((PLANE_SIZE, 2, 2, 2, 8, 512), jnp.float32),
        in_specs=[SMEM] + [VMEM] * 7,
        out_specs=VMEM,
        scratch_shapes=[pltpu.VMEM((2, 512, 512), jnp.float32)],
        compiler_params=PARAMS,
        name="inverse",
    )(positions, change, far, probe, *table)


def body(object_field, probe_modes, amplitude, positions):
    modes = 32
    table = [jnp.asarray(t) for t in tables()]
    probe = probe_modes[0]
    halo = moved(object_field, along_ring(-1))
    far, intensity = forward(positions, object_field, halo, probe, table)

    mine = lax.axis_index("y") * 4 + lax.axis_index("x")
    rows = SIDE // PLANE_SIZE
    summed = jnp.sum(lax.all_to_all(intensity, PLANE, 0, 0), 0)
    summed = summed + moved(summed, other_half)
    measured = lax.dynamic_slice_in_dim(amplitude, mine * rows, rows, 1)
    change = measured / jnp.sqrt(summed + 0.05 * modes) - 1.0
    change = jnp.broadcast_to(change[None], intensity.shape)
    change = lax.all_to_all(change, PLANE, 0, 0)

    gradient = inverse(positions, change, far, probe, table)
    gradient = jnp.sum(lax.all_to_all(gradient, PLANE, 0, 0), 0)
    total = gradient[0] + moved(gradient[1], along_ring(1))
    half = lax.axis_index("zhi")
    kept = lax.dynamic_index_in_dim(total, half, 1, keepdims=False)
    sent = lax.dynamic_index_in_dim(total, 1 - half, 1, keepdims=False)
    total = kept + moved(sent, other_half)
    place = (lax.axis_index("y") * 2 + half) * 4 + lax.axis_index("x")
    own = lax.dynamic_slice_in_dim(object_field, place * 8, 8, 1)
    return own + 0.5 * total / modes


def solution(mesh):
    fine = Mesh(mesh.devices.reshape(SIZES), AXES)
    tile, spec = ("zlo", "core"), ("y", "zhi", "x")
    placed = (
        P(None, tile, None),
        P(spec, None, None, None),
        P(tile, None, None),
        P(tile, None),
    )
    return jax.shard_map(
        body, mesh=fine, in_specs=placed, out_specs=P(None, tile + spec, None), check_vma=False
    )
```

time: 1570 us -> 186 us (0.12)
  the two profiles are of different devices: /device:TPU:32 before, /device:TPU:2 now
where the time goes in v1:
time: 186 us; the launch traced here: 185 us
  blocking collectives  61.3 us (33%)
  starting transfers between devices  52.5 us (28%)
  waiting for transfers between devices  41.4 us (22%)
  Pallas kernels  18.9 us (10%)
  local copies, waits for them, and re-layouts  7.36 us (4%)
  other arithmetic  3.8 us (2%)
    ppermute x4, starting transfers between devices, moved(): return lax.ppermute(value, AXES, pairs_of(move))  52.5 us
    ppermute x4, waiting for transfers between devices, moved(): return lax.ppermute(value, AXES, pairs_of(move))  41.4 us
    all_to_all x1, blocking collectives, body(): gradient = jnp.sum(lax.all_to_all(gradient, PLANE, 0, 0), 0)  26.3 us
    all_to_all x1, blocking collectives, body(): summed = jnp.sum(lax.all_to_all(intensity, PLANE, 0, 0), 0)  19 us
    all_to_all x1, blocking collectives, body(): change = lax.all_to_all(change, PLANE, 0, 0)  15.9 us
    pallas_call x1, Pallas kernels, forward(): pl.pallas_call(forward_kernel, out_shape=(jax.ShapeDtypeStruct((count, 2,...  9.73 us
    pallas_call x1, Pallas kernels, inverse(): pl.pallas_call(inverse_kernel, out_shape=jax.ShapeDtypeStruct((PLANE_SIZE...  9.21 us
    unnamed x23, local copies, waits for them, and re-layouts  7.22 us
  transfers between devices with their start and end apart: 4, of which 4 were waited for; matrix products, arithmetic and copies ran while one was open for 0% of the time, Pallas kernels for 0%

profile of v1, /device:TPU:2, one launch (start us, length us, event | category | flops | bytes accessed | tf_op | source)
XLA Modules:
  0.0 185.4 jit_solution(16968924504883315220)
XLA Ops:
  0.0 16.2 %collective-permute-start = (f32[2,256,512]{2,1,0:T(8,128)}, f32[2,256,512]{2,1,0:T(8,128)S(1)}, u32[]{:S(2)}, u32[]{:S(2)}) collective-permute-start(f32[2,256,512]{2,1,0:T(8,128)} %own.1), channel_id=1, source_target_pairs={{0,996},{1,997},{2,998},{3,999},{4,992},{5,993},{6,994},{7,995},{8... | collective-permute-start | bytes 3145736 | tf_op jit(solution)/shard_map/ppermute | solution.py:43
  16.2 0.8 copy.12.pos
  17.0 11.9 %collective-permute-done.halo = f32[2,256,512]{2,1,0:T(8,128)S(1)} collective-permute-done((f32[2,256,512]{2,1,0:T(8,128)}, f32[2,256,512]{2,1,0:T(8,128)S(1)}, u32[]{:S(2)}, u32[]{:S(2)}) %collective-permute-start) | collective-permute-done | bytes 1048608 | tf_op jit(solution)/shard_map/ppermute | solution.py:43
  28.8 1.0 copy-done
  29.9 1.0 copy-done.2
  30.9 1.0 copy-done.4
  32.0 1.0 copy-done.6
  33.0 1.0 copy-done.8
  34.1 1.2 copy-done.10
  35.3 9.7 %forward.1 = (f32[4,2,256,256]{3,2,1,0:T(8,128)S(1)}, f32[16,4,16,256]{3,2,1,0:T(8,128)S(1)}) custom-call(s32[4,2]{1,0:T(4,128)S(1)} %copy.12.pos, f32[2,256,512]{2,1,0:T(8,128)S(1)} %copy-done.10, f32[2,256,512]{2,1,0:T(8,128)S(1)} %collective-permute-done.halo, f32[2,256,256]{2,1,0:T(8,128)S(1)} %bitcast.15, bf16[512,512]{1,0:T(8,128)(2,1)S(1)} %copy-done.8, ...), custom_call_target="tpu_custom_call" | custom-call | tf_op jit(solution)/shard_map/forward/pallas_call | solution.py:139
  45.0 19.0 %all_to_all.15 = f32[16,4,16,256]{3,2,1,0:T(8,128)} all-to-all(f32[16,4,16,256]{3,2,1,0:T(8,128)S(1)} %get-tuple-element.7), channel_id=1, replica_groups=mesh['zlo'=16,'core'=2,'y'=4,'zhi'=2,'x'=4] {'y','x'}, dimensions={0} | all-to-all | bytes 2097152 | tf_op jit(solution)/shard_map/all_to_all | solution.py:174
  64.0 1.4 reduce_sum.18
  65.4 18.1 %collective-permute-start.1 = (f32[4,16,256]{2,1,0:T(8,128)S(1)}, f32[4,16,256]{2,1,0:T(8,128)S(1)}, u32[]{:S(2)}, u32[]{:S(2)}) collective-permute-start(f32[4,16,256]{2,1,0:T(8,128)S(1)} %reduce_sum.18), channel_id=1, source_target_pairs={{0,4},{1,5},{2,6},{3,7},{4,0},{5,1},{6,2},{7,3},{8,12},{9,13},{10,... | collective-permute-start | bytes 196616 | tf_op jit(solution)/shard_map/ppermute | solution.py:43
  83.5 0.0 copy-start.5
  83.5 0.0 copy-start.7
  83.6 0.0 copy-start.9
  83.6 6.6 %collective-permute-done.1 = f32[4,16,256]{2,1,0:T(8,128)S(1)} collective-permute-done((f32[4,16,256]{2,1,0:T(8,128)S(1)}, f32[4,16,256]{2,1,0:T(8,128)S(1)}, u32[]{:S(2)}, u32[]{:S(2)}) %collective-permute-start.1) | collective-permute-done | bytes 65568 | tf_op jit(solution)/shard_map/ppermute | solution.py:43
  90.2 0.9 multiply_add_fusion
  91.0 0.1 broadcast_in_dim.2
  91.1 15.9 %all_to_all.16.change = f32[16,4,16,256]{3,2,1,0:T(8,128)S(1)} all-to-all(f32[16,4,16,256]{3,2,1,0:T(8,128)S(1)} %broadcast_in_dim.2), channel_id=1, replica_groups=mesh['zlo'=16,'core'=2,'y'=4,'zhi'=2,'x'=4] {'y','x'}, dimensions={0} | all-to-all | bytes 2097152 | tf_op jit(solution)/shard_map/all_to_all | solution.py:179
  107.1 0.0 copy-done.1
  107.1 0.0 copy-done.3
  107.1 0.0 copy-done.5
  107.1 0.0 copy-done.7
  107.1 9.2 %inverse.1 = f32[16,2,2,2,8,512]{5,4,3,2,1,0:T(8,128)S(1)} custom-call(s32[4,2]{1,0:T(4,128)S(1)} %copy.12.pos, f32[16,4,16,256]{3,2,1,0:T(8,128)S(1)} %all_to_all.16.change, f32[4,2,256,256]{3,2,1,0:T(8,128)S(1)} %get-tuple-element.8.far, f32[2,256,256]{2,1,0:T(8,128)S(1)} %bitcast.16, bf16[512,512]{1,0:T(8,128)(2,1)S(1)} %copy-done.9, ...), custom_call_target="tpu_custom_call" | custom-call | tf_op jit(solution)/shard_map/inverse/pallas_call | solution.py:154
  116.3 26.3 %all_to_all.17 = f32[16,2,2,2,8,512]{5,4,3,2,1,0:T(8,128)S(1)} all-to-all(f32[16,2,2,2,8,512]{5,4,3,2,1,0:T(8,128)S(1)} %inverse.1), channel_id=1, replica_groups=mesh['zlo'=16,'core'=2,'y'=4,'zhi'=2,'x'=4] {'y','x'}, dimensions={0} | all-to-all | bytes 4194304 | tf_op jit(solution)/shard_map/all_to_all | solution.py:182
  142.7 0.2 reduce_sum.19
  142.9 0.0 collective-permute-start.2
  142.9 17.0 %collective-permute-done.2 = f32[2,2,8,512]{3,2,1,0:T(8,128)S(1)} collective-permute-done((f32[2,2,8,512]{3,2,1,0:T(8,128)S(1)}, f32[2,2,8,512]{3,2,1,0:T(8,128)S(1)}, u32[]{:S(2)}, u32[]{:S(2)}) %collective-permute-start.2) | collective-permute-done | bytes 65568 | tf_op jit(solution)/shard_map/ppermute | solution.py:43
  159.9 18.2 %collective-permute-start.3 = (f32[2,8,512]{2,1,0:T(8,128)S(1)}, f32[2,8,512]{2,1,0:T(8,128)S(1)}, u32[]{:S(2)}, u32[]{:S(2)}) collective-permute-start(f32[2,8,512]{2,1,0:T(8,128)S(1)} %dynamic-slice_bitcast_fusion), channel_id=1, source_target_pairs={{0,4},{1,5},{2,6},{3,7},{4,0},{5,1},{6,2},{7,3},{8,12},{9,13},{10,... | collective-permute-start | bytes 98312 | tf_op jit(solution)/shard_map/ppermute | solution.py:43
  178.1 5.9 %collective-permute-done.3 = f32[2,8,512]{2,1,0:T(8,128)S(1)} collective-permute-done((f32[2,8,512]{2,1,0:T(8,128)S(1)}, f32[2,8,512]{2,1,0:T(8,128)S(1)}, u32[]{:S(2)}, u32[]{:S(2)}) %collective-permute-start.3) | collective-permute-done | bytes 32800 | tf_op jit(solution)/shard_map/ppermute | solution.py:43
  184.0 1.4 fusion.2
  (12 shorter events, 0.0 us)
Async XLA Ops:
  0.0 28.8 %collective-permute-start = (f32[2,256,512]{2,1,0:T(8,128)}, f32[2,256,512]{2,1,0:T(8,128)S(1)}, u32[]{:S(2)}, u32[]{:S(2)}) collective-permute-start(f32[2,256,512]{2,1,0:T(8,128)} %own.1), channel_id=1, source_target_pairs={{0,996},{1,997},{2,998},{3,999},{4,992},{5,993},{6,994},{7,995},{8... | collective-permute-start | bytes 3145736 | tf_op jit(solution)/shard_map/ppermute | solution.py:43
  28.8 1.0 copy-start
  29.9 1.0 copy-start.2
  30.9 1.0 copy-start.4
  32.0 1.0 copy-start.6
  33.0 1.0 copy-start.8
  34.1 1.2 copy-start.10
  64.0 43.1 %copy-start.1 = (f32[1,2,256,256]{3,2,1,0:T(8,128)S(1)}, f32[1,2,256,256]{3,2,1,0:T(8,128)}, u32[]{:S(2)}) copy-start(f32[1,2,256,256]{3,2,1,0:T(8,128)} %param.9) | copy-start | bytes 1572868
  64.0 43.1 %copy-start.3 = (bf16[512,512]{1,0:T(8,128)(2,1)S(1)}, bf16[512,512]{1,0:T(8,128)(2,1)}, u32[]{:S(2)}) copy-start(bf16[512,512]{1,0:T(8,128)(2,1)} %constant.57.clone.il) | copy-start | bytes 1572868
  65.4 24.7 %collective-permute-start.1 = (f32[4,16,256]{2,1,0:T(8,128)S(1)}, f32[4,16,256]{2,1,0:T(8,128)S(1)}, u32[]{:S(2)}, u32[]{:S(2)}) collective-permute-start(f32[4,16,256]{2,1,0:T(8,128)S(1)} %reduce_sum.18), channel_id=1, source_target_pairs={{0,4},{1,5},{2,6},{3,7},{4,0},{5,1},{6,2},{7,3},{8,12},{9,13},{10,... | collective-permute-start | bytes 196616 | tf_op jit(solution)/shard_map/ppermute | solution.py:43
  83.5 23.6 %copy-start.5 = (bf16[512,512]{1,0:T(8,128)(2,1)S(1)}, bf16[512,512]{1,0:T(8,128)(2,1)}, u32[]{:S(2)}) copy-start(bf16[512,512]{1,0:T(8,128)(2,1)} %constant.56.clone.ih) | copy-start | bytes 1572868
  83.5 23.5 %copy-start.7 = (bf16[512,512]{1,0:T(8,128)(2,1)S(1)}, bf16[512,512]{1,0:T(8,128)(2,1)}, u32[]{:S(2)}) copy-start(bf16[512,512]{1,0:T(8,128)(2,1)} %constant.55.clone.fl) | copy-start | bytes 1572868
  83.6 23.5 %copy-start.9 = (bf16[512,512]{1,0:T(8,128)(2,1)S(1)}, bf16[512,512]{1,0:T(8,128)(2,1)}, u32[]{:S(2)}) copy-start(bf16[512,512]{1,0:T(8,128)(2,1)} %constant.54.clone.fh) | copy-start | bytes 1572868
  142.9 17.0 %collective-permute-start.2 = (f32[2,2,8,512]{3,2,1,0:T(8,128)S(1)}, f32[2,2,8,512]{3,2,1,0:T(8,128)S(1)}, u32[]{:S(2)}, u32[]{:S(2)}) collective-permute-start(f32[2,2,8,512]{3,2,1,0:T(8,128)S(1)} %slice_bitcast_fusion), channel_id=1, source_target_pairs={{0,32},{1,33},{2,34},{3,35},{4,36},{5,37},{6,38},{7,39},{8,40},{9,... | collective-permute-start | bytes 196616 | tf_op jit(solution)/shard_map/ppermute | solution.py:43
  159.9 24.1 %collective-permute-start.3 = (f32[2,8,512]{2,1,0:T(8,128)S(1)}, f32[2,8,512]{2,1,0:T(8,128)S(1)}, u32[]{:S(2)}, u32[]{:S(2)}) collective-permute-start(f32[2,8,512]{2,1,0:T(8,128)S(1)} %dynamic-slice_bitcast_fusion), channel_id=1, source_target_pairs={{0,4},{1,5},{2,6},{3,7},{4,0},{5,1},{6,2},{7,3},{8,12},{9,13},{10,... | collective-permute-start | bytes 98312 | tf_op jit(solution)/shard_map/ppermute | solution.py:43

commit v2 on v1

v2 whole, which is shorter than its diff:
```python
import math

import jax
import jax.numpy as jnp
import ml_dtypes
import numpy as np
from jax import lax
from jax.experimental import pallas as pl
from jax.experimental.pallas import tpu as pltpu
from jax.sharding import Mesh, PartitionSpec as P

AXES = ("zlo", "core", "y", "zhi", "x")
SIZES = (16, 2, 4, 2, 4)
PLANE = ("y", "x")
SIDE = 256
HALF = SIDE // 2
WIDTH = 512
COUNT = 4
MODES = 32
PLANE_SIZE = 16
ROWS = SIDE // PLANE_SIZE
SPAN = SIDE + 8


def pairs_of(move):
    count = math.prod(SIZES)
    pairs = []
    for source in range(count):
        place = np.unravel_index(source, SIZES)
        target = np.ravel_multi_index(move(*(int(v) for v in place)), SIZES)
        pairs.append((source, int(target)))
    return pairs


def along_ring(steps):
    def move(zlo, core, y, zhi, x):
        chip, core = divmod(((zhi * 16 + zlo) * 2 + core + steps) % 64, 2)
        return chip % 16, core, y, chip // 16, x

    return move


def other_core(zlo, core, y, zhi, x):
    return zlo, 1 - core, y, zhi, x


def moved(value, move):
    return lax.ppermute(value, AXES, pairs_of(move))


def tables():
    out = np.zeros((2, 2, 2, SIDE, SIDE), ml_dtypes.bfloat16)
    for parity in range(2):
        freq = 2 * np.arange(HALF) + parity
        angle = (np.outer(freq, np.arange(HALF)) % SIDE) * (2.0 * math.pi / SIDE)
        cos, sin = np.cos(angle) / 16.0, np.sin(angle) / 16.0
        whole = np.block([[cos, sin], [-sin, cos]])
        for turned, table in enumerate((whole, whole.T)):
            high = table.astype(np.float32).astype(ml_dtypes.bfloat16)
            low = (table - high.astype(np.float64)).astype(np.float32)
            out[turned, parity, 0] = high
            out[turned, parity, 1] = low.astype(ml_dtypes.bfloat16)
    return out


def halves(value):
    high = value.astype(jnp.bfloat16)
    return high, (value - high.astype(jnp.float32)).astype(jnp.bfloat16)


def dot(a, b):
    return jnp.dot(a, b, preferred_element_type=jnp.float32)


def product(a, b):
    return dot(a[0], b[0]) + (dot(a[0], b[1]) + dot(a[1], b[0]))


def side_by_side(*parts):
    return jnp.concatenate(parts, 1)


def stacked(*parts):
    return jnp.concatenate(parts, 0)


def own_share(amp, plane):
    out_row = lax.broadcasted_iota(jnp.int32, (COUNT * ROWS, COUNT * 2 * ROWS), 0)
    in_row = lax.broadcasted_iota(jnp.int32, (COUNT * ROWS, COUNT * 2 * ROWS), 1)
    take_rows = jnp.where(in_row == 2 * out_row + plane // 8, 1.0, 0.0).astype(jnp.bfloat16)
    in_col = lax.broadcasted_iota(jnp.int32, (SIDE, SIDE), 0)
    out_col = lax.broadcasted_iota(jnp.int32, (SIDE, SIDE), 1)
    wanted = jnp.where(out_col < HALF, 2 * out_col, 2 * out_col - (SIDE - 1))
    take_cols = jnp.where(in_col == wanted, 1.0, 0.0).astype(jnp.bfloat16)
    value, total = amp.reshape(COUNT * 2 * ROWS, SIDE), 0.0
    for _ in range(3):
        part = value.astype(jnp.bfloat16)
        value = value - part.astype(jnp.float32)
        total = total + dot(dot(take_rows, part).astype(jnp.bfloat16), take_cols)
    return total.reshape(COUNT, ROWS, SIDE)


def forward_kernel(
    pos, flags, own_hbm, halo_hbm, probe_hbm, gathered_hbm, swapped_hbm, amp_hbm, table_hbm,
    far, intensity, measured, probes, ext, other, swap, amp, table, sems,
):
    core, zhi, plane = flags[0], flags[1], flags[2]
    start = pl.multiple_of(lax.rem(plane, 8) * 2 * ROWS, 2 * ROWS)
    ends = (
        (amp_hbm.at[:, pl.ds(start, 2 * ROWS)], amp),
        (own_hbm, ext.at[:, pl.ds(0, SIDE)]),
        (halo_hbm, ext.at[:, pl.ds(SIDE, SIDE)]),
        (probe_hbm, probes.at[0]),
        (gathered_hbm.at[1 - zhi], other),
        (swapped_hbm, swap),
        (table_hbm, table),
    )
    copies = [pltpu.make_async_copy(*pair, sems.at[i]) for i, pair in enumerate(ends)]
    for copy in copies:
        copy.start()
    copies[0].wait()
    measured[...] = own_share(amp[...], plane)
    for copy in copies[1:]:
        copy.wait()
    probes[1, 0] = jnp.where(core == 0, other[...], swap[...])
    probes[1, 1] = jnp.where(core == 0, swap[...], other[...])

    def times(turned, parity):
        return table[turned, parity, 0], table[turned, parity, 1]

    def pattern(p, carry):
        row, col = pos[p, 0], pos[p, 1]
        base = pl.multiple_of(row // 8 * 8, 8)
        left = lax.rem(WIDTH - col, WIDTH)
        up = lax.rem(SPAN - (row - base), SPAN)

        def window(part):
            rows = pltpu.roll(ext[part, pl.ds(base, SPAN), :], left, 1)[:, :SIDE]
            return pltpu.roll(rows, up, 0)[:SIDE]

        patch_re, patch_im = window(0), window(1)
        sums, differences = [], []
        for m in range(2):
            wave_re = probes[m, 0] * patch_re - probes[m, 1] * patch_im
            wave_im = probes[m, 0] * patch_im + probes[m, 1] * patch_re
            sums.append(stacked(wave_re[:HALF] + wave_re[HALF:], wave_im[:HALF] + wave_im[HALF:]))
            differences.append(
                stacked(wave_re[:HALF] - wave_re[HALF:], wave_im[:HALF] - wave_im[HALF:])
            )
        even = product(times(0, 0), halves(side_by_side(*sums)))
        odd = product(times(0, 1), halves(side_by_side(*differences)))
        sums, differences = [], []
        for m in range(2):
            near, away = slice(m * SIDE, m * SIDE + HALF), slice(m * SIDE + HALF, (m + 1) * SIDE)
            plus = [part[:, near] + part[:, away] for part in (even, odd)]
            minus = [part[:, near] - part[:, away] for part in (even, odd)]
            for kept, parts in ((sums, plus), (differences, minus)):
                kept += [side_by_side(part[:HALF], part[HALF:]) for part in parts]
        for parity, parts in ((0, sums), (1, differences)):
            out = product(halves(stacked(*parts)), times(1, parity))
            far[p, parity] = out
            strength = out[:, :HALF] * out[:, :HALF] + out[:, HALF:] * out[:, HALF:]
            strength = strength[:SIDE] + strength[SIDE:]
            columns = pl.ds(parity * HALF, HALF)
            intensity[:, p, :, columns] = strength.reshape(PLANE_SIZE, ROWS, HALF)
        return carry

    lax.fori_loop(0, COUNT, pattern, 0)


def inverse_kernel(pos, flags, change, far_hbm, probes_hbm, table_hbm, out, grad, far, probes, table, sems):
    ends = ((far_hbm, far), (probes_hbm, probes), (table_hbm, table))
    copies = [pltpu.make_async_copy(*pair, sems.at[i]) for i, pair in enumerate(ends)]
    for copy in copies:
        copy.start()
    grad[...] = jnp.zeros_like(grad)
    for copy in copies:
        copy.wait()

    def times(turned, parity):
        return table[turned, parity, 0], table[turned, parity, 1]

    def pattern(p, carry):
        row, col = pos[p, 0], pos[p, 1]
        factor = change[:, p].reshape(SIDE, SIDE)
        scaled = []
        for parity in range(2):
            half = factor[:, parity * HALF : (parity + 1) * HALF]
            half = stacked(side_by_side(half, half), side_by_side(half, half))
            scaled.append(far[p, parity] * half)
        parts = []
        for parity in range(2):
            blocks = []
            for m in range(2):
                for side in range(2):
                    start = m * SIDE + parity * HALF
                    block = scaled[side][start : start + HALF]
                    blocks.append(stacked(block[:, :HALF], block[:, HALF:]))
            parts.append(product(times(1, parity), halves(side_by_side(*blocks))))
        near, away = parts[0] + parts[1], parts[0] - parts[1]
        parts = []
        for parity in range(2):
            blocks = []
            for m in range(2):
                for rows in (near, away):
                    start = (2 * m + parity) * HALF
                    block = rows[:, start : start + HALF]
                    blocks.append(side_by_side(block[:HALF], block[HALF:]))
            parts.append(product(halves(stacked(*blocks)), times(0, parity)))
        near, away = parts[0] + parts[1], parts[0] - parts[1]
        add_re, add_im = 0.0, 0.0
        for m in range(2):
            rows = slice(m * SIDE, (m + 1) * SIDE)
            diff_re = side_by_side(near[rows, :HALF], away[rows, :HALF])
            diff_im = side_by_side(near[rows, HALF:], away[rows, HALF:])
            add_re += probes[m, 0] * diff_re + probes[m, 1] * diff_im
            add_im += probes[m, 0] * diff_im - probes[m, 1] * diff_re
        base = pl.multiple_of(row // 8 * 8, 8)
        below = jnp.zeros((SPAN - SIDE, SIDE), jnp.float32)
        beside = jnp.zeros((SPAN, WIDTH - SIDE), jnp.float32)
        for part, add in ((0, add_re), (1, add_im)):
            placed = pltpu.roll(stacked(add, below), row - base, 0)
            placed = pltpu.roll(side_by_side(placed, beside), col, 1)
            grad[part, pl.ds(base, SPAN), :] += placed
        return carry

    lax.fori_loop(0, COUNT, pattern, 0)
    for d in range(PLANE_SIZE):
        for lower in range(2):
            start = lower * SIDE + (d // 4) * 64 + flags[1 + 2 * lower] * 32 + (d % 4) * 8
            out[d, lower] = grad[:, pl.ds(pl.multiple_of(start, 8), 8), :]


VMEM = pl.BlockSpec(memory_space=pltpu.VMEM)
SMEM = pl.BlockSpec(memory_space=pltpu.SMEM)
ANY = pl.BlockSpec(memory_space=pl.ANY)
PARAMS = pltpu.CompilerParams(vmem_limit_bytes=44 * 1024 * 1024)
TABLE_VMEM = pltpu.VMEM((2, 2, 2, SIDE, SIDE), jnp.bfloat16)


def floats(*shape):
    return jax.ShapeDtypeStruct(shape, jnp.float32)


def forward(*operands):
    return pl.pallas_call(
        forward_kernel,
        out_shape=(
            floats(COUNT, 2, 2 * SIDE, SIDE),
            floats(PLANE_SIZE, COUNT, ROWS, SIDE),
            floats(COUNT, ROWS, SIDE),
            floats(2, 2, SIDE, SIDE),
        ),
        in_specs=[SMEM] * 2 + [ANY] * 7,
        out_specs=[VMEM] * 4,
        scratch_shapes=[
            pltpu.VMEM((2, WIDTH, WIDTH), jnp.float32),
            pltpu.VMEM((SIDE, SIDE), jnp.float32),
            pltpu.VMEM((SIDE, SIDE), jnp.float32),
            pltpu.VMEM((COUNT, 2 * ROWS, SIDE), jnp.float32),
            TABLE_VMEM,
            pltpu.SemaphoreType.DMA((7,)),
        ],
        compiler_params=PARAMS,
        name="forward",
    )(*operands)


def inverse(*operands):
    return pl.pallas_call(
        inverse_kernel,
        out_shape=floats(PLANE_SIZE, 2, 2, 8, WIDTH),
        in_specs=[SMEM] * 2 + [VMEM] + [ANY] * 3,
        out_specs=VMEM,
        scratch_shapes=[
            pltpu.VMEM((2, WIDTH, WIDTH), jnp.float32),
            pltpu.VMEM((COUNT, 2, 2 * SIDE, SIDE), jnp.float32),
            pltpu.VMEM((2, 2, SIDE, SIDE), jnp.float32),
            TABLE_VMEM,
            pltpu.SemaphoreType.DMA((3,)),
        ],
        compiler_params=PARAMS,
        name="inverse",
    )(*operands)


def body(object_field, probe_modes, amplitude, positions):
    table = jnp.asarray(tables())
    zlo, core = lax.axis_index("zlo"), lax.axis_index("core")
    y, zhi, x = (lax.axis_index(name) for name in ("y", "zhi", "x"))
    lower_half = jnp.where((zlo == 15) & (core == 1), 1 - zhi, zhi)
    flags = jnp.stack([core, zhi, y * 4 + x, lower_half]).astype(jnp.int32)

    halo = moved(object_field, along_ring(-1))
    piece = lax.dynamic_slice(probe_modes[0], (core, zlo * ROWS, 0), (1, ROWS, SIDE))[0]
    gathered = lax.all_gather(piece, ("zhi", "zlo"), axis=0, tiled=True).reshape(2, SIDE, SIDE)
    swapped = moved(lax.dynamic_index_in_dim(gathered, 1 - zhi, 0, keepdims=False), other_core)

    far, intensity, measured, probes = forward(
        positions, flags, object_field, halo, probe_modes[0], gathered, swapped, amplitude, table
    )
    summed = jnp.sum(lax.all_to_all(intensity, PLANE, 0, 0), 0)
    change = measured / jnp.sqrt(summed + 0.05 * MODES) - 1.0
    change = lax.all_to_all(jnp.broadcast_to(change[None], intensity.shape), PLANE, 0, 0)

    gradient = inverse(positions, flags, change, far, probes, table)
    gradient = jnp.sum(lax.all_to_all(gradient, PLANE, 0, 0), 0)
    total = gradient[0] + moved(gradient[1], along_ring(1))
    own = lax.dynamic_slice_in_dim(object_field, ((y * 2 + zhi) * 4 + x) * 8, 8, 1)
    return own + 0.5 * total / MODES


def solution(mesh):
    fine = Mesh(mesh.devices.reshape(SIZES), AXES)
    tile, spec = ("zlo", "core"), ("y", "zhi", "x")
    placed = (
        P(None, tile, None),
        P(spec, None, None, None),
        P(tile, None, None),
        P(tile, None),
    )
    return jax.shard_map(
        body, mesh=fine, in_specs=placed, out_specs=P(None, tile + spec, None), check_vma=False
    )
```

time: 186 us -> 179 us (0.962)
  blocking collectives: 61.3 us -> 127 us
  waiting for transfers between devices: 41.4 us -> 5.16 us
  starting transfers between devices: 52.5 us -> 18.1 us
  other arithmetic: 3.8 us -> 1.62 us
    all_gather x0 -> x1, blocking collectives: none -> 64.9 us  [body(): lax.all_gather(piece, ('zhi', 'zlo'), axis=0, tiled=True)]
    ppermute x4 -> x3, waiting for transfers between devices: 41.4 us -> 5.16 us  [moved(): return lax.ppermute(value, AXES, pairs_of(move))]
    ppermute x4 -> x3, starting transfers between devices: 52.5 us -> 18.1 us  [moved(): return lax.ppermute(value, AXES, pairs_of(move))]
    all_to_all x1, blocking collectives: 26.3 us -> 19.2 us  [body(): gradient = jnp.sum(lax.all_to_all(gradient, PLANE, 0, 0), 0)]
    all_to_all x1, blocking collectives: 19 us -> 23.5 us  [body(): summed = jnp.sum(lax.all_to_all(intensity, PLANE, 0, 0), 0)]
    all_to_all x1, blocking collectives: 15.9 us -> 19.6 us  [body(): lax.all_to_all(jnp.broadcast_to(change[None], intensity.shape), PLANE, 0, 0)]
    unnamed x23 -> x13, local copies, waits for them, and re-layouts: 7.22 us -> 7.68 us
  transfers between devices with their start and end apart: 4 -> 3, of which waited for: 4 -> 2; matrix products, arithmetic and copies ran while one was open for 0% -> 1% of each run, Pallas kernels for 0% -> 0%
where the time goes in v2:
time: 179 us; the launch traced here: 178 us
  blocking collectives  127 us (71%)
  starting transfers between devices  18.1 us (10%)
  Pallas kernels  17.4 us (10%)
  local copies, waits for them, and re-layouts  8.53 us (5%)
  waiting for transfers between devices  5.16 us (3%)
    all_gather x1, blocking collectives, body(): lax.all_gather(piece, ('zhi', 'zlo'), axis=0, tiled=True)  64.9 us
    all_to_all x1, blocking collectives, body(): summed = jnp.sum(lax.all_to_all(intensity, PLANE, 0, 0), 0)  23.5 us
    all_to_all x1, blocking collectives, body(): lax.all_to_all(jnp.broadcast_to(change[None], intensity.shape), PLANE, 0, 0)  19.6 us
    all_to_all x1, blocking collectives, body(): gradient = jnp.sum(lax.all_to_all(gradient, PLANE, 0, 0), 0)  19.2 us
    ppermute x3, starting transfers between devices, moved(): return lax.ppermute(value, AXES, pairs_of(move))  18.1 us
    pallas_call x1, Pallas kernels, forward(): pl.pallas_call(forward_kernel, out_shape=(floats(COUNT, 2, 2 * SIDE, SIDE...  10.1 us
    unnamed x13, local copies, waits for them, and re-layouts  7.68 us
    pallas_call x1, Pallas kernels, inverse(): pl.pallas_call(inverse_kernel, out_shape=floats(PLANE_SIZE, 2, 2, 8, WIDT...  7.28 us
  transfers between devices with their start and end apart: 3, of which 2 were waited for; matrix products, arithmetic and copies ran while one was open for 1% of the time, Pallas kernels for 0%

profile of v2, /device:TPU:2, one launch (start us, length us, event | category | flops | bytes accessed | tf_op | source)
XLA Modules:
  0.0 178.2 jit_solution(1757704921211911370)
XLA Ops:
  0.0 16.2 %collective-permute-start = (f32[2,256,512]{2,1,0:T(8,128)}, f32[2,256,512]{2,1,0:T(8,128)S(1)}, u32[]{:S(2)}, u32[]{:S(2)}) collective-permute-start(f32[2,256,512]{2,1,0:T(8,128)} %own_hbm.1), channel_id=1, source_target_pairs={{0,996},{1,997},{2,998},{3,999},{4,992},{5,993},{6,994},{7,995},{8... | collective-permute-start | bytes 3145736 | tf_op jit(solution)/shard_map/ppermute | solution.py:48
  16.2 0.7 constant_dynamic-slice_fusion
  16.9 64.9 %all-gather = f32[1,1,512,256]{3,2,1,0:T(8,128)S(1)} all-gather(f32[1,1,16,256]{3,2,1,0:T(8,128)S(1)} %constant_dynamic-slice_fusion), channel_id=2, replica_groups=mesh['zlo'=16,'core'=2,'y'=4,'zhi'=2,'x'=4] {'zhi','zlo'}, dimensions={2}, use_global_device_ids=true | all-gather | bytes 540672 | tf_op jit(solution)/shard_map/all_gather | solution.py:296
  81.9 1.9 %collective-permute-start.1 = (f32[256,256]{1,0:T(8,128)S(1)}, f32[256,256]{1,0:T(8,128)S(1)}, u32[]{:S(2)}, u32[]{:S(2)}) collective-permute-start(f32[256,256]{1,0:T(8,128)S(1)} %dynamic-slice_bitcast_fusion), channel_id=1, source_target_pairs={{0,32},{1,33},{2,34},{3,35},{4,36},{5,37},{6,38},{7,39},{8,40},{9,... | collective-permute-start | bytes 786440 | tf_op jit(solution)/shard_map/ppermute | solution.py:48
  83.8 0.8 copy.7.pos
  84.6 0.1 pad_add_fusion.flags
  84.7 0.6 collective-permute-done.1.swapped_hbm
  85.3 0.0 collective-permute-done.halo_hbm
  85.3 0.0 copy-start.1
  85.3 1.2 copy-done.1
  86.6 0.0 copy-start.3
  86.6 1.2 copy-done.3
  87.8 0.0 copy-start.4
  87.8 1.2 copy-done.4
  89.0 0.0 copy-start.5
  89.0 1.0 copy-done.5
  90.0 10.1 %forward.1 = (f32[4,2,512,256]{3,2,1,0:T(8,128)}, f32[16,4,16,256]{3,2,1,0:T(8,128)S(1)}, f32[4,16,256]{2,1,0:T(8,128)S(1)}, f32[2,2,256,256]{3,2,1,0:T(8,128)S(1)}) custom-call(s32[4,2]{1,0:T(4,128)S(1)} %copy.7.pos, s32[4]{0:T(128)S(1)} %pad_add_fusion.flags, f32[2,256,512]{2,1,0:T(8,128)S(1)} %copy-done.3, ...), custom_call_target="tpu_custom_call" | custom-call | tf_op jit(solution)/shard_map/forward/pallas_call | solution.py:246
  100.2 0.0 copy-start.2
  100.2 23.5 %all_to_all.15 = f32[16,4,16,256]{3,2,1,0:T(8,128)S(1)} all-to-all(f32[16,4,16,256]{3,2,1,0:T(8,128)S(1)} %get-tuple-element.10), channel_id=1, replica_groups=mesh['zlo'=16,'core'=2,'y'=4,'zhi'=2,'x'=4] {'y','x'}, dimensions={0} | all-to-all | bytes 2097152 | tf_op jit(solution)/shard_map/all_to_all | solution.py:302
  123.7 0.1 reduce_sum.18
  123.8 0.1 broadcast_in_dim.2
  123.9 19.6 %all_to_all.16.change = f32[16,4,16,256]{3,2,1,0:T(8,128)S(1)} all-to-all(f32[16,4,16,256]{3,2,1,0:T(8,128)S(1)} %broadcast_in_dim.2), channel_id=1, replica_groups=mesh['zlo'=16,'core'=2,'y'=4,'zhi'=2,'x'=4] {'y','x'}, dimensions={0} | all-to-all | bytes 2097152 | tf_op jit(solution)/shard_map/all_to_all | solution.py:304
  143.6 0.0 copy-done.2
  143.6 0.0 copy-start
  143.6 2.2 %copy-done = f32[4,2,512,256]{3,2,1,0:T(8,128)S(1)} copy-done((f32[4,2,512,256]{3,2,1,0:T(8,128)S(1)}, f32[4,2,512,256]{3,2,1,0:T(8,128)}, u32[]{:S(2)}) %copy-start) | copy-done | bytes 4194328
  145.8 7.3 %inverse.1 = f32[16,2,2,8,512]{4,3,2,1,0:T(8,128)S(1)} custom-call(s32[4,2]{1,0:T(4,128)S(1)} %copy.7.pos, s32[4]{0:T(128)S(1)} %pad_add_fusion.flags, f32[16,4,16,256]{3,2,1,0:T(8,128)S(1)} %all_to_all.16.change, f32[4,2,512,256]{3,2,1,0:T(8,128)S(1)} %copy-done, f32[2,2,256,256]{3,2,1,0:T(8,128)S(1)} %get-tuple-element.12.probes_hbm, ...), custom_call_target="tpu_custom_call" | custom-call | tf_op jit(solution)/shard_map/inverse/pallas_call | solution.py:270
  153.0 19.2 %all_to_all.17 = f32[16,2,2,8,512]{4,3,2,1,0:T(8,128)S(1)} all-to-all(f32[16,2,2,8,512]{4,3,2,1,0:T(8,128)S(1)} %inverse.1), channel_id=1, replica_groups=mesh['zlo'=16,'core'=2,'y'=4,'zhi'=2,'x'=4] {'y','x'}, dimensions={0} | all-to-all | bytes 2097152 | tf_op jit(solution)/shard_map/all_to_all | solution.py:307
  172.2 0.1 reduce_sum.19
  172.3 0.0 collective-permute-start.2
  172.3 4.5 %collective-permute-done.2 = f32[2,8,512]{2,1,0:T(8,128)S(1)} collective-permute-done((f32[2,8,512]{2,1,0:T(8,128)S(1)}, f32[2,8,512]{2,1,0:T(8,128)S(1)}, u32[]{:S(2)}, u32[]{:S(2)}) %collective-permute-start.2) | collective-permute-done | bytes 32800 | tf_op jit(solution)/shard_map/ppermute | solution.py:48
  176.9 1.4 fusion.2
  (3 shorter events, 0.0 us)
Async XLA Ops:
  0.0 85.3 %collective-permute-start = (f32[2,256,512]{2,1,0:T(8,128)}, f32[2,256,512]{2,1,0:T(8,128)S(1)}, u32[]{:S(2)}, u32[]{:S(2)}) collective-permute-start(f32[2,256,512]{2,1,0:T(8,128)} %own_hbm.1), channel_id=1, source_target_pairs={{0,996},{1,997},{2,998},{3,999},{4,992},{5,993},{6,994},{7,995},{8... | collective-permute-start | bytes 3145736 | tf_op jit(solution)/shard_map/ppermute | solution.py:48
  81.9 3.4 %collective-permute-start.1 = (f32[256,256]{1,0:T(8,128)S(1)}, f32[256,256]{1,0:T(8,128)S(1)}, u32[]{:S(2)}, u32[]{:S(2)}) collective-permute-start(f32[256,256]{1,0:T(8,128)S(1)} %dynamic-slice_bitcast_fusion), channel_id=1, source_target_pairs={{0,32},{1,33},{2,34},{3,35},{4,36},{5,37},{6,38},{7,39},{8,40},{9,... | collective-permute-start | bytes 786440 | tf_op jit(solution)/shard_map/ppermute | solution.py:48
  85.3 1.2 copy-start.1
  86.6 1.2 copy-start.3
  87.8 1.2 copy-start.4
  89.0 1.0 copy-start.5
  100.2 43.4 %copy-start.2 = (bf16[2,2,2,256,256]{4,3,2,1,0:T(8,128)(2,1)S(1)}, bf16[2,2,2,256,256]{4,3,2,1,0:T(8,128)(2,1)}, u32[]{:S(2)}) copy-start(bf16[2,2,2,256,256]{4,3,2,1,0:T(8,128)(2,1)} %constant.59.clone.table_hbm) | copy-start | bytes 3145732
  143.6 2.2 %copy-start = (f32[4,2,512,256]{3,2,1,0:T(8,128)S(1)}, f32[4,2,512,256]{3,2,1,0:T(8,128)}, u32[]{:S(2)}) copy-start(f32[4,2,512,256]{3,2,1,0:T(8,128)} %get-tuple-element.11.far_hbm) | copy-start | bytes 12582916
  172.3 4.6 %collective-permute-start.2 = (f32[2,8,512]{2,1,0:T(8,128)S(1)}, f32[2,8,512]{2,1,0:T(8,128)S(1)}, u32[]{:S(2)}, u32[]{:S(2)}) collective-permute-start(f32[2,8,512]{2,1,0:T(8,128)S(1)} %slice_bitcast_fusion), channel_id=1, source_target_pairs={{0,32},{1,33},{2,34},{3,35},{4,36},{5,37},{6,38},{7,39},{8,40},{9,... | collective-permute-start | bytes 98312 | tf_op jit(solution)/shard_map/ppermute | solution.py:48

commit v3 on v2

v3 whole, which is shorter than its diff:
```python
import math

import jax
import jax.numpy as jnp
import ml_dtypes
import numpy as np
from jax import lax
from jax.experimental import pallas as pl
from jax.experimental.pallas import tpu as pltpu
from jax.sharding import Mesh, PartitionSpec as P

AXES = ("zlo", "core", "y", "zhi", "x")
SIZES = (16, 2, 4, 2, 4)
PLANE = ("y", "x")
SIDE = 256
HALF = SIDE // 2
WIDTH = 512
COUNT = 4
MODES = 32
PLANE_SIZE = 16
ROWS = SIDE // PLANE_SIZE
SPAN = SIDE + 8


def pairs_of(move):
    count = math.prod(SIZES)
    pairs = []
    for source in range(count):
        place = np.unravel_index(source, SIZES)
        target = np.ravel_multi_index(move(*(int(v) for v in place)), SIZES)
        pairs.append((source, int(target)))
    return pairs


def along_ring(steps):
    def move(zlo, core, y, zhi, x):
        chip, core = divmod(((zhi * 16 + zlo) * 2 + core + steps) % 64, 2)
        return chip % 16, core, y, chip // 16, x

    return move


def other_core(zlo, core, y, zhi, x):
    return zlo, 1 - core, y, zhi, x


def other_half(zlo, core, y, zhi, x):
    return zlo, core, y, 1 - zhi, x


def next_chip(zlo, core, y, zhi, x):
    return zlo ^ 1, core, y, zhi, x


def next_other(zlo, core, y, zhi, x):
    return zlo ^ 1, 1 - core, y, zhi, x


def across(zlo, core, y, zhi, x):
    chip = zhi * 16 + zlo
    chip = (chip + (8 if chip // 8 % 2 else -8)) % 32
    return chip % 16, core, y, chip // 16, x


def moved(value, move):
    return lax.ppermute(value, AXES, pairs_of(move))


def tables():
    out = np.zeros((2, 2, 2, SIDE, SIDE), ml_dtypes.bfloat16)
    for parity in range(2):
        freq = 2 * np.arange(HALF) + parity
        angle = (np.outer(freq, np.arange(HALF)) % SIDE) * (2.0 * math.pi / SIDE)
        cos, sin = np.cos(angle) / 16.0, np.sin(angle) / 16.0
        whole = np.block([[cos, sin], [-sin, cos]])
        for turned, table in enumerate((whole, whole.T)):
            high = table.astype(np.float32).astype(ml_dtypes.bfloat16)
            low = (table - high.astype(np.float64)).astype(np.float32)
            out[turned, parity, 0] = high
            out[turned, parity, 1] = low.astype(ml_dtypes.bfloat16)
    return out


def halves(value):
    high = value.astype(jnp.bfloat16)
    return high, (value - high.astype(jnp.float32)).astype(jnp.bfloat16)


def dot(a, b):
    return jnp.dot(a, b, preferred_element_type=jnp.float32)


def product(a, b):
    return dot(a[0], b[0]) + (dot(a[0], b[1]) + dot(a[1], b[0]))


def side_by_side(*parts):
    return jnp.concatenate(parts, 1)


def stacked(*parts):
    return jnp.concatenate(parts, 0)


def own_share(amp, plane):
    out_row = lax.broadcasted_iota(jnp.int32, (COUNT * ROWS, COUNT * 2 * ROWS), 0)
    in_row = lax.broadcasted_iota(jnp.int32, (COUNT * ROWS, COUNT * 2 * ROWS), 1)
    take_rows = jnp.where(in_row == 2 * out_row + plane // 8, 1.0, 0.0).astype(jnp.bfloat16)
    in_col = lax.broadcasted_iota(jnp.int32, (SIDE, SIDE), 0)
    out_col = lax.broadcasted_iota(jnp.int32, (SIDE, SIDE), 1)
    wanted = jnp.where(out_col < HALF, 2 * out_col, 2 * out_col - (SIDE - 1))
    take_cols = jnp.where(in_col == wanted, 1.0, 0.0).astype(jnp.bfloat16)
    value, total = amp.reshape(COUNT * 2 * ROWS, SIDE), 0.0
    for _ in range(3):
        part = value.astype(jnp.bfloat16)
        value = value - part.astype(jnp.float32)
        total = total + dot(dot(take_rows, part).astype(jnp.bfloat16), take_cols)
    return total.reshape(COUNT, ROWS, SIDE)


def to_frequencies(waves, table):
    parts = []
    for parity, sign in ((0, 1.0), (1, -1.0)):
        blocks = [stacked(*(part[:HALF] + sign * part[HALF:] for part in wave)) for wave in waves]
        parts.append(product(times(table, 0, parity), halves(side_by_side(*blocks))))
    outs = []
    for parity, sign in ((0, 1.0), (1, -1.0)):
        blocks = []
        for w in range(2):
            middle = w * SIDE + HALF
            for part in parts:
                block = part[:, middle - HALF : middle] + sign * part[:, middle : middle + HALF]
                blocks.append(side_by_side(block[:HALF], block[HALF:]))
        outs.append(product(halves(stacked(*blocks)), times(table, 1, parity)))
    return outs


def to_samples(far, table):
    parts = []
    for parity in range(2):
        blocks = []
        for w in range(2):
            start = w * SIDE + parity * HALF
            for side in far:
                block = side[start : start + HALF]
                blocks.append(stacked(block[:, :HALF], block[:, HALF:]))
        parts.append(product(times(table, 1, parity), halves(side_by_side(*blocks))))
    both = parts[0] + parts[1], parts[0] - parts[1]
    parts = []
    for parity in range(2):
        blocks = []
        for w in range(2):
            start = (2 * w + parity) * HALF
            for rows in both:
                block = rows[:, start : start + HALF]
                blocks.append(side_by_side(block[:HALF], block[HALF:]))
        parts.append(product(halves(stacked(*blocks)), times(table, 0, parity)))
    near, away = parts[0] + parts[1], parts[0] - parts[1]
    waves = []
    for w in range(2):
        rows = slice(w * SIDE, (w + 1) * SIDE)
        waves.append(
            (
                side_by_side(near[rows, :HALF], away[rows, :HALF]),
                side_by_side(near[rows, HALF:], away[rows, HALF:]),
            )
        )
    return waves


def times(table, turned, parity):
    return table[turned, parity, 0], table[turned, parity, 1]


def lit(probe_re, probe_im, patch_re, patch_im):
    return probe_re * patch_re - probe_im * patch_im, probe_re * patch_im + probe_im * patch_re


def started(pairs, sems):
    copies = [pltpu.make_async_copy(*pair, sems.at[i]) for i, pair in enumerate(pairs)]
    for copy in copies:
        copy.start()
    return copies


def own_kernel(
    pos, halo, own_hbm, probe_hbm, table_hbm,
    far_hbm, patch_hbm, intensity, ext, probe, table, far, patch, sems, out_sems,
):
    pairs = (
        (own_hbm, ext.at[:, pl.ds(0, SIDE)]),
        (probe_hbm, probe),
        (table_hbm, table),
    )
    copies = started(pairs, sems)
    ext[:, SIDE:] = halo[...]
    for copy in copies:
        copy.wait()

    def out_copies(q):
        return (
            pltpu.make_async_copy(far.at[q], far_hbm.at[q], out_sems.at[0, q]),
            pltpu.make_async_copy(patch.at[q], patch_hbm.at[q], out_sems.at[1, q]),
        )

    def pair(q, carry):
        waves = []
        for w in range(2):
            row, col = pos[2 * q + w, 0], pos[2 * q + w, 1]
            base = pl.multiple_of(row // 8 * 8, 8)
            left = lax.rem(WIDTH - col, WIDTH)
            up = lax.rem(SPAN - (row - base), SPAN)
            window = []
            for part in range(2):
                rows = pltpu.roll(ext[part, pl.ds(base, SPAN), :], left, 1)[:, :SIDE]
                window.append(pltpu.roll(rows, up, 0)[:SIDE])
                patch[q, w, part] = window[part]
            waves.append(lit(probe[0], probe[1], *window))
        for parity, out in enumerate(to_frequencies(waves, table)):
            far[q, parity] = out
            strength = out[:, :HALF] * out[:, :HALF] + out[:, HALF:] * out[:, HALF:]
            columns = pl.ds(parity * HALF, HALF)
            for w in range(2):
                rows = strength[w * SIDE : (w + 1) * SIDE]
                intensity[:, 2 * q + w, :, columns] = rows.reshape(PLANE_SIZE, ROWS, HALF)
        for copy in out_copies(q):
            copy.start()
        return carry

    lax.fori_loop(0, COUNT // 2, pair, 0)
    for q in range(COUNT // 2):
        for copy in out_copies(q):
            copy.wait()


def other_kernel(
    flags, patch_hbm, amp_hbm, table_hbm, first, second, crossed_first, crossed_second,
    far_hbm, probe_hbm, measured, patch, amp, table, probe, far, sems, out_sems,
):
    core, plane, odd = flags[0], flags[2], flags[4]
    start = pl.multiple_of(lax.rem(plane, 8) * 2 * ROWS, 2 * ROWS)
    pairs = (
        (amp_hbm.at[:, pl.ds(start, 2 * ROWS)], amp),
        (table_hbm, table),
        (patch_hbm, patch),
    )
    copies = started(pairs, sems)
    copies[0].wait()
    measured[...] = own_share(amp[...], plane)
    for copy in copies[1:]:
        copy.wait()
    for channel in range(2):
        for half in range(2):
            of_own = jnp.where(odd == half, first[...], second[...])
            of_other = jnp.where(odd == half, crossed_first[...], crossed_second[...])
            value = jnp.where(core == channel, of_own, of_other)
            probe[channel, half * HALF : (half + 1) * HALF] = value
    probe_copy = pltpu.make_async_copy(probe, probe_hbm, out_sems.at[COUNT // 2])
    probe_copy.start()

    def far_copy(q):
        return pltpu.make_async_copy(far.at[q], far_hbm.at[q], out_sems.at[q])

    def pair(q, carry):
        waves = [lit(probe[0], probe[1], patch[q, w, 0], patch[q, w, 1]) for w in range(2)]
        for parity, out in enumerate(to_frequencies(waves, table)):
            far[q, parity] = out
        far_copy(q).start()
        return carry

    lax.fori_loop(0, COUNT // 2, pair, 0)
    for q in range(COUNT // 2):
        far_copy(q).wait()
    probe_copy.wait()


def collect_kernel(shares, piece_in, summed, piece_out):
    summed[...] = jnp.sum(shares[...], 0)
    piece_out[...] = piece_in[...]


def change_kernel(summed, arrived, measured, out):
    total = summed[...] + arrived[...]
    change = measured[...] / jnp.sqrt(total + 0.05 * MODES) - 1.0
    for d in range(PLANE_SIZE):
        out[d] = change


def inverse_kernel(
    pos, flags, change, far_own_hbm, far_other_hbm, probe_own_hbm, probe_other_hbm, table_hbm,
    out, grad, far, probe, table, sems, far_sems,
):
    pairs = ((probe_own_hbm, probe.at[0]), (probe_other_hbm, probe.at[1]), (table_hbm, table))
    copies = started(pairs, sems)

    def far_copies(q):
        return [
            pltpu.make_async_copy(source.at[q], far.at[m, q], far_sems.at[m, q])
            for m, source in enumerate((far_own_hbm, far_other_hbm))
        ]

    for q in range(COUNT // 2):
        for copy in far_copies(q):
            copy.start()
    grad[...] = jnp.zeros_like(grad)
    for copy in copies:
        copy.wait()

    def pair(q, carry):
        for copy in far_copies(q):
            copy.wait()
        factors = []
        for parity in range(2):
            columns = pl.ds(parity * HALF, HALF)
            rows = [change[:, 2 * q + w, :, columns].reshape(SIDE, HALF) for w in range(2)]
            factors.append(side_by_side(stacked(*rows), stacked(*rows)))
        adds = [[0.0, 0.0], [0.0, 0.0]]
        for m in range(2):
            waves = to_samples([far[m, q, side] * factors[side] for side in range(2)], table)
            for add, (real, imag) in zip(adds, waves):
                add[0] += probe[m, 0] * real + probe[m, 1] * imag
                add[1] += probe[m, 0] * imag - probe[m, 1] * real
        below = jnp.zeros((SPAN - SIDE, SIDE), jnp.float32)
        beside = jnp.zeros((SPAN, WIDTH - SIDE), jnp.float32)
        for w in range(2):
            row, col = pos[2 * q + w, 0], pos[2 * q + w, 1]
            base = pl.multiple_of(row // 8 * 8, 8)
            for part in range(2):
                placed = pltpu.roll(stacked(adds[w][part], below), row - base, 0)
                placed = pltpu.roll(side_by_side(placed, beside), col, 1)
                grad[part, pl.ds(base, SPAN), :] += placed
        return carry

    lax.fori_loop(0, COUNT // 2, pair, 0)
    for d in range(PLANE_SIZE):
        for lower in range(2):
            start = lower * SIDE + (d // 4) * 64 + flags[1 + 2 * lower] * 32 + (d % 4) * 8
            out[d, lower] = grad[:, pl.ds(pl.multiple_of(start, 8), 8), :]


VMEM = pl.BlockSpec(memory_space=pltpu.VMEM)
SMEM = pl.BlockSpec(memory_space=pltpu.SMEM)
HBM = pl.BlockSpec(memory_space=pltpu.HBM)
PAIRS = COUNT // 2
FAR = (PAIRS, 2, 2 * SIDE, SIDE)
PATCH = (PAIRS, 2, 2, SIDE, SIDE)
DMA = pltpu.SemaphoreType.DMA


def floats(*shape):
    return jax.ShapeDtypeStruct(shape, jnp.float32)


def scratch(*shape):
    return pltpu.VMEM(shape, jnp.float32)


TABLE = pltpu.VMEM((2, 2, 2, SIDE, SIDE), jnp.bfloat16)


def call(kernel, name, in_specs, outs, scratches, operands, work=0, limit=32):
    moves = sum(math.prod(v.shape) * v.dtype.itemsize for v in operands)
    return pl.pallas_call(
        kernel,
        out_shape=[shape for shape, _ in outs],
        in_specs=in_specs,
        out_specs=[spec for _, spec in outs],
        scratch_shapes=scratches,
        compiler_params=pltpu.CompilerParams(vmem_limit_bytes=limit * 1024 * 1024),
        cost_estimate=pl.CostEstimate(flops=work, bytes_accessed=moves, transcendentals=0),
        name=name,
    )(*operands)


def body(object_field, probe_modes, amplitude, positions):
    table = jnp.asarray(tables())
    work = COUNT * 12 * 2 * SIDE**3
    zlo, core = lax.axis_index("zlo"), lax.axis_index("core")
    y, zhi, x = (lax.axis_index(name) for name in ("y", "zhi", "x"))
    odd = lax.rem(zlo, 2)
    lower_half = jnp.where((zlo == 15) & (core == 1), 1 - zhi, zhi)
    flags = jnp.stack([core, zhi, y * 4 + x, lower_half, odd]).astype(jnp.int32)
    probe = probe_modes[0]

    halo = moved(object_field, along_ring(-1))
    piece = lax.dynamic_slice(probe, (core, odd * HALF, 0), (1, HALF, SIDE))[0]
    first = moved(piece, across)
    far_own, patches, intensity = call(
        own_kernel,
        "own",
        [SMEM, VMEM] + [HBM] * 3,
        [(floats(*FAR), HBM), (floats(*PATCH), HBM), (floats(PLANE_SIZE, COUNT, ROWS, SIDE), VMEM)],
        [
            scratch(2, WIDTH, WIDTH),
            scratch(2, SIDE, SIDE),
            TABLE,
            scratch(*FAR),
            scratch(*PATCH),
            DMA((3,)),
            DMA((2, PAIRS)),
        ],
        (positions, halo, object_field, probe, table),
        work,
    )
    shares = lax.all_to_all(intensity, PLANE, 0, 0)
    summed, first = call(
        collect_kernel,
        "collect",
        [VMEM] * 2,
        [(floats(COUNT, ROWS, SIDE), VMEM), (floats(HALF, SIDE), VMEM)],
        [],
        (shares, first),
    )
    arrived = moved(summed, other_half)
    others = [moved(first, move) for move in (next_chip, other_core, next_other)]
    far_other, probe_other, measured = call(
        other_kernel,
        "other",
        [SMEM] + [HBM] * 3 + [VMEM] * 4,
        [(floats(*FAR), HBM), (floats(2, SIDE, SIDE), HBM), (floats(COUNT, ROWS, SIDE), VMEM)],
        [
            scratch(*PATCH),
            scratch(COUNT, 2 * ROWS, SIDE),
            TABLE,
            scratch(2, SIDE, SIDE),
            scratch(*FAR),
            DMA((3,)),
            DMA((PAIRS + 1,)),
        ],
        (flags, patches, amplitude, table, first, *others),
        work,
    )
    (change,) = call(
        change_kernel,
        "change",
        [VMEM] * 3,
        [(floats(PLANE_SIZE, COUNT, ROWS, SIDE), VMEM)],
        [],
        (summed, arrived, measured),
    )
    change = lax.all_to_all(change, PLANE, 0, 0)
    (gradient,) = call(
        inverse_kernel,
        "inverse",
        [SMEM] * 2 + [VMEM] + [HBM] * 5,
        [(floats(PLANE_SIZE, 2, 2, 8, WIDTH), VMEM)],
        [
            scratch(2, WIDTH, WIDTH),
            scratch(2, *FAR),
            scratch(2, 2, SIDE, SIDE),
            TABLE,
            DMA((3,)),
            DMA((2, PAIRS)),
        ],
        (positions, flags, change, far_own, far_other, probe, probe_other, table),
        2 * work,
    )
    gradient = jnp.sum(lax.all_to_all(gradient, PLANE, 0, 0), 0)
    total = gradient[0] + moved(gradient[1], along_ring(1))
    own = lax.dynamic_slice_in_dim(object_field, ((y * 2 + zhi) * 4 + x) * 8, 8, 1)
    return own + 0.5 * total / MODES


def solution(mesh):
    fine = Mesh(mesh.devices.reshape(SIZES), AXES)
    tile, spec = ("zlo", "core"), ("y", "zhi", "x")
    placed = (
        P(None, tile, None),
        P(spec, None, None, None),
        P(tile, None, None),
        P(tile, None),
    )
    return jax.shard_map(
        body, mesh=fine, in_specs=placed, out_specs=P(None, tile + spec, None), check_vma=False
    )
```

time: 179 us -> 168 us (0.939)
  the two profiles are of different devices: /device:TPU:2 before, /device:TPU:224 now
where the time goes in v3:
time: 168 us
  starting transfers between devices  49.9 us (30%)
  waiting for transfers between devices  44.7 us (27%)
  blocking collectives  44 us (26%)
  Pallas kernels  17.4 us (10%)
  local copies, waits for them, and re-layouts  9.83 us (6%)
    ppermute x7, waiting for transfers between devices, moved(): return lax.ppermute(value, AXES, pairs_of(move))  44.7 us
    ppermute x7, starting transfers between devices, moved(): return lax.ppermute(value, AXES, pairs_of(move))  42.7 us
    all_to_all x1, blocking collectives, body(): change = lax.all_to_all(change, PLANE, 0, 0)  24.5 us
    all_to_all x1, blocking collectives, body(): gradient = jnp.sum(lax.all_to_all(gradient, PLANE, 0, 0), 0)  19.5 us
    pallas_call x5, Pallas kernels, call(): pl.pallas_call(kernel, out_shape=[shape for shape, _ in outs], in_specs=i...  17.4 us
    unnamed x23, local copies, waits for them, and re-layouts  9.72 us
    all_to_all x1, starting transfers between devices, body(): shares = lax.all_to_all(intensity, PLANE, 0, 0)  7.17 us
  transfers between devices with their start and end apart: 8, of which 4 were waited for; matrix products, arithmetic and copies ran while one was open for 1% of the time, Pallas kernels for 2%

profile of v3, /device:TPU:224, one launch (start us, length us, event | category | flops | bytes accessed | tf_op | source)
XLA Modules:
  0.0 167.5 jit_solution(14740155852413372013)
XLA Ops:
  0.0 0.0 collective-permute-start
  0.0 0.8 copy.7.pos
  0.8 11.9 %collective-permute-done.halo = f32[2,256,512]{2,1,0:T(8,128)S(1)} collective-permute-done((f32[2,256,512]{2,1,0:T(8,128)}, f32[2,256,512]{2,1,0:T(8,128)S(1)}, u32[]{:S(2)}, u32[]{:S(2)}) %collective-permute-start) | collective-permute-done | bytes 1048608 | tf_op jit(solution)/shard_map/ppermute | solution.py:66
  12.6 1.0 copy-done
  13.7 1.2 copy-done.2
  14.9 1.2 copy-done.4
  16.1 6.1 %own.1 = (f32[2,2,512,256]{3,2,1,0:T(8,128)S(1)}, f32[2,2,2,256,256]{4,3,2,1,0:T(8,128)S(1)}, f32[16,4,16,256]{3,2,1,0:T(8,128)}) custom-call(s32[4,2]{1,0:T(4,128)S(1)} %copy.7.pos, f32[2,256,512]{2,1,0:T(8,128)S(1)} %collective-permute-done.halo, f32[2,256,512]{2,1,0:T(8,128)S(1)} %copy-done.2, f32[2,256,256]{2,1,0:T(8,128)S(1)} %bitcast.18, ...), custom_call_target="tpu_custom_call" | custom-call | flops 1610612736 | bytes 3670048 | tf_op jit(solution)/shard_map/own/pallas_call | solution.py:363
  22.3 1.3 copy-done.7
  23.6 1.3 copy-done.9
  24.9 7.2 %all-to-all-start = ((f32[16,4,16,256]{3,2,1,0:T(8,128)}), f32[16,4,16,256]{3,2,1,0:T(8,128)S(1)}, u32[]{:S(2)}, u32[]{:S(2)}) async-start(f32[16,4,16,256]{3,2,1,0:T(8,128)} %get-tuple-element.13), calls=%async_computation | async-start | bytes 2097152 | tf_op jit(solution)/shard_map/all_to_all | solution.py:405
  32.2 15.9 %collective-permute-start.1 = (f32[128,256]{1,0:T(8,128)S(1)}, f32[128,256]{1,0:T(8,128)S(1)}, u32[]{:S(2)}, u32[]{:S(2)}) collective-permute-start(f32[128,256]{1,0:T(8,128)S(1)} %dynamic-slice_bitcast_fusion), channel_id=1, source_target_pairs={{0,516},{1,517},{2,518},{3,519},{4,512},{5,513},{6,514},{7,515},{8... | collective-permute-start | bytes 393224 | tf_op jit(solution)/shard_map/ppermute | solution.py:66
  48.1 23.4 %collective-permute-done.1.piece_in = f32[128,256]{1,0:T(8,128)S(1)} collective-permute-done((f32[128,256]{1,0:T(8,128)S(1)}, f32[128,256]{1,0:T(8,128)S(1)}, u32[]{:S(2)}, u32[]{:S(2)}) %collective-permute-start.1) | collective-permute-done | bytes 131104 | tf_op jit(solution)/shard_map/ppermute | solution.py:66
  71.5 0.1 collect.1
  71.6 1.9 %collective-permute-start.3 = (f32[128,256]{1,0:T(8,128)S(1)}, f32[128,256]{1,0:T(8,128)S(1)}, u32[]{:S(2)}, u32[]{:S(2)}) collective-permute-start(f32[128,256]{1,0:T(8,128)S(1)} %get-tuple-element.16.first), channel_id=1, source_target_pairs={{0,64},{1,65},{2,66},{3,67},{4,68},{5,69},{6,70},{7,71},{8,72},{9,... | collective-permute-start | bytes 393224 | tf_op jit(solution)/shard_map/ppermute | solution.py:66
  73.5 2.3 %collective-permute-start.4 = (f32[128,256]{1,0:T(8,128)S(1)}, f32[128,256]{1,0:T(8,128)S(1)}, u32[]{:S(2)}, u32[]{:S(2)}) collective-permute-start(f32[128,256]{1,0:T(8,128)S(1)} %get-tuple-element.16.first), channel_id=1, source_target_pairs={{0,32},{1,33},{2,34},{3,35},{4,36},{5,37},{6,38},{7,39},{8,40},{9,... | collective-permute-start | bytes 393224 | tf_op jit(solution)/shard_map/ppermute | solution.py:66
  75.9 3.6 %collective-permute-start.5 = (f32[128,256]{1,0:T(8,128)S(1)}, f32[128,256]{1,0:T(8,128)S(1)}, u32[]{:S(2)}, u32[]{:S(2)}) collective-permute-start(f32[128,256]{1,0:T(8,128)S(1)} %get-tuple-element.16.first), channel_id=1, source_target_pairs={{0,96},{1,97},{2,98},{3,99},{4,100},{5,101},{6,102},{7,103},{8,104... | collective-permute-start | bytes 393224 | tf_op jit(solution)/shard_map/ppermute | solution.py:66
  79.5 0.1 stack.23.flags
  79.6 18.9 %collective-permute-start.2 = (f32[4,16,256]{2,1,0:T(8,128)S(1)}, f32[4,16,256]{2,1,0:T(8,128)S(1)}, u32[]{:S(2)}, u32[]{:S(2)}) collective-permute-start(f32[4,16,256]{2,1,0:T(8,128)S(1)} %get-tuple-element.14.summed), channel_id=1, source_target_pairs={{0,4},{1,5},{2,6},{3,7},{4,0},{5,1},{6,2},{7,3},{8,12},{9,13},{10,... | collective-permute-start | bytes 196616 | tf_op jit(solution)/shard_map/ppermute | solution.py:66
  98.5 0.0 copy-start.5
  98.5 1.2 copy-done.5
  99.7 1.6 copy-done.8
  101.3 4.0 %other.1 = (f32[2,2,512,256]{3,2,1,0:T(8,128)S(1)}, f32[2,256,256]{2,1,0:T(8,128)S(1)}, f32[4,16,256]{2,1,0:T(8,128)S(1)}) custom-call(s32[5]{0:T(128)S(1)} %stack.23.flags, f32[2,2,2,256,256]{4,3,2,1,0:T(8,128)S(1)} %copy-done.8, f32[4,256,256]{2,1,0:T(8,128)S(1)} %copy-done.3, bf16[2,2,2,256,256]{4,3,2,1,0:T(8,128)(2,1)S(1)} %copy-done.5, ...), custom_call_target="tpu_custom_call" | custom-call | flops 1610612736 | bytes 4718612 | tf_op jit(solution)/shard_map/other/pallas_call | solution.py:363
  105.3 0.0 copy-start.6
  105.3 6.1 %collective-permute-done.2.arrived = f32[4,16,256]{2,1,0:T(8,128)S(1)} collective-permute-done((f32[4,16,256]{2,1,0:T(8,128)S(1)}, f32[4,16,256]{2,1,0:T(8,128)S(1)}, u32[]{:S(2)}, u32[]{:S(2)}) %collective-permute-start.2) | collective-permute-done | bytes 65568 | tf_op jit(solution)/shard_map/ppermute | solution.py:66
  111.4 0.1 change.1
  111.6 24.5 %all_to_all.15.change = f32[16,4,16,256]{3,2,1,0:T(8,128)S(1)} all-to-all(f32[16,4,16,256]{3,2,1,0:T(8,128)S(1)} %change.1), channel_id=1, replica_groups=mesh['zlo'=16,'core'=2,'y'=4,'zhi'=2,'x'=4] {'y','x'}, dimensions={0} | all-to-all | bytes 2097152 | tf_op jit(solution)/shard_map/all_to_all | solution.py:441
  136.0 7.1 %inverse.1 = f32[16,2,2,8,512]{4,3,2,1,0:T(8,128)S(1)} custom-call(s32[4,2]{1,0:T(4,128)S(1)} %copy.7.pos, s32[5]{0:T(128)S(1)} %stack.23.flags, f32[16,4,16,256]{3,2,1,0:T(8,128)S(1)} %all_to_all.15.change, f32[2,2,512,256]{3,2,1,0:T(8,128)S(1)} %copy-done.10, f32[2,2,512,256]{3,2,1,0:T(8,128)S(1)} %get-tuple-element.19.far_other_hbm, ...), custom_call_target="tpu_custom_call" | custom-call | flops 3221225472 | bytes 7340084 | tf_op jit(solution)/shard_map/inverse/pallas_call | solution.py:363
  143.2 19.5 %all_to_all.16 = f32[16,2,2,8,512]{4,3,2,1,0:T(8,128)S(1)} all-to-all(f32[16,2,2,8,512]{4,3,2,1,0:T(8,128)S(1)} %inverse.1), channel_id=1, replica_groups=mesh['zlo'=16,'core'=2,'y'=4,'zhi'=2,'x'=4] {'y','x'}, dimensions={0} | all-to-all | bytes 2097152 | tf_op jit(solution)/shard_map/all_to_all | solution.py:458
  162.7 0.1 reduce_sum.9
  162.8 0.0 collective-permute-start.6
  162.8 3.3 %collective-permute-done.6 = f32[2,8,512]{2,1,0:T(8,128)S(1)} collective-permute-done((f32[2,8,512]{2,1,0:T(8,128)S(1)}, f32[2,8,512]{2,1,0:T(8,128)S(1)}, u32[]{:S(2)}, u32[]{:S(2)}) %collective-permute-start.6) | collective-permute-done | bytes 32800 | tf_op jit(solution)/shard_map/ppermute | solution.py:66
  166.1 1.4 fusion.2
  (19 shorter events, 0.1 us)
Async XLA Ops:
  0.0 12.6 %collective-permute-start = (f32[2,256,512]{2,1,0:T(8,128)}, f32[2,256,512]{2,1,0:T(8,128)S(1)}, u32[]{:S(2)}, u32[]{:S(2)}) collective-permute-start(f32[2,256,512]{2,1,0:T(8,128)} %own_hbm.1), channel_id=1, source_target_pairs={{0,996},{1,997},{2,998},{3,999},{4,992},{5,993},{6,994},{7,995},{8... | collective-permute-start | bytes 3145736 | tf_op jit(solution)/shard_map/ppermute | solution.py:66
  12.6 1.0 copy-start
  13.7 1.2 copy-start.2
  14.9 1.2 copy-start.4
  22.3 1.3 copy-start.7
  23.6 1.3 copy-start.9
  24.9 7.2 %copy-start.1 = (f32[1,2,256,256]{3,2,1,0:T(8,128)S(1)}, f32[1,2,256,256]{3,2,1,0:T(8,128)}, u32[]{:S(2)}) copy-start(f32[1,2,256,256]{3,2,1,0:T(8,128)} %param.6) | copy-start | bytes 1572868
  24.9 73.5 %copy-start.3 = (f32[4,256,256]{2,1,0:T(8,128)S(1)}, f32[4,256,256]{2,1,0:T(8,128)}, u32[]{:S(2)}) copy-start(f32[4,256,256]{2,1,0:T(8,128)} %amp_hbm.1) | copy-start | bytes 3145732
  24.9 46.6 %all-to-all-start = ((f32[16,4,16,256]{3,2,1,0:T(8,128)}), f32[16,4,16,256]{3,2,1,0:T(8,128)S(1)}, u32[]{:S(2)}, u32[]{:S(2)}) async-start(f32[16,4,16,256]{3,2,1,0:T(8,128)} %get-tuple-element.13), calls=%async_computation | async-start | bytes 2097152 | tf_op jit(solution)/shard_map/all_to_all | solution.py:405
  32.2 39.3 %collective-permute-start.1 = (f32[128,256]{1,0:T(8,128)S(1)}, f32[128,256]{1,0:T(8,128)S(1)}, u32[]{:S(2)}, u32[]{:S(2)}) collective-permute-start(f32[128,256]{1,0:T(8,128)S(1)} %dynamic-slice_bitcast_fusion), channel_id=1, source_target_pairs={{0,516},{1,517},{2,518},{3,519},{4,512},{5,513},{6,514},{7,515},{8... | collective-permute-start | bytes 393224 | tf_op jit(solution)/shard_map/ppermute | solution.py:66
  71.6 26.9 %collective-permute-start.3 = (f32[128,256]{1,0:T(8,128)S(1)}, f32[128,256]{1,0:T(8,128)S(1)}, u32[]{:S(2)}, u32[]{:S(2)}) collective-permute-start(f32[128,256]{1,0:T(8,128)S(1)} %get-tuple-element.16.first), channel_id=1, source_target_pairs={{0,64},{1,65},{2,66},{3,67},{4,68},{5,69},{6,70},{7,71},{8,72},{9,... | collective-permute-start | bytes 393224 | tf_op jit(solution)/shard_map/ppermute | solution.py:66
  73.5 24.9 %collective-permute-start.4 = (f32[128,256]{1,0:T(8,128)S(1)}, f32[128,256]{1,0:T(8,128)S(1)}, u32[]{:S(2)}, u32[]{:S(2)}) collective-permute-start(f32[128,256]{1,0:T(8,128)S(1)} %get-tuple-element.16.first), channel_id=1, source_target_pairs={{0,32},{1,33},{2,34},{3,35},{4,36},{5,37},{6,38},{7,39},{8,40},{9,... | collective-permute-start | bytes 393224 | tf_op jit(solution)/shard_map/ppermute | solution.py:66
  75.9 22.6 %collective-permute-start.5 = (f32[128,256]{1,0:T(8,128)S(1)}, f32[128,256]{1,0:T(8,128)S(1)}, u32[]{:S(2)}, u32[]{:S(2)}) collective-permute-start(f32[128,256]{1,0:T(8,128)S(1)} %get-tuple-element.16.first), channel_id=1, source_target_pairs={{0,96},{1,97},{2,98},{3,99},{4,100},{5,101},{6,102},{7,103},{8,104... | collective-permute-start | bytes 393224 | tf_op jit(solution)/shard_map/ppermute | solution.py:66
  79.6 31.9 %collective-permute-start.2 = (f32[4,16,256]{2,1,0:T(8,128)S(1)}, f32[4,16,256]{2,1,0:T(8,128)S(1)}, u32[]{:S(2)}, u32[]{:S(2)}) collective-permute-start(f32[4,16,256]{2,1,0:T(8,128)S(1)} %get-tuple-element.14.summed), channel_id=1, source_target_pairs={{0,4},{1,5},{2,6},{3,7},{4,0},{5,1},{6,2},{7,3},{8,12},{9,13},{10,... | collective-permute-start | bytes 196616 | tf_op jit(solution)/shard_map/ppermute | solution.py:66
  98.5 1.2 copy-start.5
  99.7 1.6 copy-start.8
  105.3 30.7 %copy-start.6 = (bf16[2,2,2,256,256]{4,3,2,1,0:T(8,128)(2,1)S(1)}, bf16[2,2,2,256,256]{4,3,2,1,0:T(8,128)(2,1)}, u32[]{:S(2)}) copy-start(bf16[2,2,2,256,256]{4,3,2,1,0:T(8,128)(2,1)} %constant.50.clone.table_hbm) | copy-start | bytes 3145732
  105.3 30.7 %copy-start.10 = (f32[2,2,512,256]{3,2,1,0:T(8,128)S(1)}, f32[2,2,512,256]{3,2,1,0:T(8,128)}, u32[]{:S(2)}) copy-start(f32[2,2,512,256]{3,2,1,0:T(8,128)} %copy-done.9) | copy-start | bytes 6291460
  162.8 3.4 %collective-permute-start.6 = (f32[2,8,512]{2,1,0:T(8,128)S(1)}, f32[2,8,512]{2,1,0:T(8,128)S(1)}, u32[]{:S(2)}, u32[]{:S(2)}) collective-permute-start(f32[2,8,512]{2,1,0:T(8,128)S(1)} %slice_bitcast_fusion), channel_id=1, source_target_pairs={{0,32},{1,33},{2,34},{3,35},{4,36},{5,37},{6,38},{7,39},{8,40},{9,... | collective-permute-start | bytes 98312 | tf_op jit(solution)/shard_map/ppermute | solution.py:66

commit v4 on v3

--- a/solution.py
+++ b/solution.py
@@ -14,6 +14,7 @@
 PLANE = ("y", "x")
 SIDE = 256
 HALF = SIDE // 2
+QUARTER = SIDE // 4
 WIDTH = 512
 COUNT = 4
 MODES = 32
@@ -52,8 +53,12 @@
     return zlo ^ 1, core, y, zhi, x
 
 
-def next_other(zlo, core, y, zhi, x):
-    return zlo ^ 1, 1 - core, y, zhi, x
+def two_on(zlo, core, y, zhi, x):
+    return zlo ^ 2, core, y, zhi, x
+
+
+def two_on_other(zlo, core, y, zhi, x):
+    return zlo ^ 2, 1 - core, y, zhi, x
 
 
 def across(zlo, core, y, zhi, x):
@@ -184,7 +189,7 @@
 
 
 def own_kernel(
-    pos, halo, own_hbm, probe_hbm, table_hbm,
+    pos, halo, own_hbm, probe_hbm, table_hbm, _,
     far_hbm, patch_hbm, intensity, ext, probe, table, far, patch, sems, out_sems,
 ):
     pairs = (
@@ -234,10 +239,10 @@
 
 
 def other_kernel(
-    flags, patch_hbm, amp_hbm, table_hbm, first, second, crossed_first, crossed_second,
+    flags, patch_hbm, amp_hbm, table_hbm, block, next_block,
     far_hbm, probe_hbm, measured, patch, amp, table, probe, far, sems, out_sems,
 ):
-    core, plane, odd = flags[0], flags[2], flags[4]
+    core, plane, quarter = flags[0], flags[2], flags[4]
     start = pl.multiple_of(lax.rem(plane, 8) * 2 * ROWS, 2 * ROWS)
     pairs = (
         (amp_hbm.at[:, pl.ds(start, 2 * ROWS)], amp),
@@ -250,11 +255,11 @@
     for copy in copies[1:]:
         copy.wait()
     for channel in range(2):
-        for half in range(2):
-            of_own = jnp.where(odd == half, first[...], second[...])
-            of_other = jnp.where(odd == half, crossed_first[...], crossed_second[...])
-            value = jnp.where(core == channel, of_own, of_other)
-            probe[channel, half * HALF : (half + 1) * HALF] = value
+        for part in range(SIDE // QUARTER):
+            apart = jnp.bitwise_xor(quarter, part)
+            place = jnp.bitwise_xor(core, channel), apart // 2
+            value = jnp.where(apart % 2 == 0, block[place], next_block[place])
+            probe[channel, part * QUARTER : (part + 1) * QUARTER] = value
     probe_copy = pltpu.make_async_copy(probe, probe_hbm, out_sems.at[COUNT // 2])
     probe_copy.start()
 
@@ -274,9 +279,12 @@
     probe_copy.wait()
 
 
-def collect_kernel(shares, piece_in, summed, piece_out):
+def collect_kernel(shares, first, second, crossed_first, crossed_second, summed, block):
     summed[...] = jnp.sum(shares[...], 0)
-    piece_out[...] = piece_in[...]
+    block[0, 0] = first[...]
+    block[0, 1] = second[...]
+    block[1, 0] = crossed_first[...]
+    block[1, 1] = crossed_second[...]
 
 
 def change_kernel(summed, arrived, measured, out):
@@ -342,6 +350,7 @@
 SMEM = pl.BlockSpec(memory_space=pltpu.SMEM)
 HBM = pl.BlockSpec(memory_space=pltpu.HBM)
 PAIRS = COUNT // 2
+LIMIT = 60
 FAR = (PAIRS, 2, 2 * SIDE, SIDE)
 PATCH = (PAIRS, 2, 2, SIDE, SIDE)
 DMA = pltpu.SemaphoreType.DMA
@@ -358,7 +367,7 @@
 TABLE = pltpu.VMEM((2, 2, 2, SIDE, SIDE), jnp.bfloat16)
 
 
-def call(kernel, name, in_specs, outs, scratches, operands, work=0, limit=32):
+def call(kernel, name, in_specs, outs, scratches, operands, work=0, limit=LIMIT):
     moves = sum(math.prod(v.shape) * v.dtype.itemsize for v in operands)
     return pl.pallas_call(
         kernel,
@@ -377,18 +386,18 @@
     work = COUNT * 12 * 2 * SIDE**3
     zlo, core = lax.axis_index("zlo"), lax.axis_index("core")
     y, zhi, x = (lax.axis_index(name) for name in ("y", "zhi", "x"))
-    odd = lax.rem(zlo, 2)
+    quarter = lax.rem(zlo, 4)
     lower_half = jnp.where((zlo == 15) & (core == 1), 1 - zhi, zhi)
-    flags = jnp.stack([core, zhi, y * 4 + x, lower_half, odd]).astype(jnp.int32)
+    flags = jnp.stack([core, zhi, y * 4 + x, lower_half, quarter]).astype(jnp.int32)
     probe = probe_modes[0]
 
     halo = moved(object_field, along_ring(-1))
-    piece = lax.dynamic_slice(probe, (core, odd * HALF, 0), (1, HALF, SIDE))[0]
+    piece = lax.dynamic_slice(probe, (core, quarter * QUARTER, 0), (1, QUARTER, SIDE))[0]
     first = moved(piece, across)
     far_own, patches, intensity = call(
         own_kernel,
         "own",
-        [SMEM, VMEM] + [HBM] * 3,
+        [SMEM, VMEM] + [HBM] * 4,
         [(floats(*FAR), HBM), (floats(*PATCH), HBM), (floats(PLANE_SIZE, COUNT, ROWS, SIDE), VMEM)],
         [
             scratch(2, WIDTH, WIDTH),
@@ -399,24 +408,26 @@
             DMA((3,)),
             DMA((2, PAIRS)),
         ],
-        (positions, halo, object_field, probe, table),
+        (positions, halo, object_field, probe, table, first),
         work,
     )
     shares = lax.all_to_all(intensity, PLANE, 0, 0)
-    summed, first = call(
+    spread = [moved(first, move) for move in (two_on, other_core, two_on_other)]
+    summed, block = call(
         collect_kernel,
         "collect",
-        [VMEM] * 2,
-        [(floats(COUNT, ROWS, SIDE), VMEM), (floats(HALF, SIDE), VMEM)],
+        [VMEM] * 5,
+        [(floats(COUNT, ROWS, SIDE), VMEM), (floats(2, 2, QUARTER, SIDE), VMEM)],
         [],
-        (shares, first),
+        (shares, first, *spread),
+        limit=32,
     )
     arrived = moved(summed, other_half)
-    others = [moved(first, move) for move in (next_chip, other_core, next_other)]
+    next_block = moved(block, next_chip)
     far_other, probe_other, measured = call(
         other_kernel,
         "other",
-        [SMEM] + [HBM] * 3 + [VMEM] * 4,
+        [SMEM] + [HBM] * 3 + [VMEM] * 2,
         [(floats(*FAR), HBM), (floats(2, SIDE, SIDE), HBM), (floats(COUNT, ROWS, SIDE), VMEM)],
         [
             scratch(*PATCH),
@@ -427,7 +438,7 @@
             DMA((3,)),
             DMA((PAIRS + 1,)),
         ],
-        (flags, patches, amplitude, table, first, *others),
+        (flags, patches, amplitude, table, block, next_block),
         work,
     )
     (change,) = call(
@@ -437,6 +448,7 @@
         [(floats(PLANE_SIZE, COUNT, ROWS, SIDE), VMEM)],
         [],
         (summed, arrived, measured),
+        limit=32,
     )
     change = lax.all_to_all(change, PLANE, 0, 0)
     (gradient,) = call(

time: 168 us -> 164 us (0.976)
  the two profiles are of different devices: /device:TPU:224 before, /device:TPU:288 now
where the time goes in v4:
time: 164 us; the launch traced here: 163 us
  starting transfers between devices  46.9 us (29%)
  blocking collectives  44.9 us (27%)
  waiting for transfers between devices  36.7 us (22%)
  Pallas kernels  27.4 us (17%)
  local copies, waits for them, and re-layouts  5.34 us (3%)
    ppermute x8, starting transfers between devices, moved(): return lax.ppermute(value, AXES, pairs_of(move))  39.7 us
    ppermute x8, waiting for transfers between devices, moved(): return lax.ppermute(value, AXES, pairs_of(move))  34.6 us
    pallas_call x5, Pallas kernels, call(): pl.pallas_call(kernel, out_shape=[shape for shape, _ in outs], in_specs=i...  27.4 us
    all_to_all x1, blocking collectives, body(): change = lax.all_to_all(change, PLANE, 0, 0)  25 us
    all_to_all x1, blocking collectives, body(): gradient = jnp.sum(lax.all_to_all(gradient, PLANE, 0, 0), 0)  19.9 us
    all_to_all x1, starting transfers between devices, body(): shares = lax.all_to_all(intensity, PLANE, 0, 0)  7.18 us
    unnamed x13, local copies, waits for them, and re-layouts  3.9 us
  transfers between devices with their start and end apart: 9, of which 5 were waited for; matrix products, arithmetic and copies ran while one was open for 2% of the time, Pallas kernels for 4%

profile of v4, /device:TPU:288, one launch (start us, length us, event | category | flops | bytes accessed | tf_op | source)
XLA Modules:
  0.0 162.9 jit_solution(1331042190814888858)
XLA Ops:
  0.0 0.8 dynamic-slice_bitcast_fusion
  0.8 15.3 %collective-permute-start.1 = (f32[64,256]{1,0:T(8,128)S(1)}, f32[64,256]{1,0:T(8,128)S(1)}, u32[]{:S(2)}, u32[]{:S(2)}) collective-permute-start(f32[64,256]{1,0:T(8,128)S(1)} %dynamic-slice_bitcast_fusion), channel_id=1, source_target_pairs={{0,516},{1,517},{2,518},{3,519},{4,512},{5,513},{6,514},{7,515},{8... | collective-permute-start | bytes 196616 | tf_op jit(solution)/shard_map/ppermute | solution.py:71
  16.1 1.3 copy.7.pos
  17.5 18.7 %collective-permute-done.1._.first = f32[64,256]{1,0:T(8,128)S(1)} collective-permute-done((f32[64,256]{1,0:T(8,128)S(1)}, f32[64,256]{1,0:T(8,128)S(1)}, u32[]{:S(2)}, u32[]{:S(2)}) %collective-permute-start.1) | collective-permute-done | bytes 65568 | tf_op jit(solution)/shard_map/ppermute | solution.py:71
  36.2 0.6 copy-done
  36.8 0.4 copy-done.4
  37.2 9.3 %own.1 = (f32[2,2,512,256]{3,2,1,0:T(8,128)}, f32[2,2,2,256,256]{4,3,2,1,0:T(8,128)}, f32[16,4,16,256]{3,2,1,0:T(8,128)}) custom-call(s32[4,2]{1,0:T(4,128)} %copy.7.pos, f32[2,256,512]{2,1,0:T(8,128)} %copy-done.4, f32[2,256,512]{2,1,0:T(8,128)} %own_hbm.1, f32[2,256,256]{2,1,0:T(8,128)} %bitcast.18, bf16[2,2,2,256,256]{4,3,2,1,0:T(8,128)(2,1)} %constant.51.clone.table_hbm, ...), custom_call_target="tpu_custom_call" | custom-call | flops 1610612736 | bytes 3735584 | tf_op jit(solution)/shard_map/own/pallas_call | solution.py:372
  46.5 7.2 %all-to-all-start = ((f32[16,4,16,256]{3,2,1,0:T(8,128)}), f32[16,4,16,256]{3,2,1,0:T(8,128)S(1)}, u32[]{:S(2)}, u32[]{:S(2)}) async-start(f32[16,4,16,256]{3,2,1,0:T(8,128)} %get-tuple-element.13), calls=%async_computation | async-start | bytes 2097152 | tf_op jit(solution)/shard_map/all_to_all | solution.py:414
  53.7 1.9 %collective-permute-start.2 = (f32[64,256]{1,0:T(8,128)S(1)}, f32[64,256]{1,0:T(8,128)S(1)}, u32[]{:S(2)}, u32[]{:S(2)}) collective-permute-start(f32[64,256]{1,0:T(8,128)S(1)} %copy-done.1), channel_id=1, source_target_pairs={{0,128},{1,129},{2,130},{3,131},{4,132},{5,133},{6,134},{7,135},{8... | collective-permute-start | bytes 196616 | tf_op jit(solution)/shard_map/ppermute | solution.py:71
  55.7 1.9 %collective-permute-start.3 = (f32[64,256]{1,0:T(8,128)S(1)}, f32[64,256]{1,0:T(8,128)S(1)}, u32[]{:S(2)}, u32[]{:S(2)}) collective-permute-start(f32[64,256]{1,0:T(8,128)S(1)} %copy-done.1), channel_id=1, source_target_pairs={{0,32},{1,33},{2,34},{3,35},{4,36},{5,37},{6,38},{7,39},{8,40},{9,... | collective-permute-start | bytes 196616 | tf_op jit(solution)/shard_map/ppermute | solution.py:71
  57.6 4.9 %collective-permute-start.4 = (f32[64,256]{1,0:T(8,128)S(1)}, f32[64,256]{1,0:T(8,128)S(1)}, u32[]{:S(2)}, u32[]{:S(2)}) collective-permute-start(f32[64,256]{1,0:T(8,128)S(1)} %copy-done.1), channel_id=1, source_target_pairs={{0,160},{1,161},{2,162},{3,163},{4,164},{5,165},{6,166},{7,167},{8... | collective-permute-start | bytes 196616 | tf_op jit(solution)/shard_map/ppermute | solution.py:71
  62.5 0.0 collective-permute-done.2.second
  62.5 0.0 collective-permute-done.3.crossed_first
  62.6 2.4 %collective-permute-done.4.crossed_second = f32[64,256]{1,0:T(8,128)S(1)} collective-permute-done((f32[64,256]{1,0:T(8,128)S(1)}, f32[64,256]{1,0:T(8,128)S(1)}, u32[]{:S(2)}, u32[]{:S(2)}) %collective-permute-start.4) | collective-permute-done | bytes 65568 | tf_op jit(solution)/shard_map/ppermute | solution.py:71
  64.9 2.1 %all-to-all-done.shares = f32[16,4,16,256]{3,2,1,0:T(8,128)S(1)} async-done(((f32[16,4,16,256]{3,2,1,0:T(8,128)}), f32[16,4,16,256]{3,2,1,0:T(8,128)S(1)}, u32[]{:S(2)}, u32[]{:S(2)}) %all-to-all-start) | async-done | bytes 1048608 | tf_op jit(solution)/shard_map/all_to_all | solution.py:414
  67.1 0.1 collect.1
  67.2 3.9 %collective-permute-start.6 = (f32[2,2,64,256]{3,2,1,0:T(8,128)S(1)}, f32[2,2,64,256]{3,2,1,0:T(8,128)S(1)}, u32[]{:S(2)}, u32[]{:S(2)}) collective-permute-start(f32[2,2,64,256]{3,2,1,0:T(8,128)S(1)} %get-tuple-element.16.block), channel_id=1, source_target_pairs={{0,64},{1,65},{2,66},{3,67},{4,68},{5,69},{6,70},{7,71},{8,72},{9,... | collective-permute-start | bytes 786440 | tf_op jit(solution)/shard_map/ppermute | solution.py:71
  71.1 0.6 stack.23.flags
  71.6 11.8 %collective-permute-start.5 = (f32[4,16,256]{2,1,0:T(8,128)S(1)}, f32[4,16,256]{2,1,0:T(8,128)S(1)}, u32[]{:S(2)}, u32[]{:S(2)}) collective-permute-start(f32[4,16,256]{2,1,0:T(8,128)S(1)} %get-tuple-element.14.summed), channel_id=1, source_target_pairs={{0,4},{1,5},{2,6},{3,7},{4,0},{5,1},{6,2},{7,3},{8,12},{9,13},{10,... | collective-permute-start | bytes 196616 | tf_op jit(solution)/shard_map/ppermute | solution.py:71
  83.5 0.0 collective-permute-done.6.next_block
  83.5 0.7 copy-done.5
  84.2 7.2 %other.1 = (f32[2,2,512,256]{3,2,1,0:T(8,128)}, f32[2,256,256]{2,1,0:T(8,128)}, f32[4,16,256]{2,1,0:T(8,128)}) custom-call(s32[5]{0:T(128)} %stack.23.flags, f32[2,2,2,256,256]{4,3,2,1,0:T(8,128)} %get-tuple-element.15.patch_hbm, f32[4,256,256]{2,1,0:T(8,128)} %amp_hbm.1, bf16[2,2,2,256,256]{4,3,2,1,0:T(8,128)(2,1)} %constant.51.clone.table_hbm, ...), custom_call_target="tpu_custom_call" | custom-call | flops 1610612736 | bytes 4718612 | tf_op jit(solution)/shard_map/other/pallas_call | solution.py:372
  91.4 10.2 %collective-permute-done.5.arrived = f32[4,16,256]{2,1,0:T(8,128)S(1)} collective-permute-done((f32[4,16,256]{2,1,0:T(8,128)S(1)}, f32[4,16,256]{2,1,0:T(8,128)S(1)}, u32[]{:S(2)}, u32[]{:S(2)}) %collective-permute-start.5) | collective-permute-done | bytes 65568 | tf_op jit(solution)/shard_map/ppermute | solution.py:71
  101.6 0.8 copy-done.2
  102.4 0.1 change.1
  102.5 25.0 %all_to_all.15.change = f32[16,4,16,256]{3,2,1,0:T(8,128)} all-to-all(f32[16,4,16,256]{3,2,1,0:T(8,128)S(1)} %change.1), channel_id=1, replica_groups=mesh['zlo'=16,'core'=2,'y'=4,'zhi'=2,'x'=4] {'y','x'}, dimensions={0} | all-to-all | bytes 2097152 | tf_op jit(solution)/shard_map/all_to_all | solution.py:453
  127.6 10.6 %inverse.1 = f32[16,2,2,8,512]{4,3,2,1,0:T(8,128)} custom-call(s32[4,2]{1,0:T(4,128)} %copy.7.pos, s32[5]{0:T(128)} %stack.23.flags, f32[16,4,16,256]{3,2,1,0:T(8,128)} %all_to_all.15.change, f32[2,2,512,256]{3,2,1,0:T(8,128)} %get-tuple-element.18.far_own_hbm, f32[2,2,512,256]{3,2,1,0:T(8,128)} %get-tuple-element.19.far_other_hbm, f32[2,256,256]{2,1,0:T(8,128)} %bitcast.19, ...), custom_call_target="tpu_custom_call" | custom-call | flops 3221225472 | bytes 7340084 | tf_op jit(solution)/shard_map/inverse/pallas_call | solution.py:372
  138.2 19.9 %all_to_all.16 = f32[16,2,2,8,512]{4,3,2,1,0:T(8,128)S(1)} all-to-all(f32[16,2,2,8,512]{4,3,2,1,0:T(8,128)} %inverse.1), channel_id=1, replica_groups=mesh['zlo'=16,'core'=2,'y'=4,'zhi'=2,'x'=4] {'y','x'}, dimensions={0} | all-to-all | bytes 2097152 | tf_op jit(solution)/shard_map/all_to_all | solution.py:470
  158.1 0.1 reduce_sum.9
  158.2 0.0 collective-permute-start.7
  158.2 3.3 %collective-permute-done.7 = f32[2,8,512]{2,1,0:T(8,128)S(1)} collective-permute-done((f32[2,8,512]{2,1,0:T(8,128)S(1)}, f32[2,8,512]{2,1,0:T(8,128)S(1)}, u32[]{:S(2)}, u32[]{:S(2)}) %collective-permute-start.7) | collective-permute-done | bytes 32800 | tf_op jit(solution)/shard_map/ppermute | solution.py:71
  161.6 1.4 fusion.2
  (11 shorter events, 0.0 us)
Async XLA Ops:
  0.0 36.2 %collective-permute-start = (f32[2,256,512]{2,1,0:T(8,128)}, f32[2,256,512]{2,1,0:T(8,128)S(1)}, u32[]{:S(2)}, u32[]{:S(2)}) collective-permute-start(f32[2,256,512]{2,1,0:T(8,128)} %own_hbm.1), channel_id=1, source_target_pairs={{0,996},{1,997},{2,998},{3,999},{4,992},{5,993},{6,994},{7,995},{8... | collective-permute-start | bytes 3145736 | tf_op jit(solution)/shard_map/ppermute | solution.py:71
  0.8 35.3 %collective-permute-start.1 = (f32[64,256]{1,0:T(8,128)S(1)}, f32[64,256]{1,0:T(8,128)S(1)}, u32[]{:S(2)}, u32[]{:S(2)}) collective-permute-start(f32[64,256]{1,0:T(8,128)S(1)} %dynamic-slice_bitcast_fusion), channel_id=1, source_target_pairs={{0,516},{1,517},{2,518},{3,519},{4,512},{5,513},{6,514},{7,515},{8... | collective-permute-start | bytes 196616 | tf_op jit(solution)/shard_map/ppermute | solution.py:71
  36.2 0.6 copy-start
  36.2 1.0 copy-start.4
  46.5 7.2 %copy-start.1 = (f32[64,256]{1,0:T(8,128)S(1)}, f32[64,256]{1,0:T(8,128)}, u32[]{:S(2)}) copy-start(f32[64,256]{1,0:T(8,128)} %copy-done) | copy-start | bytes 196612
  46.5 20.5 %all-to-all-start = ((f32[16,4,16,256]{3,2,1,0:T(8,128)}), f32[16,4,16,256]{3,2,1,0:T(8,128)S(1)}, u32[]{:S(2)}, u32[]{:S(2)}) async-start(f32[16,4,16,256]{3,2,1,0:T(8,128)} %get-tuple-element.13), calls=%async_computation | async-start | bytes 2097152 | tf_op jit(solution)/shard_map/all_to_all | solution.py:414
  53.7 8.8 %collective-permute-start.2 = (f32[64,256]{1,0:T(8,128)S(1)}, f32[64,256]{1,0:T(8,128)S(1)}, u32[]{:S(2)}, u32[]{:S(2)}) collective-permute-start(f32[64,256]{1,0:T(8,128)S(1)} %copy-done.1), channel_id=1, source_target_pairs={{0,128},{1,129},{2,130},{3,131},{4,132},{5,133},{6,134},{7,135},{8... | collective-permute-start | bytes 196616 | tf_op jit(solution)/shard_map/ppermute | solution.py:71
  55.7 6.9 %collective-permute-start.3 = (f32[64,256]{1,0:T(8,128)S(1)}, f32[64,256]{1,0:T(8,128)S(1)}, u32[]{:S(2)}, u32[]{:S(2)}) collective-permute-start(f32[64,256]{1,0:T(8,128)S(1)} %copy-done.1), channel_id=1, source_target_pairs={{0,32},{1,33},{2,34},{3,35},{4,36},{5,37},{6,38},{7,39},{8,40},{9,... | collective-permute-start | bytes 196616 | tf_op jit(solution)/shard_map/ppermute | solution.py:71
  57.6 7.3 %collective-permute-start.4 = (f32[64,256]{1,0:T(8,128)S(1)}, f32[64,256]{1,0:T(8,128)S(1)}, u32[]{:S(2)}, u32[]{:S(2)}) collective-permute-start(f32[64,256]{1,0:T(8,128)S(1)} %copy-done.1), channel_id=1, source_target_pairs={{0,160},{1,161},{2,162},{3,163},{4,164},{5,165},{6,166},{7,167},{8... | collective-permute-start | bytes 196616 | tf_op jit(solution)/shard_map/ppermute | solution.py:71
  67.1 16.4 %copy-start.3 = (f32[2,2,64,256]{3,2,1,0:T(8,128)}, f32[2,2,64,256]{3,2,1,0:T(8,128)S(1)}, u32[]{:S(2)}) copy-start(f32[2,2,64,256]{3,2,1,0:T(8,128)S(1)} %get-tuple-element.16.block) | copy-start | bytes 786436
  67.2 16.3 %collective-permute-start.6 = (f32[2,2,64,256]{3,2,1,0:T(8,128)S(1)}, f32[2,2,64,256]{3,2,1,0:T(8,128)S(1)}, u32[]{:S(2)}, u32[]{:S(2)}) collective-permute-start(f32[2,2,64,256]{3,2,1,0:T(8,128)S(1)} %get-tuple-element.16.block), channel_id=1, source_target_pairs={{0,64},{1,65},{2,66},{3,67},{4,68},{5,69},{6,70},{7,71},{8,72},{9,... | collective-permute-start | bytes 786440 | tf_op jit(solution)/shard_map/ppermute | solution.py:71
  71.6 29.9 %collective-permute-start.5 = (f32[4,16,256]{2,1,0:T(8,128)S(1)}, f32[4,16,256]{2,1,0:T(8,128)S(1)}, u32[]{:S(2)}, u32[]{:S(2)}) collective-permute-start(f32[4,16,256]{2,1,0:T(8,128)S(1)} %get-tuple-element.14.summed), channel_id=1, source_target_pairs={{0,4},{1,5},{2,6},{3,7},{4,0},{5,1},{6,2},{7,3},{8,12},{9,13},{10,... | collective-permute-start | bytes 196616 | tf_op jit(solution)/shard_map/ppermute | solution.py:71
  83.5 0.7 copy-start.5
  101.6 0.8 copy-start.2
  158.2 3.4 %collective-permute-start.7 = (f32[2,8,512]{2,1,0:T(8,128)S(1)}, f32[2,8,512]{2,1,0:T(8,128)S(1)}, u32[]{:S(2)}, u32[]{:S(2)}) collective-permute-start(f32[2,8,512]{2,1,0:T(8,128)S(1)} %slice_bitcast_fusion), channel_id=1, source_target_pairs={{0,32},{1,33},{2,34},{3,35},{4,36},{5,37},{6,38},{7,39},{8,40},{9,... | collective-permute-start | bytes 98312 | tf_op jit(solution)/shard_map/ppermute | solution.py:71

commit v5 on v4

--- a/solution.py
+++ b/solution.py
@@ -181,6 +181,18 @@
     return probe_re * patch_re - probe_im * patch_im, probe_re * patch_im + probe_im * patch_re
 
 
+def windows(pos, ext, pattern):
+    row, col = pos[pattern, 0], pos[pattern, 1]
+    base = pl.multiple_of(row // 8 * 8, 8)
+    left = lax.rem(WIDTH - col, WIDTH)
+    up = lax.rem(SPAN - (row - base), SPAN)
+    out = []
+    for part in range(2):
+        rows = pltpu.roll(ext[part, pl.ds(base, SPAN), :], left, 1)[:, :SIDE]
+        out.append(pltpu.roll(rows, up, 0)[:SIDE])
+    return out
+
+
 def started(pairs, sems):
     copies = [pltpu.make_async_copy(*pair, sems.at[i]) for i, pair in enumerate(pairs)]
     for copy in copies:
@@ -189,38 +201,29 @@
 
 
 def own_kernel(
-    pos, halo, own_hbm, probe_hbm, table_hbm, _,
-    far_hbm, patch_hbm, intensity, ext, probe, table, far, patch, sems, out_sems,
+    pos, own_hbm, halo_hbm, probe_hbm, table_hbm,
+    far_hbm, intensity_hbm, ext, probe, table, far, intensity, sems, out_sems,
 ):
     pairs = (
         (own_hbm, ext.at[:, pl.ds(0, SIDE)]),
+        (halo_hbm, ext.at[:, pl.ds(SIDE, SIDE)]),
         (probe_hbm, probe),
         (table_hbm, table),
     )
-    copies = started(pairs, sems)
-    ext[:, SIDE:] = halo[...]
-    for copy in copies:
+    for copy in started(pairs, sems):
         copy.wait()
 
     def out_copies(q):
+        rows = pl.ds(2 * q, 2)
         return (
+            pltpu.make_async_copy(
+                intensity.at[:, rows], intensity_hbm.at[:, rows], out_sems.at[1, q]
+            ),
             pltpu.make_async_copy(far.at[q], far_hbm.at[q], out_sems.at[0, q]),
-            pltpu.make_async_copy(patch.at[q], patch_hbm.at[q], out_sems.at[1, q]),
         )
 
     def pair(q, carry):
-        waves = []
-        for w in range(2):
-            row, col = pos[2 * q + w, 0], pos[2 * q + w, 1]
-            base = pl.multiple_of(row // 8 * 8, 8)
-            left = lax.rem(WIDTH - col, WIDTH)
-            up = lax.rem(SPAN - (row - base), SPAN)
-            window = []
-            for part in range(2):
-                rows = pltpu.roll(ext[part, pl.ds(base, SPAN), :], left, 1)[:, :SIDE]
-                window.append(pltpu.roll(rows, up, 0)[:SIDE])
-                patch[q, w, part] = window[part]
-            waves.append(lit(probe[0], probe[1], *window))
+        waves = [lit(probe[0], probe[1], *windows(pos, ext, 2 * q + w)) for w in range(2)]
         for parity, out in enumerate(to_frequencies(waves, table)):
             far[q, parity] = out
             strength = out[:, :HALF] * out[:, :HALF] + out[:, HALF:] * out[:, HALF:]
@@ -232,22 +235,27 @@
             copy.start()
         return carry
 
-    lax.fori_loop(0, COUNT // 2, pair, 0)
-    for q in range(COUNT // 2):
+    lax.fori_loop(0, PAIRS, pair, 0)
+    for q in range(PAIRS):
         for copy in out_copies(q):
             copy.wait()
 
 
+def gate_kernel(array, _, out):
+    pass
+
+
 def other_kernel(
-    flags, patch_hbm, amp_hbm, table_hbm, block, next_block,
-    far_hbm, probe_hbm, measured, patch, amp, table, probe, far, sems, out_sems,
+    pos, flags, own_hbm, halo_hbm, amp_hbm, table_hbm, block, next_block,
+    far_hbm, probe_hbm, measured, ext, amp, table, probe, far, sems, out_sems,
 ):
     core, plane, quarter = flags[0], flags[2], flags[4]
     start = pl.multiple_of(lax.rem(plane, 8) * 2 * ROWS, 2 * ROWS)
     pairs = (
         (amp_hbm.at[:, pl.ds(start, 2 * ROWS)], amp),
         (table_hbm, table),
-        (patch_hbm, patch),
+        (own_hbm, ext.at[:, pl.ds(0, SIDE)]),
+        (halo_hbm, ext.at[:, pl.ds(SIDE, SIDE)]),
     )
     copies = started(pairs, sems)
     copies[0].wait()
@@ -267,7 +275,7 @@
         return pltpu.make_async_copy(far.at[q], far_hbm.at[q], out_sems.at[q])
 
     def pair(q, carry):
-        waves = [lit(probe[0], probe[1], patch[q, w, 0], patch[q, w, 1]) for w in range(2)]
+        waves = [lit(probe[0], probe[1], *windows(pos, ext, 2 * q + w)) for w in range(2)]
         for parity, out in enumerate(to_frequencies(waves, table)):
             far[q, parity] = out
         far_copy(q).start()
@@ -296,7 +304,7 @@
 
 def inverse_kernel(
     pos, flags, change, far_own_hbm, far_other_hbm, probe_own_hbm, probe_other_hbm, table_hbm,
-    out, grad, far, probe, table, sems, far_sems,
+    upper, lower, grad, far, probe, table, sems, far_sems,
 ):
     pairs = ((probe_own_hbm, probe.at[0]), (probe_other_hbm, probe.at[1]), (table_hbm, table))
     copies = started(pairs, sems)
@@ -341,18 +349,19 @@
 
     lax.fori_loop(0, COUNT // 2, pair, 0)
     for d in range(PLANE_SIZE):
-        for lower in range(2):
-            start = lower * SIDE + (d // 4) * 64 + flags[1 + 2 * lower] * 32 + (d % 4) * 8
-            out[d, lower] = grad[:, pl.ds(pl.multiple_of(start, 8), 8), :]
+        start = (d // 4) * 64 + (d % 4) * 8
+        for out, half, first in ((upper, flags[1], 0), (lower, flags[3], SIDE)):
+            rows = pl.ds(pl.multiple_of(start + half * 32 + first, 8), 8)
+            out[d] = grad[:, rows, :]
 
 
 VMEM = pl.BlockSpec(memory_space=pltpu.VMEM)
 SMEM = pl.BlockSpec(memory_space=pltpu.SMEM)
 HBM = pl.BlockSpec(memory_space=pltpu.HBM)
 PAIRS = COUNT // 2
-LIMIT = 60
+ALL_VMEM, MOST_VMEM, SOME_VMEM = 60, 54, 32
 FAR = (PAIRS, 2, 2 * SIDE, SIDE)
-PATCH = (PAIRS, 2, 2, SIDE, SIDE)
+SHARES = (PLANE_SIZE, COUNT, ROWS, SIDE)
 DMA = pltpu.SemaphoreType.DMA
 
 
@@ -367,8 +376,7 @@
 TABLE = pltpu.VMEM((2, 2, 2, SIDE, SIDE), jnp.bfloat16)
 
 
-def call(kernel, name, in_specs, outs, scratches, operands, work=0, limit=LIMIT):
-    moves = sum(math.prod(v.shape) * v.dtype.itemsize for v in operands)
+def call(kernel, name, in_specs, outs, scratches, operands, limit, aliases=None):
     return pl.pallas_call(
         kernel,
         out_shape=[shape for shape, _ in outs],
@@ -376,14 +384,14 @@
         out_specs=[spec for _, spec in outs],
         scratch_shapes=scratches,
         compiler_params=pltpu.CompilerParams(vmem_limit_bytes=limit * 1024 * 1024),
-        cost_estimate=pl.CostEstimate(flops=work, bytes_accessed=moves, transcendentals=0),
+        cost_estimate=pl.CostEstimate(flops=0, bytes_accessed=0, transcendentals=0),
+        input_output_aliases=aliases or {},
         name=name,
     )(*operands)
 
 
 def body(object_field, probe_modes, amplitude, positions):
     table = jnp.asarray(tables())
-    work = COUNT * 12 * 2 * SIDE**3
     zlo, core = lax.axis_index("zlo"), lax.axis_index("core")
     y, zhi, x = (lax.axis_index(name) for name in ("y", "zhi", "x"))
     quarter = lax.rem(zlo, 4)
@@ -394,22 +402,32 @@
     halo = moved(object_field, along_ring(-1))
     piece = lax.dynamic_slice(probe, (core, quarter * QUARTER, 0), (1, QUARTER, SIDE))[0]
     first = moved(piece, across)
-    far_own, patches, intensity = call(
+    far_own, intensity = call(
         own_kernel,
         "own",
-        [SMEM, VMEM] + [HBM] * 4,
-        [(floats(*FAR), HBM), (floats(*PATCH), HBM), (floats(PLANE_SIZE, COUNT, ROWS, SIDE), VMEM)],
+        [SMEM] + [HBM] * 4,
+        [(floats(*FAR), HBM), (floats(*SHARES), HBM)],
         [
             scratch(2, WIDTH, WIDTH),
             scratch(2, SIDE, SIDE),
             TABLE,
             scratch(*FAR),
-            scratch(*PATCH),
-            DMA((3,)),
+            scratch(*SHARES),
+            DMA((4,)),
             DMA((2, PAIRS)),
         ],
-        (positions, halo, object_field, probe, table, first),
-        work,
+        (positions, object_field, halo, probe, table),
+        ALL_VMEM,
+    )
+    (intensity,) = call(
+        gate_kernel,
+        "gate",
+        [HBM] * 2,
+        [(floats(*SHARES), HBM)],
+        [],
+        (intensity, first),
+        MOST_VMEM,
+        {0: 0},
     )
     shares = lax.all_to_all(intensity, PLANE, 0, 0)
     spread = [moved(first, move) for move in (two_on, other_core, two_on_other)]
@@ -420,42 +438,42 @@
         [(floats(COUNT, ROWS, SIDE), VMEM), (floats(2, 2, QUARTER, SIDE), VMEM)],
         [],
         (shares, first, *spread),
-        limit=32,
+        SOME_VMEM,
     )
     arrived = moved(summed, other_half)
     next_block = moved(block, next_chip)
     far_other, probe_other, measured = call(
         other_kernel,
         "other",
-        [SMEM] + [HBM] * 3 + [VMEM] * 2,
+        [SMEM] * 2 + [HBM] * 4 + [VMEM] * 2,
         [(floats(*FAR), HBM), (floats(2, SIDE, SIDE), HBM), (floats(COUNT, ROWS, SIDE), VMEM)],
         [
-            scratch(*PATCH),
+            scratch(2, WIDTH, WIDTH),
             scratch(COUNT, 2 * ROWS, SIDE),
             TABLE,
             scratch(2, SIDE, SIDE),
             scratch(*FAR),
-            DMA((3,)),
+            DMA((4,)),
             DMA((PAIRS + 1,)),
         ],
-        (flags, patches, amplitude, table, block, next_block),
-        work,
+        (positions, flags, object_field, halo, amplitude, table, block, next_block),
+        SOME_VMEM,
     )
     (change,) = call(
         change_kernel,
         "change",
         [VMEM] * 3,
-        [(floats(PLANE_SIZE, COUNT, ROWS, SIDE), VMEM)],
+        [(floats(*SHARES), VMEM)],
         [],
         (summed, arrived, measured),
-        limit=32,
+        SOME_VMEM,
     )
     change = lax.all_to_all(change, PLANE, 0, 0)
-    (gradient,) = call(
+    upper, lower = call(
         inverse_kernel,
         "inverse",
         [SMEM] * 2 + [VMEM] + [HBM] * 5,
-        [(floats(PLANE_SIZE, 2, 2, 8, WIDTH), VMEM)],
+        [(floats(PLANE_SIZE, 2, 8, WIDTH), VMEM)] * 2,
         [
             scratch(2, WIDTH, WIDTH),
             scratch(2, *FAR),
@@ -465,10 +483,10 @@
             DMA((2, PAIRS)),
         ],
         (positions, flags, change, far_own, far_other, probe, probe_other, table),
-        2 * work,
-    )
-    gradient = jnp.sum(lax.all_to_all(gradient, PLANE, 0, 0), 0)
-    total = gradient[0] + moved(gradient[1], along_ring(1))
+        SOME_VMEM,
+    )
+    gradient = upper + moved(lower, along_ring(1))
+    total = jnp.sum(lax.all_to_all(gradient, PLANE, 0, 0), 0)
     own = lax.dynamic_slice_in_dim(object_field, ((y * 2 + zhi) * 4 + x) * 8, 8, 1)
     return own + 0.5 * total / MODES
 

time: 164 us -> 157 us (0.957)
  the two profiles are of different devices: /device:TPU:288 before, /device:TPU:64 now
where the time goes in v5:
time: 157 us; the launch traced here: 156 us
  starting transfers between devices  71.9 us (46%)
  blocking collectives  27.2 us (17%)
  waiting for transfers between devices  24.6 us (16%)
  Pallas kernels  20.6 us (13%)
  local copies, waits for them, and re-layouts  10.1 us (6%)
    ppermute x8, starting transfers between devices, moved(): return lax.ppermute(value, AXES, pairs_of(move))  61.2 us
    all_to_all x1, blocking collectives, body(): change = lax.all_to_all(change, PLANE, 0, 0)  27.2 us
    pallas_call x6, Pallas kernels, call(): pl.pallas_call(kernel, out_shape=[shape for shape, _ in outs], in_specs=i...  20.6 us
    ppermute x8, waiting for transfers between devices, moved(): return lax.ppermute(value, AXES, pairs_of(move))  14.6 us
    all_to_all x1, waiting for transfers between devices, body(): total = jnp.sum(lax.all_to_all(gradient, PLANE, 0, 0), 0)  10.1 us
    unnamed x29, local copies, waits for them, and re-layouts  9.15 us
    all_to_all x1, starting transfers between devices, body(): shares = lax.all_to_all(intensity, PLANE, 0, 0)  7.17 us
    all_to_all x1, starting transfers between devices, body(): total = jnp.sum(lax.all_to_all(gradient, PLANE, 0, 0), 0)  3.57 us
  transfers between devices with their start and end apart: 10, of which 4 were waited for; matrix products, arithmetic and copies ran while one was open for 1% of the time, Pallas kernels for 9%

profile of v5, /device:TPU:64, one launch (start us, length us, event | category | flops | bytes accessed | tf_op | source)
XLA Modules:
  0.0 156.2 jit_solution(12605719124481128558)
XLA Ops:
  0.0 0.8 dynamic-slice_bitcast_fusion
  0.8 21.6 %collective-permute-start.1 = (f32[64,256]{1,0:T(8,128)S(1)}, f32[64,256]{1,0:T(8,128)S(1)}, u32[]{:S(2)}, u32[]{:S(2)}) collective-permute-start(f32[64,256]{1,0:T(8,128)S(1)} %dynamic-slice_bitcast_fusion), channel_id=1, source_target_pairs={{0,516},{1,517},{2,518},{3,519},{4,512},{5,513},{6,514},{7,515},{8... | collective-permute-start | bytes 196616 | tf_op jit(solution)/shard_map/ppermute | solution.py:71
  22.5 1.3 copy.9.pos
  23.8 1.0 copy-done.2
  24.8 7.9 %own.1 = (f32[2,2,512,256]{3,2,1,0:T(8,128)}, f32[16,4,16,256]{3,2,1,0:T(8,128)}) custom-call(s32[4,2]{1,0:T(4,128)} %copy.9.pos, f32[2,256,512]{2,1,0:T(8,128)} %own_hbm.3, f32[2,256,512]{2,1,0:T(8,128)} %copy-done.2, f32[2,256,256]{2,1,0:T(8,128)} %bitcast.8, bf16[2,2,2,256,256]{4,3,2,1,0:T(8,128)(2,1)} %constant.51.clone.table_hbm), custom_call_target="tpu_custom_call" | custom-call | tf_op jit(solution)/shard_map/own/pallas_call | solution.py:380
  32.7 0.6 copy-done.7
  33.3 7.2 %all-to-all-start = ((f32[16,4,16,256]{3,2,1,0:T(8,128)}), f32[16,4,16,256]{3,2,1,0:T(8,128)S(1)}, u32[]{:S(2)}, u32[]{:S(2)}) async-start(f32[16,4,16,256]{3,2,1,0:T(8,128)} %gate.1), calls=%async_computation | async-start | bytes 2097152 | tf_op jit(solution)/shard_map/all_to_all | solution.py:432
  40.5 3.9 %collective-permute-start.4 = (f32[64,256]{1,0:T(8,128)}, f32[64,256]{1,0:T(8,128)S(1)}, u32[]{:S(2)}, u32[]{:S(2)}) collective-permute-start(f32[64,256]{1,0:T(8,128)} %copy-done.7), channel_id=1, source_target_pairs={{0,160},{1,161},{2,162},{3,163},{4,164},{5,165},{6,166},{7,167},{8... | collective-permute-start | bytes 196616 | tf_op jit(solution)/shard_map/ppermute | solution.py:71
  44.4 15.2 %collective-permute-start.3 = (f32[64,256]{1,0:T(8,128)}, f32[64,256]{1,0:T(8,128)S(1)}, u32[]{:S(2)}, u32[]{:S(2)}) collective-permute-start(f32[64,256]{1,0:T(8,128)} %copy-done.7), channel_id=1, source_target_pairs={{0,32},{1,33},{2,34},{3,35},{4,36},{5,37},{6,38},{7,39},{8,40},{9,... | collective-permute-start | bytes 196616 | tf_op jit(solution)/shard_map/ppermute | solution.py:71
  59.7 1.9 %collective-permute-start.2 = (f32[64,256]{1,0:T(8,128)}, f32[64,256]{1,0:T(8,128)S(1)}, u32[]{:S(2)}, u32[]{:S(2)}) collective-permute-start(f32[64,256]{1,0:T(8,128)} %copy-done.7), channel_id=1, source_target_pairs={{0,128},{1,129},{2,130},{3,131},{4,132},{5,133},{6,134},{7,135},{8... | collective-permute-start | bytes 196616 | tf_op jit(solution)/shard_map/ppermute | solution.py:71
  61.6 0.6 copy-done.9
  62.3 4.7 %collective-permute-done.2.second = f32[64,256]{1,0:T(8,128)S(1)} collective-permute-done((f32[64,256]{1,0:T(8,128)}, f32[64,256]{1,0:T(8,128)S(1)}, u32[]{:S(2)}, u32[]{:S(2)}) %collective-permute-start.2) | collective-permute-done | bytes 65568 | tf_op jit(solution)/shard_map/ppermute | solution.py:71
  67.0 0.6 copy-done.11
  67.6 0.8 copy-done.8
  68.4 0.8 copy-done.10
  69.3 0.8 copy-done.12
  70.1 0.1 collect.1
  70.2 1.9 %collective-permute-start.6 = (f32[2,2,64,256]{3,2,1,0:T(8,128)S(1)}, f32[2,2,64,256]{3,2,1,0:T(8,128)S(1)}, u32[]{:S(2)}, u32[]{:S(2)}) collective-permute-start(f32[2,2,64,256]{3,2,1,0:T(8,128)S(1)} %get-tuple-element.16.block), channel_id=1, source_target_pairs={{0,64},{1,65},{2,66},{3,67},{4,68},{5,69},{6,70},{7,71},{8,72},{9,... | collective-permute-start | bytes 786440 | tf_op jit(solution)/shard_map/ppermute | solution.py:71
  72.1 16.5 %collective-permute-start.5 = (f32[4,16,256]{2,1,0:T(8,128)S(1)}, f32[4,16,256]{2,1,0:T(8,128)S(1)}, u32[]{:S(2)}, u32[]{:S(2)}) collective-permute-start(f32[4,16,256]{2,1,0:T(8,128)S(1)} %get-tuple-element.15.summed), channel_id=1, source_target_pairs={{0,4},{1,5},{2,6},{3,7},{4,0},{5,1},{6,2},{7,3},{8,12},{9,13},{10,... | collective-permute-start | bytes 196616 | tf_op jit(solution)/shard_map/ppermute | solution.py:71
  88.6 0.1 stack.23.flags
  88.7 1.2 copy-done.3
  90.0 1.2 copy-done.6
  91.2 5.5 %other.1 = (f32[2,2,512,256]{3,2,1,0:T(8,128)S(1)}, f32[2,256,256]{2,1,0:T(8,128)S(1)}, f32[4,16,256]{2,1,0:T(8,128)S(1)}) custom-call(s32[4,2]{1,0:T(4,128)S(1)} %copy-done.13, s32[5]{0:T(128)S(1)} %stack.23.flags, f32[2,256,512]{2,1,0:T(8,128)S(1)} %copy-done.1, f32[2,256,512]{2,1,0:T(8,128)S(1)} %copy-done.3, f32[4,256,256]{2,1,0:T(8,128)S(1)} %copy-done.6, ...), custom_call_target="tpu_custom_call" | custom-call | tf_op jit(solution)/shard_map/other/pallas_call | solution.py:380
  96.7 1.2 collective-permute-done.5.arrived
  98.0 0.1 change.1
  98.1 27.2 %all_to_all.15.change = f32[16,4,16,256]{3,2,1,0:T(8,128)S(1)} all-to-all(f32[16,4,16,256]{3,2,1,0:T(8,128)S(1)} %change.1), channel_id=1, replica_groups=mesh['zlo'=16,'core'=2,'y'=4,'zhi'=2,'x'=4] {'y','x'}, dimensions={0} | all-to-all | bytes 2097152 | tf_op jit(solution)/shard_map/all_to_all | solution.py:471
  125.3 7.0 %inverse.1 = (f32[16,2,8,512]{3,2,1,0:T(8,128)S(1)}, f32[16,2,8,512]{3,2,1,0:T(8,128)S(1)}) custom-call(s32[4,2]{1,0:T(4,128)S(1)} %copy-done.13, s32[5]{0:T(128)S(1)} %stack.23.flags, f32[16,4,16,256]{3,2,1,0:T(8,128)S(1)} %all_to_all.15.change, f32[2,2,512,256]{3,2,1,0:T(8,128)S(1)} %copy-done.5, f32[2,2,512,256]{3,2,1,0:T(8,128)S(1)} %get-tuple-element.19.far_other_hbm, ...), custom_call_target="tpu_custom_call" | custom-call | tf_op jit(solution)/shard_map/inverse/pallas_call | solution.py:380
  132.4 8.6 %collective-permute-done.7 = f32[16,2,8,512]{3,2,1,0:T(8,128)S(1)} collective-permute-done((f32[16,2,8,512]{3,2,1,0:T(8,128)S(1)}, f32[16,2,8,512]{3,2,1,0:T(8,128)S(1)}, u32[]{:S(2)}, u32[]{:S(2)}) %collective-permute-start.7) | collective-permute-done | bytes 524320 | tf_op jit(solution)/shard_map/ppermute | solution.py:71
  141.0 0.9 add.30
  141.9 3.6 %all-to-all-start.2 = ((f32[16,2,8,512]{3,2,1,0:T(8,128)}), f32[16,2,8,512]{3,2,1,0:T(8,128)S(1)}, u32[]{:S(2)}, u32[]{:S(2)}) async-start(f32[16,2,8,512]{3,2,1,0:T(8,128)} %add.30), calls=%async_computation.2 | async-start | bytes 1048576 | tf_op jit(solution)/shard_map/all_to_all | solution.py:489
  145.5 10.1 %all-to-all-done.2 = f32[16,2,8,512]{3,2,1,0:T(8,128)S(1)} async-done(((f32[16,2,8,512]{3,2,1,0:T(8,128)}), f32[16,2,8,512]{3,2,1,0:T(8,128)S(1)}, u32[]{:S(2)}, u32[]{:S(2)}) %all-to-all-start.2) | async-done | bytes 524320 | tf_op jit(solution)/shard_map/all_to_all | solution.py:489
  155.6 0.6 multiply_add_fusion
  (29 shorter events, 0.1 us)
Async XLA Ops:
  0.0 23.8 %collective-permute-start = (f32[2,256,512]{2,1,0:T(8,128)}, f32[2,256,512]{2,1,0:T(8,128)S(1)}, u32[]{:S(2)}, u32[]{:S(2)}) collective-permute-start(f32[2,256,512]{2,1,0:T(8,128)} %own_hbm.3), channel_id=1, source_target_pairs={{0,996},{1,997},{2,998},{3,999},{4,992},{5,993},{6,994},{7,995},{8... | collective-permute-start | bytes 3145736 | tf_op jit(solution)/shard_map/ppermute | solution.py:71
  0.8 31.8 %collective-permute-start.1 = (f32[64,256]{1,0:T(8,128)S(1)}, f32[64,256]{1,0:T(8,128)S(1)}, u32[]{:S(2)}, u32[]{:S(2)}) collective-permute-start(f32[64,256]{1,0:T(8,128)S(1)} %dynamic-slice_bitcast_fusion), channel_id=1, source_target_pairs={{0,516},{1,517},{2,518},{3,519},{4,512},{5,513},{6,514},{7,515},{8... | collective-permute-start | bytes 196616 | tf_op jit(solution)/shard_map/ppermute | solution.py:71
  23.8 1.0 copy-start.2
  32.7 0.6 copy-start.7
  33.3 55.4 %copy-start.13 = (s32[4,2]{1,0:T(4,128)S(1)}, s32[4,2]{1,0:T(4,128)}, u32[]{:S(2)}) copy-start(s32[4,2]{1,0:T(4,128)} %copy.9.pos) | copy-start | bytes 100
  33.3 55.4 %copy-start = (bf16[2,2,2,256,256]{4,3,2,1,0:T(8,128)(2,1)S(1)}, bf16[2,2,2,256,256]{4,3,2,1,0:T(8,128)(2,1)}, u32[]{:S(2)}) copy-start(bf16[2,2,2,256,256]{4,3,2,1,0:T(8,128)(2,1)} %constant.51.clone.table_hbm) | copy-start | bytes 3145732
  33.3 55.4 %copy-start.1 = (f32[2,256,512]{2,1,0:T(8,128)S(1)}, f32[2,256,512]{2,1,0:T(8,128)}, u32[]{:S(2)}) copy-start(f32[2,256,512]{2,1,0:T(8,128)} %own_hbm.3) | copy-start | bytes 3145732
  33.3 34.2 %all-to-all-start = ((f32[16,4,16,256]{3,2,1,0:T(8,128)}), f32[16,4,16,256]{3,2,1,0:T(8,128)S(1)}, u32[]{:S(2)}, u32[]{:S(2)}) async-start(f32[16,4,16,256]{3,2,1,0:T(8,128)} %gate.1), calls=%async_computation | async-start | bytes 2097152 | tf_op jit(solution)/shard_map/all_to_all | solution.py:432
  40.5 21.1 %collective-permute-start.4 = (f32[64,256]{1,0:T(8,128)}, f32[64,256]{1,0:T(8,128)S(1)}, u32[]{:S(2)}, u32[]{:S(2)}) collective-permute-start(f32[64,256]{1,0:T(8,128)} %copy-done.7), channel_id=1, source_target_pairs={{0,160},{1,161},{2,162},{3,163},{4,164},{5,165},{6,166},{7,167},{8... | collective-permute-start | bytes 196616 | tf_op jit(solution)/shard_map/ppermute | solution.py:71
  44.4 17.2 %collective-permute-start.3 = (f32[64,256]{1,0:T(8,128)}, f32[64,256]{1,0:T(8,128)S(1)}, u32[]{:S(2)}, u32[]{:S(2)}) collective-permute-start(f32[64,256]{1,0:T(8,128)} %copy-done.7), channel_id=1, source_target_pairs={{0,32},{1,33},{2,34},{3,35},{4,36},{5,37},{6,38},{7,39},{8,40},{9,... | collective-permute-start | bytes 196616 | tf_op jit(solution)/shard_map/ppermute | solution.py:71
  59.7 7.3 %collective-permute-start.2 = (f32[64,256]{1,0:T(8,128)}, f32[64,256]{1,0:T(8,128)S(1)}, u32[]{:S(2)}, u32[]{:S(2)}) collective-permute-start(f32[64,256]{1,0:T(8,128)} %copy-done.7), channel_id=1, source_target_pairs={{0,128},{1,129},{2,130},{3,131},{4,132},{5,133},{6,134},{7,135},{8... | collective-permute-start | bytes 196616 | tf_op jit(solution)/shard_map/ppermute | solution.py:71
  61.6 0.6 copy-start.9
  67.0 0.6 copy-start.11
  67.6 0.8 copy-start.8
  68.4 0.8 copy-start.10
  69.3 0.8 copy-start.12
  70.2 18.5 %collective-permute-start.6 = (f32[2,2,64,256]{3,2,1,0:T(8,128)S(1)}, f32[2,2,64,256]{3,2,1,0:T(8,128)S(1)}, u32[]{:S(2)}, u32[]{:S(2)}) collective-permute-start(f32[2,2,64,256]{3,2,1,0:T(8,128)S(1)} %get-tuple-element.16.block), channel_id=1, source_target_pairs={{0,64},{1,65},{2,66},{3,67},{4,68},{5,69},{6,70},{7,71},{8,72},{9,... | collective-permute-start | bytes 786440 | tf_op jit(solution)/shard_map/ppermute | solution.py:71
  72.1 25.9 %collective-permute-start.5 = (f32[4,16,256]{2,1,0:T(8,128)S(1)}, f32[4,16,256]{2,1,0:T(8,128)S(1)}, u32[]{:S(2)}, u32[]{:S(2)}) collective-permute-start(f32[4,16,256]{2,1,0:T(8,128)S(1)} %get-tuple-element.15.summed), channel_id=1, source_target_pairs={{0,4},{1,5},{2,6},{3,7},{4,0},{5,1},{6,2},{7,3},{8,12},{9,13},{10,... | collective-permute-start | bytes 196616 | tf_op jit(solution)/shard_map/ppermute | solution.py:71
  88.7 1.2 copy-start.3
  90.0 1.2 copy-start.6
  96.7 28.6 %copy-start.4 = (f32[1,2,256,256]{3,2,1,0:T(8,128)S(1)}, f32[1,2,256,256]{3,2,1,0:T(8,128)}, u32[]{:S(2)}) copy-start(f32[1,2,256,256]{3,2,1,0:T(8,128)} %param.6) | copy-start | bytes 1572868
  96.7 28.6 %copy-start.5 = (f32[2,2,512,256]{3,2,1,0:T(8,128)S(1)}, f32[2,2,512,256]{3,2,1,0:T(8,128)}, u32[]{:S(2)}) copy-start(f32[2,2,512,256]{3,2,1,0:T(8,128)} %get-tuple-element.18.far_own_hbm) | copy-start | bytes 6291460
  132.3 8.6 %collective-permute-start.7 = (f32[16,2,8,512]{3,2,1,0:T(8,128)S(1)}, f32[16,2,8,512]{3,2,1,0:T(8,128)S(1)}, u32[]{:S(2)}, u32[]{:S(2)}) collective-permute-start(f32[16,2,8,512]{3,2,1,0:T(8,128)S(1)} %get-tuple-element.22), channel_id=1, source_target_pairs={{0,32},{1,33},{2,34},{3,35},{4,36},{5,37},{6,38},{7,39},{8,40},{9,... | collective-permute-start | bytes 1572872 | tf_op jit(solution)/shard_map/ppermute | solution.py:71
  141.9 13.7 %all-to-all-start.2 = ((f32[16,2,8,512]{3,2,1,0:T(8,128)}), f32[16,2,8,512]{3,2,1,0:T(8,128)S(1)}, u32[]{:S(2)}, u32[]{:S(2)}) async-start(f32[16,2,8,512]{3,2,1,0:T(8,128)} %add.30), calls=%async_computation.2 | async-start | bytes 1048576 | tf_op jit(solution)/shard_map/all_to_all | solution.py:489

commit v6 on v5

--- a/solution.py
+++ b/solution.py
@@ -235,14 +235,10 @@
             copy.start()
         return carry
 
-    lax.fori_loop(0, PAIRS, pair, 0)
+    lax.fori_loop(0, PAIRS, pair, 0, unroll=True)
     for q in range(PAIRS):
         for copy in out_copies(q):
             copy.wait()
-
-
-def gate_kernel(array, _, out):
-    pass
 
 
 def other_kernel(
@@ -359,7 +355,7 @@
 SMEM = pl.BlockSpec(memory_space=pltpu.SMEM)
 HBM = pl.BlockSpec(memory_space=pltpu.HBM)
 PAIRS = COUNT // 2
-ALL_VMEM, MOST_VMEM, SOME_VMEM = 60, 54, 32
+ALL_VMEM, SOME_VMEM = 60, 32
 FAR = (PAIRS, 2, 2 * SIDE, SIDE)
 SHARES = (PLANE_SIZE, COUNT, ROWS, SIDE)
 DMA = pltpu.SemaphoreType.DMA
@@ -376,7 +372,7 @@
 TABLE = pltpu.VMEM((2, 2, 2, SIDE, SIDE), jnp.bfloat16)
 
 
-def call(kernel, name, in_specs, outs, scratches, operands, limit, aliases=None):
+def call(kernel, name, in_specs, outs, scratches, operands, limit):
     return pl.pallas_call(
         kernel,
         out_shape=[shape for shape, _ in outs],
@@ -385,7 +381,6 @@
         scratch_shapes=scratches,
         compiler_params=pltpu.CompilerParams(vmem_limit_bytes=limit * 1024 * 1024),
         cost_estimate=pl.CostEstimate(flops=0, bytes_accessed=0, transcendentals=0),
-        input_output_aliases=aliases or {},
         name=name,
     )(*operands)
 
@@ -419,16 +414,7 @@
         (positions, object_field, halo, probe, table),
         ALL_VMEM,
     )
-    (intensity,) = call(
-        gate_kernel,
-        "gate",
-        [HBM] * 2,
-        [(floats(*SHARES), HBM)],
-        [],
-        (intensity, first),
-        MOST_VMEM,
-        {0: 0},
-    )
+    intensity, first = lax.optimization_barrier((intensity, first))
     shares = lax.all_to_all(intensity, PLANE, 0, 0)
     spread = [moved(first, move) for move in (two_on, other_core, two_on_other)]
     summed, block = call(
@@ -457,7 +443,7 @@
             DMA((PAIRS + 1,)),
         ],
         (positions, flags, object_field, halo, amplitude, table, block, next_block),
-        SOME_VMEM,
+        ALL_VMEM,
     )
     (change,) = call(
         change_kernel,

time: 157 us -> 153 us (0.975)
  the two profiles are of different devices: /device:TPU:64 before, /device:TPU:32 now
where the time goes in v6:
time: 153 us
  starting transfers between devices  69.4 us (45%)
  waiting for transfers between devices  30.7 us (20%)
  Pallas kernels  23.1 us (15%)
  blocking collectives  19.9 us (13%)
  local copies, waits for them, and re-layouts  6.98 us (5%)
  other arithmetic  2.32 us (2%)
    ppermute x8, starting transfers between devices, moved(): return lax.ppermute(value, AXES, pairs_of(move))  58.8 us
    pallas_call x5, Pallas kernels, call(): pl.pallas_call(kernel, out_shape=[shape for shape, _ in outs], in_specs=i...  23.1 us
    all_to_all x1, blocking collectives, body(): change = lax.all_to_all(change, PLANE, 0, 0)  19.9 us
    ppermute x8, waiting for transfers between devices, moved(): return lax.ppermute(value, AXES, pairs_of(move))  13.8 us
    all_to_all x1, waiting for transfers between devices, body(): total = jnp.sum(lax.all_to_all(gradient, PLANE, 0, 0), 0)  12 us
    all_to_all x1, starting transfers between devices, body(): shares = lax.all_to_all(intensity, PLANE, 0, 0)  7.03 us
    unnamed x23, local copies, waits for them, and re-layouts  5.5 us
    all_to_all x1, waiting for transfers between devices, body(): shares = lax.all_to_all(intensity, PLANE, 0, 0)  4.9 us
  transfers between devices with their start and end apart: 10, of which 6 were waited for; matrix products, arithmetic and copies ran while one was open for 2% of the time, Pallas kernels for 10%

profile of v6, /device:TPU:32, one launch (start us, length us, event | category | flops | bytes accessed | tf_op | source)
XLA Modules:
  0.0 152.6 jit_solution(4012808851449136191)
XLA Ops:
  0.0 0.8 dynamic-slice_bitcast_fusion
  0.8 22.5 %collective-permute-start.1 = (f32[64,256]{1,0:T(8,128)S(1)}, f32[64,256]{1,0:T(8,128)S(1)}, u32[]{:S(2)}, u32[]{:S(2)}) collective-permute-start(f32[64,256]{1,0:T(8,128)S(1)} %dynamic-slice_bitcast_fusion), channel_id=1, source_target_pairs={{0,516},{1,517},{2,518},{3,519},{4,512},{5,513},{6,514},{7,515},{8... | collective-permute-start | bytes 196616 | tf_op jit(solution)/shard_map/ppermute | solution.py:71
  23.4 1.3 copy.8.pos
  24.7 1.0 copy-done.9
  25.7 7.1 %own.1 = (f32[2,2,512,256]{3,2,1,0:T(8,128)}, f32[16,4,16,256]{3,2,1,0:T(8,128)}) custom-call(s32[4,2]{1,0:T(4,128)} %copy.8.pos, f32[2,256,512]{2,1,0:T(8,128)} %own_hbm.3, f32[2,256,512]{2,1,0:T(8,128)} %copy-done.9, f32[2,256,256]{2,1,0:T(8,128)} %bitcast.8, bf16[2,2,2,256,256]{4,3,2,1,0:T(8,128)(2,1)} %constant.51.clone.table_hbm), custom_call_target="tpu_custom_call" | custom-call | tf_op jit(solution)/shard_map/own/pallas_call | solution.py:376
  32.9 0.6 collective-permute-done.1.first
  33.5 7.0 %all-to-all-start = ((f32[16,4,16,256]{3,2,1,0:T(8,128)}), f32[16,4,16,256]{3,2,1,0:T(8,128)S(1)}, u32[]{:S(2)}, u32[]{:S(2)}) async-start(f32[16,4,16,256]{3,2,1,0:T(8,128)} %get-tuple-element.17), calls=%async_computation | async-start | bytes 2097152 | tf_op jit(solution)/shard_map/all_to_all | solution.py:418
  40.5 1.9 %collective-permute-start.4 = (f32[64,256]{1,0:T(8,128)S(1)}, f32[64,256]{1,0:T(8,128)S(1)}, u32[]{:S(2)}, u32[]{:S(2)}) collective-permute-start(f32[64,256]{1,0:T(8,128)S(1)} %collective-permute-done.1.first), channel_id=1, source_target_pairs={{0,160},{1,161},{2,162},{3,163},{4,164},{5,165},{6,166},{7,167},{8... | collective-permute-start | bytes 196616 | tf_op jit(solution)/shard_map/ppermute | solution.py:71
  42.4 2.9 %collective-permute-start.3 = (f32[64,256]{1,0:T(8,128)S(1)}, f32[64,256]{1,0:T(8,128)S(1)}, u32[]{:S(2)}, u32[]{:S(2)}) collective-permute-start(f32[64,256]{1,0:T(8,128)S(1)} %collective-permute-done.1.first), channel_id=1, source_target_pairs={{0,32},{1,33},{2,34},{3,35},{4,36},{5,37},{6,38},{7,39},{8,40},{9,... | collective-permute-start | bytes 196616 | tf_op jit(solution)/shard_map/ppermute | solution.py:71
  45.4 3.9 %collective-permute-start.2 = (f32[64,256]{1,0:T(8,128)S(1)}, f32[64,256]{1,0:T(8,128)S(1)}, u32[]{:S(2)}, u32[]{:S(2)}) collective-permute-start(f32[64,256]{1,0:T(8,128)S(1)} %collective-permute-done.1.first), channel_id=1, source_target_pairs={{0,128},{1,129},{2,130},{3,131},{4,132},{5,133},{6,134},{7,135},{8... | collective-permute-start | bytes 196616 | tf_op jit(solution)/shard_map/ppermute | solution.py:71
  49.3 3.1 %collective-permute-done.2.second = f32[64,256]{1,0:T(8,128)S(1)} collective-permute-done((f32[64,256]{1,0:T(8,128)S(1)}, f32[64,256]{1,0:T(8,128)S(1)}, u32[]{:S(2)}, u32[]{:S(2)}) %collective-permute-start.2) | collective-permute-done | bytes 65568 | tf_op jit(solution)/shard_map/ppermute | solution.py:71
  52.4 4.9 %all-to-all-done.shares = f32[16,4,16,256]{3,2,1,0:T(8,128)S(1)} async-done(((f32[16,4,16,256]{3,2,1,0:T(8,128)}), f32[16,4,16,256]{3,2,1,0:T(8,128)S(1)}, u32[]{:S(2)}, u32[]{:S(2)}) %all-to-all-start) | async-done | bytes 1048608 | tf_op jit(solution)/shard_map/all_to_all | solution.py:418
  57.3 0.1 collect.1
  57.4 12.7 %collective-permute-start.6 = (f32[2,2,64,256]{3,2,1,0:T(8,128)S(1)}, f32[2,2,64,256]{3,2,1,0:T(8,128)S(1)}, u32[]{:S(2)}, u32[]{:S(2)}) collective-permute-start(f32[2,2,64,256]{3,2,1,0:T(8,128)S(1)} %get-tuple-element.20.block), channel_id=1, source_target_pairs={{0,64},{1,65},{2,66},{3,67},{4,68},{5,69},{6,70},{7,71},{8,72},{9,... | collective-permute-start | bytes 786440 | tf_op jit(solution)/shard_map/ppermute | solution.py:71
  70.1 14.9 %collective-permute-start.5 = (f32[4,16,256]{2,1,0:T(8,128)S(1)}, f32[4,16,256]{2,1,0:T(8,128)S(1)}, u32[]{:S(2)}, u32[]{:S(2)}) collective-permute-start(f32[4,16,256]{2,1,0:T(8,128)S(1)} %get-tuple-element.19.summed), channel_id=1, source_target_pairs={{0,4},{1,5},{2,6},{3,7},{4,0},{5,1},{6,2},{7,3},{8,12},{9,13},{10,... | collective-permute-start | bytes 196616 | tf_op jit(solution)/shard_map/ppermute | solution.py:71
  85.0 0.6 stack.23.flags
  85.6 0.7 copy-done.10
  86.3 8.8 %other.1 = (f32[2,2,512,256]{3,2,1,0:T(8,128)}, f32[2,256,256]{2,1,0:T(8,128)}, f32[4,16,256]{2,1,0:T(8,128)}) custom-call(s32[4,2]{1,0:T(4,128)} %copy.8.pos, s32[5]{0:T(128)} %stack.23.flags, f32[2,256,512]{2,1,0:T(8,128)} %own_hbm.3, f32[2,256,512]{2,1,0:T(8,128)} %copy-done.9, f32[4,256,256]{2,1,0:T(8,128)} %amp_hbm.1, ...), custom_call_target="tpu_custom_call" | custom-call | tf_op jit(solution)/shard_map/other/pallas_call | solution.py:376
  95.1 0.0 copy-start
  95.1 0.0 copy-start.1
  95.1 1.5 collective-permute-done.5.arrived
  96.7 0.8 copy-done.6
  97.5 0.1 change.1
  97.6 19.9 %all_to_all.15.change = f32[16,4,16,256]{3,2,1,0:T(8,128)S(1)} all-to-all(f32[16,4,16,256]{3,2,1,0:T(8,128)S(1)} %change.1), channel_id=1, replica_groups=mesh['zlo'=16,'core'=2,'y'=4,'zhi'=2,'x'=4] {'y','x'}, dimensions={0} | all-to-all | bytes 2097152 | tf_op jit(solution)/shard_map/all_to_all | solution.py:457
  117.5 1.6 %copy-done.3 = f32[2,2,512,256]{3,2,1,0:T(8,128)S(1)} copy-done((f32[2,2,512,256]{3,2,1,0:T(8,128)S(1)}, f32[2,2,512,256]{3,2,1,0:T(8,128)}, u32[]{:S(2)}) %copy-start.3) | copy-done | bytes 2097176
  119.1 7.0 %inverse.1 = (f32[16,2,8,512]{3,2,1,0:T(8,128)S(1)}, f32[16,2,8,512]{3,2,1,0:T(8,128)S(1)}) custom-call(s32[4,2]{1,0:T(4,128)S(1)} %copy-done.7, s32[5]{0:T(128)S(1)} %copy-done.8, f32[16,4,16,256]{3,2,1,0:T(8,128)S(1)} %all_to_all.15.change, f32[2,2,512,256]{3,2,1,0:T(8,128)S(1)} %copy-done.2, f32[2,2,512,256]{3,2,1,0:T(8,128)S(1)} %copy-done.3, ...), custom_call_target="tpu_custom_call" | custom-call | tf_op jit(solution)/shard_map/inverse/pallas_call | solution.py:376
  126.2 0.0 collective-permute-start.7
  126.2 8.6 %collective-permute-done.7 = f32[16,2,8,512]{3,2,1,0:T(8,128)S(1)} collective-permute-done((f32[16,2,8,512]{3,2,1,0:T(8,128)S(1)}, f32[16,2,8,512]{3,2,1,0:T(8,128)S(1)}, u32[]{:S(2)}, u32[]{:S(2)}) %collective-permute-start.7) | collective-permute-done | bytes 524320 | tf_op jit(solution)/shard_map/ppermute | solution.py:71
  134.8 0.9 add.30
  135.7 3.6 %all-to-all-start.2 = ((f32[16,2,8,512]{3,2,1,0:T(8,128)}), f32[16,2,8,512]{3,2,1,0:T(8,128)S(1)}, u32[]{:S(2)}, u32[]{:S(2)}) async-start(f32[16,2,8,512]{3,2,1,0:T(8,128)} %add.30), calls=%async_computation.2 | async-start | bytes 1048576 | tf_op jit(solution)/shard_map/all_to_all | solution.py:475
  139.3 12.0 %all-to-all-done.2 = f32[16,2,8,512]{3,2,1,0:T(8,128)S(1)} async-done(((f32[16,2,8,512]{3,2,1,0:T(8,128)}), f32[16,2,8,512]{3,2,1,0:T(8,128)S(1)}, u32[]{:S(2)}, u32[]{:S(2)}) %all-to-all-start.2) | async-done | bytes 524320 | tf_op jit(solution)/shard_map/all_to_all | solution.py:475
  151.3 1.4 multiply_add_fusion
  (22 shorter events, 0.1 us)
Async XLA Ops:
  0.0 24.7 %collective-permute-start = (f32[2,256,512]{2,1,0:T(8,128)}, f32[2,256,512]{2,1,0:T(8,128)S(1)}, u32[]{:S(2)}, u32[]{:S(2)}) collective-permute-start(f32[2,256,512]{2,1,0:T(8,128)} %own_hbm.3), channel_id=1, source_target_pairs={{0,996},{1,997},{2,998},{3,999},{4,992},{5,993},{6,994},{7,995},{8... | collective-permute-start | bytes 3145736 | tf_op jit(solution)/shard_map/ppermute | solution.py:71
  0.8 32.6 %collective-permute-start.1 = (f32[64,256]{1,0:T(8,128)S(1)}, f32[64,256]{1,0:T(8,128)S(1)}, u32[]{:S(2)}, u32[]{:S(2)}) collective-permute-start(f32[64,256]{1,0:T(8,128)S(1)} %dynamic-slice_bitcast_fusion), channel_id=1, source_target_pairs={{0,516},{1,517},{2,518},{3,519},{4,512},{5,513},{6,514},{7,515},{8... | collective-permute-start | bytes 196616 | tf_op jit(solution)/shard_map/ppermute | solution.py:71
  24.7 1.0 copy-start.9
  33.5 23.9 %all-to-all-start = ((f32[16,4,16,256]{3,2,1,0:T(8,128)}), f32[16,4,16,256]{3,2,1,0:T(8,128)S(1)}, u32[]{:S(2)}, u32[]{:S(2)}) async-start(f32[16,4,16,256]{3,2,1,0:T(8,128)} %get-tuple-element.17), calls=%async_computation | async-start | bytes 2097152 | tf_op jit(solution)/shard_map/all_to_all | solution.py:418
  40.5 8.8 %collective-permute-start.4 = (f32[64,256]{1,0:T(8,128)S(1)}, f32[64,256]{1,0:T(8,128)S(1)}, u32[]{:S(2)}, u32[]{:S(2)}) collective-permute-start(f32[64,256]{1,0:T(8,128)S(1)} %collective-permute-done.1.first), channel_id=1, source_target_pairs={{0,160},{1,161},{2,162},{3,163},{4,164},{5,165},{6,166},{7,167},{8... | collective-permute-start | bytes 196616 | tf_op jit(solution)/shard_map/ppermute | solution.py:71
  42.4 6.9 %collective-permute-start.3 = (f32[64,256]{1,0:T(8,128)S(1)}, f32[64,256]{1,0:T(8,128)S(1)}, u32[]{:S(2)}, u32[]{:S(2)}) collective-permute-start(f32[64,256]{1,0:T(8,128)S(1)} %collective-permute-done.1.first), channel_id=1, source_target_pairs={{0,32},{1,33},{2,34},{3,35},{4,36},{5,37},{6,38},{7,39},{8,40},{9,... | collective-permute-start | bytes 196616 | tf_op jit(solution)/shard_map/ppermute | solution.py:71
  45.4 7.1 %collective-permute-start.2 = (f32[64,256]{1,0:T(8,128)S(1)}, f32[64,256]{1,0:T(8,128)S(1)}, u32[]{:S(2)}, u32[]{:S(2)}) collective-permute-start(f32[64,256]{1,0:T(8,128)S(1)} %collective-permute-done.1.first), channel_id=1, source_target_pairs={{0,128},{1,129},{2,130},{3,131},{4,132},{5,133},{6,134},{7,135},{8... | collective-permute-start | bytes 196616 | tf_op jit(solution)/shard_map/ppermute | solution.py:71
  57.4 28.2 %copy-start.5 = (f32[2,2,64,256]{3,2,1,0:T(8,128)}, f32[2,2,64,256]{3,2,1,0:T(8,128)S(1)}, u32[]{:S(2)}) copy-start(f32[2,2,64,256]{3,2,1,0:T(8,128)S(1)} %get-tuple-element.20.block) | copy-start | bytes 786436
  57.4 28.2 %collective-permute-start.6 = (f32[2,2,64,256]{3,2,1,0:T(8,128)S(1)}, f32[2,2,64,256]{3,2,1,0:T(8,128)S(1)}, u32[]{:S(2)}, u32[]{:S(2)}) collective-permute-start(f32[2,2,64,256]{3,2,1,0:T(8,128)S(1)} %get-tuple-element.20.block), channel_id=1, source_target_pairs={{0,64},{1,65},{2,66},{3,67},{4,68},{5,69},{6,70},{7,71},{8,72},{9,... | collective-permute-start | bytes 786440 | tf_op jit(solution)/shard_map/ppermute | solution.py:71
  70.1 26.6 %collective-permute-start.5 = (f32[4,16,256]{2,1,0:T(8,128)S(1)}, f32[4,16,256]{2,1,0:T(8,128)S(1)}, u32[]{:S(2)}, u32[]{:S(2)}) collective-permute-start(f32[4,16,256]{2,1,0:T(8,128)S(1)} %get-tuple-element.19.summed), channel_id=1, source_target_pairs={{0,4},{1,5},{2,6},{3,7},{4,0},{5,1},{6,2},{7,3},{8,12},{9,13},{10,... | collective-permute-start | bytes 196616 | tf_op jit(solution)/shard_map/ppermute | solution.py:71
  85.6 0.7 copy-start.10
  86.3 31.2 %copy-start.2 = (f32[2,2,512,256]{3,2,1,0:T(8,128)S(1)}, f32[2,2,512,256]{3,2,1,0:T(8,128)}, u32[]{:S(2)}) copy-start(f32[2,2,512,256]{3,2,1,0:T(8,128)} %get-tuple-element.22.far_own_hbm) | copy-start | bytes 6291460
  86.3 31.2 %copy-start.7 = (s32[4,2]{1,0:T(4,128)S(1)}, s32[4,2]{1,0:T(4,128)}, u32[]{:S(2)}) copy-start(s32[4,2]{1,0:T(4,128)} %copy.8.pos) | copy-start | bytes 100
  86.3 31.2 %copy-start.8 = (s32[5]{0:T(128)S(1)}, s32[5]{0:T(128)}, u32[]{:S(2)}) copy-start(s32[5]{0:T(128)} %stack.23.flags) | copy-start | bytes 64
  95.1 22.4 %copy-start = (bf16[2,2,2,256,256]{4,3,2,1,0:T(8,128)(2,1)S(1)}, bf16[2,2,2,256,256]{4,3,2,1,0:T(8,128)(2,1)}, u32[]{:S(2)}) copy-start(bf16[2,2,2,256,256]{4,3,2,1,0:T(8,128)(2,1)} %constant.51.clone.table_hbm) | copy-start | bytes 3145732
  95.1 22.4 %copy-start.1 = (f32[1,2,256,256]{3,2,1,0:T(8,128)S(1)}, f32[1,2,256,256]{3,2,1,0:T(8,128)}, u32[]{:S(2)}) copy-start(f32[1,2,256,256]{3,2,1,0:T(8,128)} %param.6) | copy-start | bytes 1572868
  95.1 22.4 %copy-start.4 = (f32[2,256,256]{2,1,0:T(8,128)S(1)}, f32[2,256,256]{2,1,0:T(8,128)}, u32[]{:S(2)}) copy-start(f32[2,256,256]{2,1,0:T(8,128)} %get-tuple-element.24.probe_other_hbm) | copy-start | bytes 1572868
  96.7 0.8 copy-start.6
  117.5 1.6 %copy-start.3 = (f32[2,2,512,256]{3,2,1,0:T(8,128)S(1)}, f32[2,2,512,256]{3,2,1,0:T(8,128)}, u32[]{:S(2)}) copy-start(f32[2,2,512,256]{3,2,1,0:T(8,128)} %get-tuple-element.23.far_other_hbm) | copy-start | bytes 6291460
  126.2 8.6 %collective-permute-start.7 = (f32[16,2,8,512]{3,2,1,0:T(8,128)S(1)}, f32[16,2,8,512]{3,2,1,0:T(8,128)S(1)}, u32[]{:S(2)}, u32[]{:S(2)}) collective-permute-start(f32[16,2,8,512]{3,2,1,0:T(8,128)S(1)} %get-tuple-element.26), channel_id=1, source_target_pairs={{0,32},{1,33},{2,34},{3,35},{4,36},{5,37},{6,38},{7,39},{8,40},{9,... | collective-permute-start | bytes 1572872 | tf_op jit(solution)/shard_map/ppermute | solution.py:71
  135.7 15.5 %all-to-all-start.2 = ((f32[16,2,8,512]{3,2,1,0:T(8,128)}), f32[16,2,8,512]{3,2,1,0:T(8,128)S(1)}, u32[]{:S(2)}, u32[]{:S(2)}) async-start(f32[16,2,8,512]{3,2,1,0:T(8,128)} %add.30), calls=%async_computation.2 | async-start | bytes 1048576 | tf_op jit(solution)/shard_map/all_to_all | solution.py:475

commit v7 on v6

--- a/solution.py
+++ b/solution.py
@@ -241,23 +241,26 @@
             copy.wait()
 
 
+def share_kernel(flags, amp_hbm, measured, amp, sem):
+    plane = flags[2]
+    start = pl.multiple_of(lax.rem(plane, 8) * 2 * ROWS, 2 * ROWS)
+    copy = pltpu.make_async_copy(amp_hbm.at[:, pl.ds(start, 2 * ROWS)], amp, sem)
+    copy.start()
+    copy.wait()
+    measured[...] = own_share(amp[...], plane)
+
+
 def other_kernel(
-    pos, flags, own_hbm, halo_hbm, amp_hbm, table_hbm, block, next_block,
-    far_hbm, probe_hbm, measured, ext, amp, table, probe, far, sems, out_sems,
+    pos, flags, own_hbm, halo_hbm, table_hbm, block, next_block,
+    far_hbm, probe_hbm, ext, table, probe, far, sems, out_sems,
 ):
-    core, plane, quarter = flags[0], flags[2], flags[4]
-    start = pl.multiple_of(lax.rem(plane, 8) * 2 * ROWS, 2 * ROWS)
+    core, quarter = flags[0], flags[4]
     pairs = (
-        (amp_hbm.at[:, pl.ds(start, 2 * ROWS)], amp),
         (table_hbm, table),
         (own_hbm, ext.at[:, pl.ds(0, SIDE)]),
         (halo_hbm, ext.at[:, pl.ds(SIDE, SIDE)]),
     )
     copies = started(pairs, sems)
-    copies[0].wait()
-    measured[...] = own_share(amp[...], plane)
-    for copy in copies[1:]:
-        copy.wait()
     for channel in range(2):
         for part in range(SIDE // QUARTER):
             apart = jnp.bitwise_xor(quarter, part)
@@ -266,6 +269,8 @@
             probe[channel, part * QUARTER : (part + 1) * QUARTER] = value
     probe_copy = pltpu.make_async_copy(probe, probe_hbm, out_sems.at[COUNT // 2])
     probe_copy.start()
+    for copy in copies:
+        copy.wait()
 
     def far_copy(q):
         return pltpu.make_async_copy(far.at[q], far_hbm.at[q], out_sems.at[q])
@@ -355,7 +360,7 @@
 SMEM = pl.BlockSpec(memory_space=pltpu.SMEM)
 HBM = pl.BlockSpec(memory_space=pltpu.HBM)
 PAIRS = COUNT // 2
-ALL_VMEM, SOME_VMEM = 60, 32
+ALL_VMEM, OTHER_VMEM, SOME_VMEM = 60, 52, 32
 FAR = (PAIRS, 2, 2 * SIDE, SIDE)
 SHARES = (PLANE_SIZE, COUNT, ROWS, SIDE)
 DMA = pltpu.SemaphoreType.DMA
@@ -395,6 +400,16 @@
     probe = probe_modes[0]
 
     halo = moved(object_field, along_ring(-1))
+    (measured,) = call(
+        share_kernel,
+        "share",
+        [SMEM, HBM],
+        [(floats(COUNT, ROWS, SIDE), VMEM)],
+        [scratch(COUNT, 2 * ROWS, SIDE), DMA(())],
+        (flags, amplitude),
+        SOME_VMEM,
+    )
+    halo, measured, flags = lax.optimization_barrier((halo, measured, flags))
     piece = lax.dynamic_slice(probe, (core, quarter * QUARTER, 0), (1, QUARTER, SIDE))[0]
     first = moved(piece, across)
     far_own, intensity = call(
@@ -426,25 +441,7 @@
         (shares, first, *spread),
         SOME_VMEM,
     )
-    arrived = moved(summed, other_half)
-    next_block = moved(block, next_chip)
-    far_other, probe_other, measured = call(
-        other_kernel,
-        "other",
-        [SMEM] * 2 + [HBM] * 4 + [VMEM] * 2,
-        [(floats(*FAR), HBM), (floats(2, SIDE, SIDE), HBM), (floats(COUNT, ROWS, SIDE), VMEM)],
-        [
-            scratch(2, WIDTH, WIDTH),
-            scratch(COUNT, 2 * ROWS, SIDE),
-            TABLE,
-            scratch(2, SIDE, SIDE),
-            scratch(*FAR),
-            DMA((4,)),
-            DMA((PAIRS + 1,)),
-        ],
-        (positions, flags, object_field, halo, amplitude, table, block, next_block),
-        ALL_VMEM,
-    )
+    arrived, block = lax.optimization_barrier((moved(summed, other_half), block))
     (change,) = call(
         change_kernel,
         "change",
@@ -453,6 +450,23 @@
         [],
         (summed, arrived, measured),
         SOME_VMEM,
+    )
+    next_block = moved(block, next_chip)
+    far_other, probe_other = call(
+        other_kernel,
+        "other",
+        [SMEM] * 2 + [HBM] * 3 + [VMEM] * 2,
+        [(floats(*FAR), HBM), (floats(2, SIDE, SIDE), HBM)],
+        [
+            scratch(2, WIDTH, WIDTH),
+            TABLE,
+            scratch(2, SIDE, SIDE),
+            scratch(*FAR),
+            DMA((3,)),
+            DMA((PAIRS + 1,)),
+        ],
+        (positions, flags, object_field, halo, table, block, next_block),
+        OTHER_VMEM,
     )
     change = lax.all_to_all(change, PLANE, 0, 0)
     upper, lower = call(

time: 153 us -> 164 us (1.072)
  the two profiles are of different devices: /device:TPU:32 before, /device:TPU:33 now
where the time goes in v7:
time: 164 us; the launch traced here: 163 us
  starting transfers between devices  97.7 us (60%)
  waiting for transfers between devices  31.7 us (19%)
  Pallas kernels  23.8 us (15%)
  local copies, waits for them, and re-layouts  7.67 us (5%)
  other arithmetic  2.31 us (1%)
    ppermute x8, starting transfers between devices, moved(): return lax.ppermute(value, AXES, pairs_of(move))  79.7 us
    pallas_call x6, Pallas kernels, call(): pl.pallas_call(kernel, out_shape=[shape for shape, _ in outs], in_specs=i...  23.8 us
    ppermute x8, waiting for transfers between devices, moved(): return lax.ppermute(value, AXES, pairs_of(move))  17.6 us
    all_to_all x1, waiting for transfers between devices, body(): total = jnp.sum(lax.all_to_all(gradient, PLANE, 0, 0), 0)  11.3 us
    all_to_all x1, starting transfers between devices, body(): shares = lax.all_to_all(intensity, PLANE, 0, 0)  6.76 us
    unnamed x15, local copies, waits for them, and re-layouts  6.74 us
    all_to_all x1, starting transfers between devices, body(): total = jnp.sum(lax.all_to_all(gradient, PLANE, 0, 0), 0)  6.35 us
    all_to_all x1, starting transfers between devices, body(): change = lax.all_to_all(change, PLANE, 0, 0)  4.94 us
  transfers between devices with their start and end apart: 11, of which 6 were waited for; matrix products, arithmetic and copies ran while one was open for 1% of the time, Pallas kernels for 10%

profile of v7, /device:TPU:33, one launch (start us, length us, event | category | flops | bytes accessed | tf_op | source)
XLA Modules:
  0.0 163.4 jit_solution(6798274734638156382)
XLA Ops:
  0.0 0.7 collective-permute-start
  0.7 0.8 dynamic-slice_bitcast_fusion
  1.5 21.8 %collective-permute-start.1 = (f32[64,256]{1,0:T(8,128)S(1)}, f32[64,256]{1,0:T(8,128)S(1)}, u32[]{:S(2)}, u32[]{:S(2)}) collective-permute-start(f32[64,256]{1,0:T(8,128)S(1)} %dynamic-slice_bitcast_fusion), channel_id=1, source_target_pairs={{0,516},{1,517},{2,518},{3,519},{4,512},{5,513},{6,514},{7,515},{8... | collective-permute-start | bytes 196616 | tf_op jit(solution)/shard_map/ppermute | solution.py:71
  23.3 1.3 copy.8.pos
  24.7 0.1 stack.23.flags
  24.8 1.2 copy-done.4
  26.0 1.0 share.1.measured
  27.0 1.0 copy-done.6
  28.0 7.1 %own.1 = (f32[2,2,512,256]{3,2,1,0:T(8,128)}, f32[16,4,16,256]{3,2,1,0:T(8,128)}) custom-call(s32[4,2]{1,0:T(4,128)} %copy.8.pos, f32[2,256,512]{2,1,0:T(8,128)} %own_hbm.3, f32[2,256,512]{2,1,0:T(8,128)} %copy-done.6, f32[2,256,256]{2,1,0:T(8,128)} %bitcast.8, bf16[2,2,2,256,256]{4,3,2,1,0:T(8,128)(2,1)} %constant.51.clone.table_hbm), custom_call_target="tpu_custom_call" | custom-call | tf_op jit(solution)/shard_map/own/pallas_call | solution.py:381
  35.2 6.8 %all-to-all-start = ((f32[16,4,16,256]{3,2,1,0:T(8,128)}), f32[16,4,16,256]{3,2,1,0:T(8,128)S(1)}, u32[]{:S(2)}, u32[]{:S(2)}) async-start(f32[16,4,16,256]{3,2,1,0:T(8,128)} %get-tuple-element.23), calls=%async_computation | async-start | bytes 2097152 | tf_op jit(solution)/shard_map/all_to_all | solution.py:433
  41.9 3.1 %collective-permute-start.2 = (f32[64,256]{1,0:T(8,128)S(1)}, f32[64,256]{1,0:T(8,128)S(1)}, u32[]{:S(2)}, u32[]{:S(2)}) collective-permute-start(f32[64,256]{1,0:T(8,128)S(1)} %collective-permute-done.1.first), channel_id=1, source_target_pairs={{0,128},{1,129},{2,130},{3,131},{4,132},{5,133},{6,134},{7,135},{8... | collective-permute-start | bytes 196616 | tf_op jit(solution)/shard_map/ppermute | solution.py:71
  45.1 3.2 %collective-permute-start.3 = (f32[64,256]{1,0:T(8,128)S(1)}, f32[64,256]{1,0:T(8,128)S(1)}, u32[]{:S(2)}, u32[]{:S(2)}) collective-permute-start(f32[64,256]{1,0:T(8,128)S(1)} %collective-permute-done.1.first), channel_id=1, source_target_pairs={{0,32},{1,33},{2,34},{3,35},{4,36},{5,37},{6,38},{7,39},{8,40},{9,... | collective-permute-start | bytes 196616 | tf_op jit(solution)/shard_map/ppermute | solution.py:71
  48.3 3.0 %collective-permute-start.4 = (f32[64,256]{1,0:T(8,128)S(1)}, f32[64,256]{1,0:T(8,128)S(1)}, u32[]{:S(2)}, u32[]{:S(2)}) collective-permute-start(f32[64,256]{1,0:T(8,128)S(1)} %collective-permute-done.1.first), channel_id=1, source_target_pairs={{0,160},{1,161},{2,162},{3,163},{4,164},{5,165},{6,166},{7,167},{8... | collective-permute-start | bytes 196616 | tf_op jit(solution)/shard_map/ppermute | solution.py:71
  51.3 3.8 %collective-permute-done.4.crossed_second = f32[64,256]{1,0:T(8,128)S(1)} collective-permute-done((f32[64,256]{1,0:T(8,128)S(1)}, f32[64,256]{1,0:T(8,128)S(1)}, u32[]{:S(2)}, u32[]{:S(2)}) %collective-permute-start.4) | collective-permute-done | bytes 65568 | tf_op jit(solution)/shard_map/ppermute | solution.py:71
  55.1 2.8 %all-to-all-done.shares = f32[16,4,16,256]{3,2,1,0:T(8,128)S(1)} async-done(((f32[16,4,16,256]{3,2,1,0:T(8,128)}), f32[16,4,16,256]{3,2,1,0:T(8,128)S(1)}, u32[]{:S(2)}, u32[]{:S(2)}) %all-to-all-start) | async-done | bytes 1048608 | tf_op jit(solution)/shard_map/all_to_all | solution.py:433
  57.9 0.1 collect.1
  57.9 21.6 %collective-permute-start.5 = (f32[4,16,256]{2,1,0:T(8,128)S(1)}, f32[4,16,256]{2,1,0:T(8,128)S(1)}, u32[]{:S(2)}, u32[]{:S(2)}) collective-permute-start(f32[4,16,256]{2,1,0:T(8,128)S(1)} %get-tuple-element.25.summed), channel_id=1, source_target_pairs={{0,4},{1,5},{2,6},{3,7},{4,0},{5,1},{6,2},{7,3},{8,12},{9,13},{10,... | collective-permute-start | bytes 196616 | tf_op jit(solution)/shard_map/ppermute | solution.py:71
  79.5 2.0 %collective-permute-done.5.arrived = f32[4,16,256]{2,1,0:T(8,128)S(1)} collective-permute-done((f32[4,16,256]{2,1,0:T(8,128)S(1)}, f32[4,16,256]{2,1,0:T(8,128)S(1)}, u32[]{:S(2)}, u32[]{:S(2)}) %collective-permute-start.5) | collective-permute-done | bytes 65568 | tf_op jit(solution)/shard_map/ppermute | solution.py:71
  81.5 1.1 change.1
  82.6 4.9 %all-to-all-start.1 = ((f32[16,4,16,256]{3,2,1,0:T(8,128)}), f32[16,4,16,256]{3,2,1,0:T(8,128)S(1)}, u32[]{:S(2)}, u32[]{:S(2)}) async-start(f32[16,4,16,256]{3,2,1,0:T(8,128)} %change.1), calls=%async_computation.1 | async-start | bytes 2097152 | tf_op jit(solution)/shard_map/all_to_all | solution.py:471
  87.6 20.8 %collective-permute-start.6 = (f32[2,2,64,256]{3,2,1,0:T(8,128)S(1)}, f32[2,2,64,256]{3,2,1,0:T(8,128)S(1)}, u32[]{:S(2)}, u32[]{:S(2)}) collective-permute-start(f32[2,2,64,256]{3,2,1,0:T(8,128)S(1)} %get-tuple-element.30.block), channel_id=1, source_target_pairs={{0,64},{1,65},{2,66},{3,67},{4,68},{5,69},{6,70},{7,71},{8,72},{9,... | collective-permute-start | bytes 786440 | tf_op jit(solution)/shard_map/ppermute | solution.py:71
  108.3 5.7 %collective-permute-done.6.next_block = f32[2,2,64,256]{3,2,1,0:T(8,128)S(1)} collective-permute-done((f32[2,2,64,256]{3,2,1,0:T(8,128)S(1)}, f32[2,2,64,256]{3,2,1,0:T(8,128)S(1)}, u32[]{:S(2)}, u32[]{:S(2)}) %collective-permute-start.6) | collective-permute-done | bytes 262176 | tf_op jit(solution)/shard_map/ppermute | solution.py:71
  114.1 7.4 %other.1 = (f32[2,2,512,256]{3,2,1,0:T(8,128)}, f32[2,256,256]{2,1,0:T(8,128)S(1)}) custom-call(s32[4,2]{1,0:T(4,128)S(1)} %copy-done.5, s32[5]{0:T(128)S(1)} %stack.23.flags, f32[2,256,512]{2,1,0:T(8,128)} %own_hbm.3, f32[2,256,512]{2,1,0:T(8,128)} %copy-done.6, bf16[2,2,2,256,256]{4,3,2,1,0:T(8,128)(2,1)} %constant.51.clone.table_hbm, ...), custom_call_target="tpu_custom_call" | custom-call | tf_op jit(solution)/shard_map/other/pallas_call | solution.py:381
  121.5 1.6 copy-done.2
  123.1 1.6 copy-done.3
  124.7 7.0 %inverse.1 = (f32[16,2,8,512]{3,2,1,0:T(8,128)S(1)}, f32[16,2,8,512]{3,2,1,0:T(8,128)S(1)}) custom-call(s32[4,2]{1,0:T(4,128)S(1)} %copy-done.5, s32[5]{0:T(128)S(1)} %stack.23.flags, f32[16,4,16,256]{3,2,1,0:T(8,128)S(1)} %all-to-all-done.1.change, f32[2,2,512,256]{3,2,1,0:T(8,128)S(1)} %copy-done.2, f32[2,2,512,256]{3,2,1,0:T(8,128)S(1)} %copy-done.3, ...), custom_call_target="tpu_custom_call" | custom-call | tf_op jit(solution)/shard_map/inverse/pallas_call | solution.py:381
  131.8 5.6 %collective-permute-start.7 = (f32[16,2,8,512]{3,2,1,0:T(8,128)S(1)}, f32[16,2,8,512]{3,2,1,0:T(8,128)S(1)}, u32[]{:S(2)}, u32[]{:S(2)}) collective-permute-start(f32[16,2,8,512]{3,2,1,0:T(8,128)S(1)} %get-tuple-element.34), channel_id=1, source_target_pairs={{0,32},{1,33},{2,34},{3,35},{4,36},{5,37},{6,38},{7,39},{8,40},{9,... | collective-permute-start | bytes 1572872 | tf_op jit(solution)/shard_map/ppermute | solution.py:71
  137.3 6.1 %collective-permute-done.7 = f32[16,2,8,512]{3,2,1,0:T(8,128)S(1)} collective-permute-done((f32[16,2,8,512]{3,2,1,0:T(8,128)S(1)}, f32[16,2,8,512]{3,2,1,0:T(8,128)S(1)}, u32[]{:S(2)}, u32[]{:S(2)}) %collective-permute-start.7) | collective-permute-done | bytes 524320 | tf_op jit(solution)/shard_map/ppermute | solution.py:71
  143.5 0.9 add.30
  144.3 6.4 %all-to-all-start.2 = ((f32[16,2,8,512]{3,2,1,0:T(8,128)}), f32[16,2,8,512]{3,2,1,0:T(8,128)S(1)}, u32[]{:S(2)}, u32[]{:S(2)}) async-start(f32[16,2,8,512]{3,2,1,0:T(8,128)} %add.30), calls=%async_computation.2 | async-start | bytes 1048576 | tf_op jit(solution)/shard_map/all_to_all | solution.py:489
  150.7 11.3 %all-to-all-done.2 = f32[16,2,8,512]{3,2,1,0:T(8,128)S(1)} async-done(((f32[16,2,8,512]{3,2,1,0:T(8,128)}), f32[16,2,8,512]{3,2,1,0:T(8,128)S(1)}, u32[]{:S(2)}, u32[]{:S(2)}) %all-to-all-start.2) | async-done | bytes 524320 | tf_op jit(solution)/shard_map/all_to_all | solution.py:489
  162.0 1.4 multiply_add_fusion
  (16 shorter events, 0.1 us)
Async XLA Ops:
  0.0 27.0 %collective-permute-start = (f32[2,256,512]{2,1,0:T(8,128)}, f32[2,256,512]{2,1,0:T(8,128)S(1)}, u32[]{:S(2)}, u32[]{:S(2)}) collective-permute-start(f32[2,256,512]{2,1,0:T(8,128)} %own_hbm.3), channel_id=1, source_target_pairs={{0,996},{1,997},{2,998},{3,999},{4,992},{5,993},{6,994},{7,995},{8... | collective-permute-start | bytes 3145736 | tf_op jit(solution)/shard_map/ppermute | solution.py:71
  1.5 33.6 %collective-permute-start.1 = (f32[64,256]{1,0:T(8,128)S(1)}, f32[64,256]{1,0:T(8,128)S(1)}, u32[]{:S(2)}, u32[]{:S(2)}) collective-permute-start(f32[64,256]{1,0:T(8,128)S(1)} %dynamic-slice_bitcast_fusion), channel_id=1, source_target_pairs={{0,516},{1,517},{2,518},{3,519},{4,512},{5,513},{6,514},{7,515},{8... | collective-permute-start | bytes 196616 | tf_op jit(solution)/shard_map/ppermute | solution.py:71
  24.8 1.2 copy-start.4
  27.0 1.0 copy-start.6
  35.2 22.7 %all-to-all-start = ((f32[16,4,16,256]{3,2,1,0:T(8,128)}), f32[16,4,16,256]{3,2,1,0:T(8,128)S(1)}, u32[]{:S(2)}, u32[]{:S(2)}) async-start(f32[16,4,16,256]{3,2,1,0:T(8,128)} %get-tuple-element.23), calls=%async_computation | async-start | bytes 2097152 | tf_op jit(solution)/shard_map/all_to_all | solution.py:433
  41.9 72.1 %copy-start.5 = (s32[4,2]{1,0:T(4,128)S(1)}, s32[4,2]{1,0:T(4,128)}, u32[]{:S(2)}) copy-start(s32[4,2]{1,0:T(4,128)} %copy.8.pos) | copy-start | bytes 100
  41.9 9.3 %collective-permute-start.2 = (f32[64,256]{1,0:T(8,128)S(1)}, f32[64,256]{1,0:T(8,128)S(1)}, u32[]{:S(2)}, u32[]{:S(2)}) collective-permute-start(f32[64,256]{1,0:T(8,128)S(1)} %collective-permute-done.1.first), channel_id=1, source_target_pairs={{0,128},{1,129},{2,130},{3,131},{4,132},{5,133},{6,134},{7,135},{8... | collective-permute-start | bytes 196616 | tf_op jit(solution)/shard_map/ppermute | solution.py:71
  45.1 6.2 %collective-permute-start.3 = (f32[64,256]{1,0:T(8,128)S(1)}, f32[64,256]{1,0:T(8,128)S(1)}, u32[]{:S(2)}, u32[]{:S(2)}) collective-permute-start(f32[64,256]{1,0:T(8,128)S(1)} %collective-permute-done.1.first), channel_id=1, source_target_pairs={{0,32},{1,33},{2,34},{3,35},{4,36},{5,37},{6,38},{7,39},{8,40},{9,... | collective-permute-start | bytes 196616 | tf_op jit(solution)/shard_map/ppermute | solution.py:71
  48.3 6.8 %collective-permute-start.4 = (f32[64,256]{1,0:T(8,128)S(1)}, f32[64,256]{1,0:T(8,128)S(1)}, u32[]{:S(2)}, u32[]{:S(2)}) collective-permute-start(f32[64,256]{1,0:T(8,128)S(1)} %collective-permute-done.1.first), channel_id=1, source_target_pairs={{0,160},{1,161},{2,162},{3,163},{4,164},{5,165},{6,166},{7,167},{8... | collective-permute-start | bytes 196616 | tf_op jit(solution)/shard_map/ppermute | solution.py:71
  57.9 23.5 %collective-permute-start.5 = (f32[4,16,256]{2,1,0:T(8,128)S(1)}, f32[4,16,256]{2,1,0:T(8,128)S(1)}, u32[]{:S(2)}, u32[]{:S(2)}) collective-permute-start(f32[4,16,256]{2,1,0:T(8,128)S(1)} %get-tuple-element.25.summed), channel_id=1, source_target_pairs={{0,4},{1,5},{2,6},{3,7},{4,0},{5,1},{6,2},{7,3},{8,12},{9,13},{10,... | collective-permute-start | bytes 196616 | tf_op jit(solution)/shard_map/ppermute | solution.py:71
  82.6 38.9 %all-to-all-start.1 = ((f32[16,4,16,256]{3,2,1,0:T(8,128)}), f32[16,4,16,256]{3,2,1,0:T(8,128)S(1)}, u32[]{:S(2)}, u32[]{:S(2)}) async-start(f32[16,4,16,256]{3,2,1,0:T(8,128)} %change.1), calls=%async_computation.1 | async-start | bytes 2097152 | tf_op jit(solution)/shard_map/all_to_all | solution.py:471
  87.5 34.0 %copy-start = (bf16[2,2,2,256,256]{4,3,2,1,0:T(8,128)(2,1)S(1)}, bf16[2,2,2,256,256]{4,3,2,1,0:T(8,128)(2,1)}, u32[]{:S(2)}) copy-start(bf16[2,2,2,256,256]{4,3,2,1,0:T(8,128)(2,1)} %constant.51.clone.table_hbm) | copy-start | bytes 3145732
  87.5 34.0 %copy-start.1 = (f32[1,2,256,256]{3,2,1,0:T(8,128)S(1)}, f32[1,2,256,256]{3,2,1,0:T(8,128)}, u32[]{:S(2)}) copy-start(f32[1,2,256,256]{3,2,1,0:T(8,128)} %param.6) | copy-start | bytes 1572868
  87.6 26.5 %collective-permute-start.6 = (f32[2,2,64,256]{3,2,1,0:T(8,128)S(1)}, f32[2,2,64,256]{3,2,1,0:T(8,128)S(1)}, u32[]{:S(2)}, u32[]{:S(2)}) collective-permute-start(f32[2,2,64,256]{3,2,1,0:T(8,128)S(1)} %get-tuple-element.30.block), channel_id=1, source_target_pairs={{0,64},{1,65},{2,66},{3,67},{4,68},{5,69},{6,70},{7,71},{8,72},{9,... | collective-permute-start | bytes 786440 | tf_op jit(solution)/shard_map/ppermute | solution.py:71
  121.5 1.6 copy-start.2
  123.1 1.6 copy-start.3
  131.8 11.7 %collective-permute-start.7 = (f32[16,2,8,512]{3,2,1,0:T(8,128)S(1)}, f32[16,2,8,512]{3,2,1,0:T(8,128)S(1)}, u32[]{:S(2)}, u32[]{:S(2)}) collective-permute-start(f32[16,2,8,512]{3,2,1,0:T(8,128)S(1)} %get-tuple-element.34), channel_id=1, source_target_pairs={{0,32},{1,33},{2,34},{3,35},{4,36},{5,37},{6,38},{7,39},{8,40},{9,... | collective-permute-start | bytes 1572872 | tf_op jit(solution)/shard_map/ppermute | solution.py:71
  144.3 17.6 %all-to-all-start.2 = ((f32[16,2,8,512]{3,2,1,0:T(8,128)}), f32[16,2,8,512]{3,2,1,0:T(8,128)S(1)}, u32[]{:S(2)}, u32[]{:S(2)}) async-start(f32[16,2,8,512]{3,2,1,0:T(8,128)} %add.30), calls=%async_computation.2 | async-start | bytes 1048576 | tf_op jit(solution)/shard_map/all_to_all | solution.py:489

commit v8 on v7

--- a/solution.py
+++ b/solution.py
@@ -441,16 +441,7 @@
         (shares, first, *spread),
         SOME_VMEM,
     )
-    arrived, block = lax.optimization_barrier((moved(summed, other_half), block))
-    (change,) = call(
-        change_kernel,
-        "change",
-        [VMEM] * 3,
-        [(floats(*SHARES), VMEM)],
-        [],
-        (summed, arrived, measured),
-        SOME_VMEM,
-    )
+    arrived = moved(summed, other_half)
     next_block = moved(block, next_chip)
     far_other, probe_other = call(
         other_kernel,
@@ -468,6 +459,16 @@
         (positions, flags, object_field, halo, table, block, next_block),
         OTHER_VMEM,
     )
+    arrived, far_other, probe_other = lax.optimization_barrier((arrived, far_other, probe_other))
+    (change,) = call(
+        change_kernel,
+        "change",
+        [VMEM] * 3,
+        [(floats(*SHARES), VMEM)],
+        [],
+        (summed, arrived, measured),
+        SOME_VMEM,
+    )
     change = lax.all_to_all(change, PLANE, 0, 0)
     upper, lower = call(
         inverse_kernel,

time: 164 us -> 154 us (0.939)
  the two profiles are of different devices: /device:TPU:33 before, /device:TPU:2 now
where the time goes in v8:
time: 154 us; the launch traced here: 153 us
  starting transfers between devices  63.5 us (41%)
  waiting for transfers between devices  34.7 us (23%)
  blocking collectives  23.5 us (15%)
  Pallas kernels  22.8 us (15%)
  local copies, waits for them, and re-layouts  6.08 us (4%)
  other arithmetic  2.3 us (1%)
    ppermute x8, starting transfers between devices, moved(): return lax.ppermute(value, AXES, pairs_of(move))  51.2 us
    ppermute x8, waiting for transfers between devices, moved(): return lax.ppermute(value, AXES, pairs_of(move))  25 us
    all_to_all x1, blocking collectives, body(): change = lax.all_to_all(change, PLANE, 0, 0)  23.5 us
    pallas_call x6, Pallas kernels, call(): pl.pallas_call(kernel, out_shape=[shape for shape, _ in outs], in_specs=i...  22.8 us
    all_to_all x1, waiting for transfers between devices, body(): total = jnp.sum(lax.all_to_all(gradient, PLANE, 0, 0), 0)  8.87 us
    all_to_all x1, starting transfers between devices, body(): shares = lax.all_to_all(intensity, PLANE, 0, 0)  7.49 us
    unnamed x15, local copies, waits for them, and re-layouts  5.15 us
    all_to_all x1, starting transfers between devices, body(): total = jnp.sum(lax.all_to_all(gradient, PLANE, 0, 0), 0)  4.82 us
  transfers between devices with their start and end apart: 10, of which 6 were waited for; matrix products, arithmetic and copies ran while one was open for 1% of the time, Pallas kernels for 10%

profile of v8, /device:TPU:2, one launch (start us, length us, event | category | flops | bytes accessed | tf_op | source)
XLA Modules:
  0.0 153.1 jit_solution(9417803473182671995)
XLA Ops:
  0.0 16.2 %collective-permute-start = (f32[2,256,512]{2,1,0:T(8,128)}, f32[2,256,512]{2,1,0:T(8,128)S(1)}, u32[]{:S(2)}, u32[]{:S(2)}) collective-permute-start(f32[2,256,512]{2,1,0:T(8,128)} %own_hbm.3), channel_id=1, source_target_pairs={{0,996},{1,997},{2,998},{3,999},{4,992},{5,993},{6,994},{7,995},{8... | collective-permute-start | bytes 3145736 | tf_op jit(solution)/shard_map/ppermute | solution.py:71
  16.2 0.8 dynamic-slice_bitcast_fusion
  17.1 8.4 %collective-permute-start.1 = (f32[64,256]{1,0:T(8,128)S(1)}, f32[64,256]{1,0:T(8,128)S(1)}, u32[]{:S(2)}, u32[]{:S(2)}) collective-permute-start(f32[64,256]{1,0:T(8,128)S(1)} %dynamic-slice_bitcast_fusion), channel_id=1, source_target_pairs={{0,516},{1,517},{2,518},{3,519},{4,512},{5,513},{6,514},{7,515},{8... | collective-permute-start | bytes 196616 | tf_op jit(solution)/shard_map/ppermute | solution.py:71
  25.5 1.3 copy.8.pos
  26.8 0.1 stack.23.flags
  26.9 1.2 copy-done.4
  28.2 1.0 share.1.measured
  29.2 10.2 %collective-permute-done.halo_hbm = f32[2,256,512]{2,1,0:T(8,128)S(1)} collective-permute-done((f32[2,256,512]{2,1,0:T(8,128)}, f32[2,256,512]{2,1,0:T(8,128)S(1)}, u32[]{:S(2)}, u32[]{:S(2)}) %collective-permute-start) | collective-permute-done | bytes 1048608 | tf_op jit(solution)/shard_map/ppermute | solution.py:71
  39.4 1.0 copy-done.6
  40.4 7.1 %own.1 = (f32[2,2,512,256]{3,2,1,0:T(8,128)}, f32[16,4,16,256]{3,2,1,0:T(8,128)}) custom-call(s32[4,2]{1,0:T(4,128)} %copy.8.pos, f32[2,256,512]{2,1,0:T(8,128)} %own_hbm.3, f32[2,256,512]{2,1,0:T(8,128)} %copy-done.6, f32[2,256,256]{2,1,0:T(8,128)} %bitcast.8, bf16[2,2,2,256,256]{4,3,2,1,0:T(8,128)(2,1)} %constant.51.clone.table_hbm), custom_call_target="tpu_custom_call" | custom-call | tf_op jit(solution)/shard_map/own/pallas_call | solution.py:381
  47.5 7.5 %all-to-all-start = ((f32[16,4,16,256]{3,2,1,0:T(8,128)}), f32[16,4,16,256]{3,2,1,0:T(8,128)S(1)}, u32[]{:S(2)}, u32[]{:S(2)}) async-start(f32[16,4,16,256]{3,2,1,0:T(8,128)} %get-tuple-element.24), calls=%async_computation | async-start | bytes 2097152 | tf_op jit(solution)/shard_map/all_to_all | solution.py:433
  55.0 1.9 %collective-permute-start.4 = (f32[64,256]{1,0:T(8,128)S(1)}, f32[64,256]{1,0:T(8,128)S(1)}, u32[]{:S(2)}, u32[]{:S(2)}) collective-permute-start(f32[64,256]{1,0:T(8,128)S(1)} %collective-permute-done.1.first), channel_id=1, source_target_pairs={{0,160},{1,161},{2,162},{3,163},{4,164},{5,165},{6,166},{7,167},{8... | collective-permute-start | bytes 196616 | tf_op jit(solution)/shard_map/ppermute | solution.py:71
  56.9 1.9 %collective-permute-start.3 = (f32[64,256]{1,0:T(8,128)S(1)}, f32[64,256]{1,0:T(8,128)S(1)}, u32[]{:S(2)}, u32[]{:S(2)}) collective-permute-start(f32[64,256]{1,0:T(8,128)S(1)} %collective-permute-done.1.first), channel_id=1, source_target_pairs={{0,32},{1,33},{2,34},{3,35},{4,36},{5,37},{6,38},{7,39},{8,40},{9,... | collective-permute-start | bytes 196616 | tf_op jit(solution)/shard_map/ppermute | solution.py:71
  58.9 4.9 %collective-permute-start.2 = (f32[64,256]{1,0:T(8,128)S(1)}, f32[64,256]{1,0:T(8,128)S(1)}, u32[]{:S(2)}, u32[]{:S(2)}) collective-permute-start(f32[64,256]{1,0:T(8,128)S(1)} %collective-permute-done.1.first), channel_id=1, source_target_pairs={{0,128},{1,129},{2,130},{3,131},{4,132},{5,133},{6,134},{7,135},{8... | collective-permute-start | bytes 196616 | tf_op jit(solution)/shard_map/ppermute | solution.py:71
  63.8 2.3 %collective-permute-done.2.second = f32[64,256]{1,0:T(8,128)S(1)} collective-permute-done((f32[64,256]{1,0:T(8,128)S(1)}, f32[64,256]{1,0:T(8,128)S(1)}, u32[]{:S(2)}, u32[]{:S(2)}) %collective-permute-start.2) | collective-permute-done | bytes 65568 | tf_op jit(solution)/shard_map/ppermute | solution.py:71
  66.2 0.8 all-to-all-done.shares
  67.0 0.1 collect.1
  67.0 1.9 %collective-permute-start.6 = (f32[2,2,64,256]{3,2,1,0:T(8,128)S(1)}, f32[2,2,64,256]{3,2,1,0:T(8,128)S(1)}, u32[]{:S(2)}, u32[]{:S(2)}) collective-permute-start(f32[2,2,64,256]{3,2,1,0:T(8,128)S(1)} %get-tuple-element.27.block), channel_id=1, source_target_pairs={{0,64},{1,65},{2,66},{3,67},{4,68},{5,69},{6,70},{7,71},{8,72},{9,... | collective-permute-start | bytes 786440 | tf_op jit(solution)/shard_map/ppermute | solution.py:71
  69.0 15.9 %collective-permute-start.5 = (f32[4,16,256]{2,1,0:T(8,128)S(1)}, f32[4,16,256]{2,1,0:T(8,128)S(1)}, u32[]{:S(2)}, u32[]{:S(2)}) collective-permute-start(f32[4,16,256]{2,1,0:T(8,128)S(1)} %get-tuple-element.26.summed), channel_id=1, source_target_pairs={{0,4},{1,5},{2,6},{3,7},{4,0},{5,1},{6,2},{7,3},{8,12},{9,13},{10,... | collective-permute-start | bytes 196616 | tf_op jit(solution)/shard_map/ppermute | solution.py:71
  84.9 7.5 %other.1 = (f32[2,2,512,256]{3,2,1,0:T(8,128)}, f32[2,256,256]{2,1,0:T(8,128)S(1)}) custom-call(s32[4,2]{1,0:T(4,128)S(1)} %copy-done.5, s32[5]{0:T(128)S(1)} %stack.23.flags, f32[2,256,512]{2,1,0:T(8,128)} %own_hbm.3, f32[2,256,512]{2,1,0:T(8,128)} %copy-done.6, bf16[2,2,2,256,256]{4,3,2,1,0:T(8,128)(2,1)} %constant.51.clone.table_hbm, ...), custom_call_target="tpu_custom_call" | custom-call | tf_op jit(solution)/shard_map/other/pallas_call | solution.py:381
  92.4 0.0 copy-start
  92.4 1.2 collective-permute-done.5.arrived
  93.6 0.1 change.1
  93.7 23.5 %all_to_all.15.change = f32[16,4,16,256]{3,2,1,0:T(8,128)S(1)} all-to-all(f32[16,4,16,256]{3,2,1,0:T(8,128)S(1)} %change.1), channel_id=1, replica_groups=mesh['zlo'=16,'core'=2,'y'=4,'zhi'=2,'x'=4] {'y','x'}, dimensions={0} | all-to-all | bytes 2097152 | tf_op jit(solution)/shard_map/all_to_all | solution.py:472
  117.2 1.6 %copy-done.3 = f32[2,2,512,256]{3,2,1,0:T(8,128)S(1)} copy-done((f32[2,2,512,256]{3,2,1,0:T(8,128)S(1)}, f32[2,2,512,256]{3,2,1,0:T(8,128)}, u32[]{:S(2)}) %copy-start.3) | copy-done | bytes 2097176
  118.8 7.0 %inverse.1 = (f32[16,2,8,512]{3,2,1,0:T(8,128)S(1)}, f32[16,2,8,512]{3,2,1,0:T(8,128)S(1)}) custom-call(s32[4,2]{1,0:T(4,128)S(1)} %copy-done.5, s32[5]{0:T(128)S(1)} %stack.23.flags, f32[16,4,16,256]{3,2,1,0:T(8,128)S(1)} %all_to_all.15.change, f32[2,2,512,256]{3,2,1,0:T(8,128)S(1)} %copy-done.2, f32[2,2,512,256]{3,2,1,0:T(8,128)S(1)} %copy-done.3, ...), custom_call_target="tpu_custom_call" | custom-call | tf_op jit(solution)/shard_map/inverse/pallas_call | solution.py:381
  125.8 0.0 collective-permute-start.7
  125.9 11.2 %collective-permute-done.7 = f32[16,2,8,512]{3,2,1,0:T(8,128)S(1)} collective-permute-done((f32[16,2,8,512]{3,2,1,0:T(8,128)S(1)}, f32[16,2,8,512]{3,2,1,0:T(8,128)S(1)}, u32[]{:S(2)}, u32[]{:S(2)}) %collective-permute-start.7) | collective-permute-done | bytes 524320 | tf_op jit(solution)/shard_map/ppermute | solution.py:71
  137.1 0.9 add.30
  138.0 4.8 %all-to-all-start.2 = ((f32[16,2,8,512]{3,2,1,0:T(8,128)}), f32[16,2,8,512]{3,2,1,0:T(8,128)S(1)}, u32[]{:S(2)}, u32[]{:S(2)}) async-start(f32[16,2,8,512]{3,2,1,0:T(8,128)} %add.30), calls=%async_computation.2 | async-start | bytes 1048576 | tf_op jit(solution)/shard_map/all_to_all | solution.py:490
  142.8 8.9 %all-to-all-done.2 = f32[16,2,8,512]{3,2,1,0:T(8,128)S(1)} async-done(((f32[16,2,8,512]{3,2,1,0:T(8,128)}), f32[16,2,8,512]{3,2,1,0:T(8,128)S(1)}, u32[]{:S(2)}, u32[]{:S(2)}) %all-to-all-start.2) | async-done | bytes 524320 | tf_op jit(solution)/shard_map/all_to_all | solution.py:490
  151.7 1.4 multiply_add_fusion
  (15 shorter events, 0.1 us)
Async XLA Ops:
  0.0 39.4 %collective-permute-start = (f32[2,256,512]{2,1,0:T(8,128)}, f32[2,256,512]{2,1,0:T(8,128)S(1)}, u32[]{:S(2)}, u32[]{:S(2)}) collective-permute-start(f32[2,256,512]{2,1,0:T(8,128)} %own_hbm.3), channel_id=1, source_target_pairs={{0,996},{1,997},{2,998},{3,999},{4,992},{5,993},{6,994},{7,995},{8... | collective-permute-start | bytes 3145736 | tf_op jit(solution)/shard_map/ppermute | solution.py:71
  17.1 30.5 %collective-permute-start.1 = (f32[64,256]{1,0:T(8,128)S(1)}, f32[64,256]{1,0:T(8,128)S(1)}, u32[]{:S(2)}, u32[]{:S(2)}) collective-permute-start(f32[64,256]{1,0:T(8,128)S(1)} %dynamic-slice_bitcast_fusion), channel_id=1, source_target_pairs={{0,516},{1,517},{2,518},{3,519},{4,512},{5,513},{6,514},{7,515},{8... | collective-permute-start | bytes 196616 | tf_op jit(solution)/shard_map/ppermute | solution.py:71
  26.9 1.2 copy-start.4
  39.4 1.0 copy-start.6
  47.5 37.3 %copy-start.5 = (s32[4,2]{1,0:T(4,128)S(1)}, s32[4,2]{1,0:T(4,128)}, u32[]{:S(2)}) copy-start(s32[4,2]{1,0:T(4,128)} %copy.8.pos) | copy-start | bytes 100
  47.5 19.4 %all-to-all-start = ((f32[16,4,16,256]{3,2,1,0:T(8,128)}), f32[16,4,16,256]{3,2,1,0:T(8,128)S(1)}, u32[]{:S(2)}, u32[]{:S(2)}) async-start(f32[16,4,16,256]{3,2,1,0:T(8,128)} %get-tuple-element.24), calls=%async_computation | async-start | bytes 2097152 | tf_op jit(solution)/shard_map/all_to_all | solution.py:433
  55.0 8.8 %collective-permute-start.4 = (f32[64,256]{1,0:T(8,128)S(1)}, f32[64,256]{1,0:T(8,128)S(1)}, u32[]{:S(2)}, u32[]{:S(2)}) collective-permute-start(f32[64,256]{1,0:T(8,128)S(1)} %collective-permute-done.1.first), channel_id=1, source_target_pairs={{0,160},{1,161},{2,162},{3,163},{4,164},{5,165},{6,166},{7,167},{8... | collective-permute-start | bytes 196616 | tf_op jit(solution)/shard_map/ppermute | solution.py:71
  56.9 6.9 %collective-permute-start.3 = (f32[64,256]{1,0:T(8,128)S(1)}, f32[64,256]{1,0:T(8,128)S(1)}, u32[]{:S(2)}, u32[]{:S(2)}) collective-permute-start(f32[64,256]{1,0:T(8,128)S(1)} %collective-permute-done.1.first), channel_id=1, source_target_pairs={{0,32},{1,33},{2,34},{3,35},{4,36},{5,37},{6,38},{7,39},{8,40},{9,... | collective-permute-start | bytes 196616 | tf_op jit(solution)/shard_map/ppermute | solution.py:71
  58.9 7.3 %collective-permute-start.2 = (f32[64,256]{1,0:T(8,128)S(1)}, f32[64,256]{1,0:T(8,128)S(1)}, u32[]{:S(2)}, u32[]{:S(2)}) collective-permute-start(f32[64,256]{1,0:T(8,128)S(1)} %collective-permute-done.1.first), channel_id=1, source_target_pairs={{0,128},{1,129},{2,130},{3,131},{4,132},{5,133},{6,134},{7,135},{8... | collective-permute-start | bytes 196616 | tf_op jit(solution)/shard_map/ppermute | solution.py:71
  67.0 17.8 %collective-permute-start.6 = (f32[2,2,64,256]{3,2,1,0:T(8,128)S(1)}, f32[2,2,64,256]{3,2,1,0:T(8,128)S(1)}, u32[]{:S(2)}, u32[]{:S(2)}) collective-permute-start(f32[2,2,64,256]{3,2,1,0:T(8,128)S(1)} %get-tuple-element.27.block), channel_id=1, source_target_pairs={{0,64},{1,65},{2,66},{3,67},{4,68},{5,69},{6,70},{7,71},{8,72},{9,... | collective-permute-start | bytes 786440 | tf_op jit(solution)/shard_map/ppermute | solution.py:71
  69.0 24.6 %collective-permute-start.5 = (f32[4,16,256]{2,1,0:T(8,128)S(1)}, f32[4,16,256]{2,1,0:T(8,128)S(1)}, u32[]{:S(2)}, u32[]{:S(2)}) collective-permute-start(f32[4,16,256]{2,1,0:T(8,128)S(1)} %get-tuple-element.26.summed), channel_id=1, source_target_pairs={{0,4},{1,5},{2,6},{3,7},{4,0},{5,1},{6,2},{7,3},{8,12},{9,13},{10,... | collective-permute-start | bytes 196616 | tf_op jit(solution)/shard_map/ppermute | solution.py:71
  84.9 32.3 %copy-start.2 = (f32[2,2,512,256]{3,2,1,0:T(8,128)S(1)}, f32[2,2,512,256]{3,2,1,0:T(8,128)}, u32[]{:S(2)}) copy-start(f32[2,2,512,256]{3,2,1,0:T(8,128)} %get-tuple-element.32.far_own_hbm) | copy-start | bytes 6291460
  92.4 24.8 %copy-start = (bf16[2,2,2,256,256]{4,3,2,1,0:T(8,128)(2,1)S(1)}, bf16[2,2,2,256,256]{4,3,2,1,0:T(8,128)(2,1)}, u32[]{:S(2)}) copy-start(bf16[2,2,2,256,256]{4,3,2,1,0:T(8,128)(2,1)} %constant.51.clone.table_hbm) | copy-start | bytes 3145732
  92.4 24.8 %copy-start.1 = (f32[1,2,256,256]{3,2,1,0:T(8,128)S(1)}, f32[1,2,256,256]{3,2,1,0:T(8,128)}, u32[]{:S(2)}) copy-start(f32[1,2,256,256]{3,2,1,0:T(8,128)} %param.6) | copy-start | bytes 1572868
  117.2 1.6 %copy-start.3 = (f32[2,2,512,256]{3,2,1,0:T(8,128)S(1)}, f32[2,2,512,256]{3,2,1,0:T(8,128)}, u32[]{:S(2)}) copy-start(f32[2,2,512,256]{3,2,1,0:T(8,128)} %get-tuple-element.33.far_other_hbm) | copy-start | bytes 6291460
  125.8 11.3 %collective-permute-start.7 = (f32[16,2,8,512]{3,2,1,0:T(8,128)S(1)}, f32[16,2,8,512]{3,2,1,0:T(8,128)S(1)}, u32[]{:S(2)}, u32[]{:S(2)}) collective-permute-start(f32[16,2,8,512]{3,2,1,0:T(8,128)S(1)} %get-tuple-element.36), channel_id=1, source_target_pairs={{0,32},{1,33},{2,34},{3,35},{4,36},{5,37},{6,38},{7,39},{8,40},{9,... | collective-permute-start | bytes 1572872 | tf_op jit(solution)/shard_map/ppermute | solution.py:71
  138.0 13.7 %all-to-all-start.2 = ((f32[16,2,8,512]{3,2,1,0:T(8,128)}), f32[16,2,8,512]{3,2,1,0:T(8,128)S(1)}, u32[]{:S(2)}, u32[]{:S(2)}) async-start(f32[16,2,8,512]{3,2,1,0:T(8,128)} %add.30), calls=%async_computation.2 | async-start | bytes 1048576 | tf_op jit(solution)/shard_map/all_to_all | solution.py:490

commit v9 on v8

--- a/solution.py
+++ b/solution.py
@@ -360,7 +360,7 @@
 SMEM = pl.BlockSpec(memory_space=pltpu.SMEM)
 HBM = pl.BlockSpec(memory_space=pltpu.HBM)
 PAIRS = COUNT // 2
-ALL_VMEM, OTHER_VMEM, SOME_VMEM = 60, 52, 32
+ALL_VMEM, OTHER_VMEM, INVERSE_VMEM, SOME_VMEM = 60, 52, 46, 32
 FAR = (PAIRS, 2, 2 * SIDE, SIDE)
 SHARES = (PLANE_SIZE, COUNT, ROWS, SIDE)
 DMA = pltpu.SemaphoreType.DMA
@@ -409,9 +409,11 @@
         (flags, amplitude),
         SOME_VMEM,
     )
-    halo, measured, flags = lax.optimization_barrier((halo, measured, flags))
     piece = lax.dynamic_slice(probe, (core, quarter * QUARTER, 0), (1, QUARTER, SIDE))[0]
+    piece, measured = lax.optimization_barrier((piece, measured))
     first = moved(piece, across)
+    own = lax.dynamic_slice_in_dim(object_field, ((y * 2 + zhi) * 4 + x) * 8, 8, 1)
+    halo, measured, flags, own = lax.optimization_barrier((halo, measured, flags, own))
     far_own, intensity = call(
         own_kernel,
         "own",
@@ -484,11 +486,10 @@
             DMA((2, PAIRS)),
         ],
         (positions, flags, change, far_own, far_other, probe, probe_other, table),
-        SOME_VMEM,
+        INVERSE_VMEM,
     )
     gradient = upper + moved(lower, along_ring(1))
     total = jnp.sum(lax.all_to_all(gradient, PLANE, 0, 0), 0)
-    own = lax.dynamic_slice_in_dim(object_field, ((y * 2 + zhi) * 4 + x) * 8, 8, 1)
     return own + 0.5 * total / MODES
 
 

time: 154 us -> 149 us (0.968)
  starting transfers between devices: 63.5 us -> 58.7 us
  blocking collectives: 23.5 us -> 27.7 us
  waiting for transfers between devices: 34.7 us -> 31.9 us
  other arithmetic: 2.3 us -> 0.74 us
    all_to_all x0 -> x1, blocking collectives: none -> 13 us  [body(): total = jnp.sum(lax.all_to_all(gradient, PLANE, 0, 0), 0)]
    all_to_all x1 -> x0, waiting for transfers between devices: 8.87 us -> none  [body(): total = jnp.sum(lax.all_to_all(gradient, PLANE, 0, 0), 0)]
    all_to_all x1, blocking collectives: 23.5 us -> 14.7 us  [body(): change = lax.all_to_all(change, PLANE, 0, 0)]
    ppermute x8, waiting for transfers between devices: 25 us -> 31.1 us  [moved(): return lax.ppermute(value, AXES, pairs_of(move))]
    all_to_all x1 -> x0, starting transfers between devices: 4.82 us -> none  [body(): total = jnp.sum(lax.all_to_all(gradient, PLANE, 0, 0), 0)]
    unnamed x15 -> x13, local copies, waits for them, and re-layouts: 5.15 us -> 3.57 us
  transfers between devices with their start and end apart: 10 -> 9, of which waited for: 6 -> 5; matrix products, arithmetic and copies ran while one was open for 1% -> 2% of each run, Pallas kernels for 10% -> 11%
where the time goes in v9:
time: 149 us; the launch traced here: 148 us
  starting transfers between devices  58.7 us (39%)
  waiting for transfers between devices  31.9 us (21%)
  blocking collectives  27.7 us (19%)
  Pallas kernels  23.8 us (16%)
  local copies, waits for them, and re-layouts  5.26 us (4%)
    ppermute x8, starting transfers between devices, moved(): return lax.ppermute(value, AXES, pairs_of(move))  51.3 us
    ppermute x8, waiting for transfers between devices, moved(): return lax.ppermute(value, AXES, pairs_of(move))  31.1 us
    pallas_call x6, Pallas kernels, call(): pl.pallas_call(kernel, out_shape=[shape for shape, _ in outs], in_specs=i...  23.8 us
    all_to_all x1, blocking collectives, body(): change = lax.all_to_all(change, PLANE, 0, 0)  14.7 us
    all_to_all x1, blocking collectives, body(): total = jnp.sum(lax.all_to_all(gradient, PLANE, 0, 0), 0)  13 us
    all_to_all x1, starting transfers between devices, body(): shares = lax.all_to_all(intensity, PLANE, 0, 0)  7.49 us
    unnamed x13, local copies, waits for them, and re-layouts  3.57 us
  transfers between devices with their start and end apart: 9, of which 5 were waited for; matrix products, arithmetic and copies ran while one was open for 2% of the time, Pallas kernels for 11%

profile of v9, /device:TPU:2, one launch (start us, length us, event | category | flops | bytes accessed | tf_op | source)
XLA Modules:
  0.0 148.4 jit_solution(8478274306912728310)
XLA Ops:
  0.0 16.2 %collective-permute-start = (f32[2,256,512]{2,1,0:T(8,128)}, f32[2,256,512]{2,1,0:T(8,128)S(1)}, u32[]{:S(2)}, u32[]{:S(2)}) collective-permute-start(f32[2,256,512]{2,1,0:T(8,128)} %own_hbm.3), channel_id=1, source_target_pairs={{0,996},{1,997},{2,998},{3,999},{4,992},{5,993},{6,994},{7,995},{8... | collective-permute-start | bytes 3145736 | tf_op jit(solution)/shard_map/ppermute | solution.py:71
  16.2 0.1 stack.23.flags
  16.3 1.2 copy-done.3
  17.5 1.0 share.1.measured
  18.5 0.9 dynamic-slice_bitcast_fusion
  19.4 8.4 %collective-permute-start.1 = (f32[64,256]{1,0:T(8,128)S(1)}, f32[64,256]{1,0:T(8,128)S(1)}, u32[]{:S(2)}, u32[]{:S(2)}) collective-permute-start(f32[64,256]{1,0:T(8,128)S(1)} %dynamic-slice_bitcast_fusion), channel_id=1, source_target_pairs={{0,516},{1,517},{2,518},{3,519},{4,512},{5,513},{6,514},{7,515},{8... | collective-permute-start | bytes 196616 | tf_op jit(solution)/shard_map/ppermute | solution.py:71
  27.9 1.3 copy.8.pos
  29.2 0.8 constant_dynamic-slice_fusion
  30.0 9.4 %collective-permute-done.halo_hbm = f32[2,256,512]{2,1,0:T(8,128)S(1)} collective-permute-done((f32[2,256,512]{2,1,0:T(8,128)}, f32[2,256,512]{2,1,0:T(8,128)S(1)}, u32[]{:S(2)}, u32[]{:S(2)}) %collective-permute-start) | collective-permute-done | bytes 1048608 | tf_op jit(solution)/shard_map/ppermute | solution.py:71
  39.4 1.0 copy-done.5
  40.4 7.2 %own.1 = (f32[2,2,512,256]{3,2,1,0:T(8,128)}, f32[16,4,16,256]{3,2,1,0:T(8,128)}) custom-call(s32[4,2]{1,0:T(4,128)} %copy.8.pos, f32[2,256,512]{2,1,0:T(8,128)} %own_hbm.3, f32[2,256,512]{2,1,0:T(8,128)} %copy-done.5, f32[2,256,256]{2,1,0:T(8,128)} %bitcast.8, bf16[2,2,2,256,256]{4,3,2,1,0:T(8,128)(2,1)} %constant.51.clone.table_hbm), custom_call_target="tpu_custom_call" | custom-call | tf_op jit(solution)/shard_map/own/pallas_call | solution.py:381
  47.5 0.0 copy-start.4
  47.6 7.5 %all-to-all-start = ((f32[16,4,16,256]{3,2,1,0:T(8,128)}), f32[16,4,16,256]{3,2,1,0:T(8,128)S(1)}, u32[]{:S(2)}, u32[]{:S(2)}) async-start(f32[16,4,16,256]{3,2,1,0:T(8,128)} %get-tuple-element.30), calls=%async_computation | async-start | bytes 2097152 | tf_op jit(solution)/shard_map/all_to_all | solution.py:435
  55.0 1.9 %collective-permute-start.4 = (f32[64,256]{1,0:T(8,128)S(1)}, f32[64,256]{1,0:T(8,128)S(1)}, u32[]{:S(2)}, u32[]{:S(2)}) collective-permute-start(f32[64,256]{1,0:T(8,128)S(1)} %collective-permute-done.1.first), channel_id=1, source_target_pairs={{0,160},{1,161},{2,162},{3,163},{4,164},{5,165},{6,166},{7,167},{8... | collective-permute-start | bytes 196616 | tf_op jit(solution)/shard_map/ppermute | solution.py:71
  57.0 1.9 %collective-permute-start.3 = (f32[64,256]{1,0:T(8,128)S(1)}, f32[64,256]{1,0:T(8,128)S(1)}, u32[]{:S(2)}, u32[]{:S(2)}) collective-permute-start(f32[64,256]{1,0:T(8,128)S(1)} %collective-permute-done.1.first), channel_id=1, source_target_pairs={{0,32},{1,33},{2,34},{3,35},{4,36},{5,37},{6,38},{7,39},{8,40},{9,... | collective-permute-start | bytes 196616 | tf_op jit(solution)/shard_map/ppermute | solution.py:71
  58.9 4.9 %collective-permute-start.2 = (f32[64,256]{1,0:T(8,128)S(1)}, f32[64,256]{1,0:T(8,128)S(1)}, u32[]{:S(2)}, u32[]{:S(2)}) collective-permute-start(f32[64,256]{1,0:T(8,128)S(1)} %collective-permute-done.1.first), channel_id=1, source_target_pairs={{0,128},{1,129},{2,130},{3,131},{4,132},{5,133},{6,134},{7,135},{8... | collective-permute-start | bytes 196616 | tf_op jit(solution)/shard_map/ppermute | solution.py:71
  63.8 2.3 %collective-permute-done.2.second = f32[64,256]{1,0:T(8,128)S(1)} collective-permute-done((f32[64,256]{1,0:T(8,128)S(1)}, f32[64,256]{1,0:T(8,128)S(1)}, u32[]{:S(2)}, u32[]{:S(2)}) %collective-permute-start.2) | collective-permute-done | bytes 65568 | tf_op jit(solution)/shard_map/ppermute | solution.py:71
  66.2 0.8 all-to-all-done.shares
  67.0 0.1 collect.1
  67.0 1.9 %collective-permute-start.6 = (f32[2,2,64,256]{3,2,1,0:T(8,128)S(1)}, f32[2,2,64,256]{3,2,1,0:T(8,128)S(1)}, u32[]{:S(2)}, u32[]{:S(2)}) collective-permute-start(f32[2,2,64,256]{3,2,1,0:T(8,128)S(1)} %get-tuple-element.33.block), channel_id=1, source_target_pairs={{0,64},{1,65},{2,66},{3,67},{4,68},{5,69},{6,70},{7,71},{8,72},{9,... | collective-permute-start | bytes 786440 | tf_op jit(solution)/shard_map/ppermute | solution.py:71
  69.0 15.9 %collective-permute-start.5 = (f32[4,16,256]{2,1,0:T(8,128)S(1)}, f32[4,16,256]{2,1,0:T(8,128)S(1)}, u32[]{:S(2)}, u32[]{:S(2)}) collective-permute-start(f32[4,16,256]{2,1,0:T(8,128)S(1)} %get-tuple-element.32.summed), channel_id=1, source_target_pairs={{0,4},{1,5},{2,6},{3,7},{4,0},{5,1},{6,2},{7,3},{8,12},{9,13},{10,... | collective-permute-start | bytes 196616 | tf_op jit(solution)/shard_map/ppermute | solution.py:71
  84.9 7.5 %other.1 = (f32[2,2,512,256]{3,2,1,0:T(8,128)}, f32[2,256,256]{2,1,0:T(8,128)S(1)}) custom-call(s32[4,2]{1,0:T(4,128)S(1)} %copy-done.4, s32[5]{0:T(128)S(1)} %stack.23.flags, f32[2,256,512]{2,1,0:T(8,128)} %own_hbm.3, f32[2,256,512]{2,1,0:T(8,128)} %copy-done.5, bf16[2,2,2,256,256]{4,3,2,1,0:T(8,128)(2,1)} %constant.51.clone.table_hbm, ...), custom_call_target="tpu_custom_call" | custom-call | tf_op jit(solution)/shard_map/other/pallas_call | solution.py:381
  92.4 0.0 copy-start
  92.5 9.5 %collective-permute-done.5.arrived = f32[4,16,256]{2,1,0:T(8,128)S(1)} collective-permute-done((f32[4,16,256]{2,1,0:T(8,128)S(1)}, f32[4,16,256]{2,1,0:T(8,128)S(1)}, u32[]{:S(2)}, u32[]{:S(2)}) %collective-permute-start.5) | collective-permute-done | bytes 65568 | tf_op jit(solution)/shard_map/ppermute | solution.py:71
  102.0 0.1 change.1
  102.1 14.7 %all_to_all.15.change = f32[16,4,16,256]{3,2,1,0:T(8,128)S(1)} all-to-all(f32[16,4,16,256]{3,2,1,0:T(8,128)S(1)} %change.1), channel_id=1, replica_groups=mesh['zlo'=16,'core'=2,'y'=4,'zhi'=2,'x'=4] {'y','x'}, dimensions={0} | all-to-all | bytes 2097152 | tf_op jit(solution)/shard_map/all_to_all | solution.py:474
  116.8 7.9 %inverse.1 = (f32[16,2,8,512]{3,2,1,0:T(8,128)S(1)}, f32[16,2,8,512]{3,2,1,0:T(8,128)S(1)}) custom-call(s32[4,2]{1,0:T(4,128)S(1)} %copy-done.4, s32[5]{0:T(128)S(1)} %stack.23.flags, f32[16,4,16,256]{3,2,1,0:T(8,128)S(1)} %all_to_all.15.change, f32[2,2,512,256]{3,2,1,0:T(8,128)S(1)} %copy-done.2, f32[2,2,512,256]{3,2,1,0:T(8,128)} %get-tuple-element.39.far_other_hbm, ...), custom_call_target="tpu_custom_call" | custom-call | tf_op jit(solution)/shard_map/inverse/pallas_call | solution.py:381
  124.8 0.0 collective-permute-start.7
  124.8 9.8 %collective-permute-done.7 = f32[16,2,8,512]{3,2,1,0:T(8,128)S(1)} collective-permute-done((f32[16,2,8,512]{3,2,1,0:T(8,128)S(1)}, f32[16,2,8,512]{3,2,1,0:T(8,128)S(1)}, u32[]{:S(2)}, u32[]{:S(2)}) %collective-permute-start.7) | collective-permute-done | bytes 524320 | tf_op jit(solution)/shard_map/ppermute | solution.py:71
  134.6 0.1 add.30
  134.7 13.0 %all_to_all.16 = f32[16,2,8,512]{3,2,1,0:T(8,128)S(1)} all-to-all(f32[16,2,8,512]{3,2,1,0:T(8,128)S(1)} %add.30), channel_id=1, replica_groups=mesh['zlo'=16,'core'=2,'y'=4,'zhi'=2,'x'=4] {'y','x'}, dimensions={0} | all-to-all | bytes 1048576 | tf_op jit(solution)/shard_map/all_to_all | solution.py:492
  147.7 0.6 multiply_add_fusion
  (13 shorter events, 0.1 us)
Async XLA Ops:
  0.0 39.4 %collective-permute-start = (f32[2,256,512]{2,1,0:T(8,128)}, f32[2,256,512]{2,1,0:T(8,128)S(1)}, u32[]{:S(2)}, u32[]{:S(2)}) collective-permute-start(f32[2,256,512]{2,1,0:T(8,128)} %own_hbm.3), channel_id=1, source_target_pairs={{0,996},{1,997},{2,998},{3,999},{4,992},{5,993},{6,994},{7,995},{8... | collective-permute-start | bytes 3145736 | tf_op jit(solution)/shard_map/ppermute | solution.py:71
  16.3 1.2 copy-start.3
  19.4 28.1 %collective-permute-start.1 = (f32[64,256]{1,0:T(8,128)S(1)}, f32[64,256]{1,0:T(8,128)S(1)}, u32[]{:S(2)}, u32[]{:S(2)}) collective-permute-start(f32[64,256]{1,0:T(8,128)S(1)} %dynamic-slice_bitcast_fusion), channel_id=1, source_target_pairs={{0,516},{1,517},{2,518},{3,519},{4,512},{5,513},{6,514},{7,515},{8... | collective-permute-start | bytes 196616 | tf_op jit(solution)/shard_map/ppermute | solution.py:71
  39.4 1.0 copy-start.5
  47.5 37.4 %copy-start.4 = (s32[4,2]{1,0:T(4,128)S(1)}, s32[4,2]{1,0:T(4,128)}, u32[]{:S(2)}) copy-start(s32[4,2]{1,0:T(4,128)} %copy.8.pos) | copy-start | bytes 100
  47.6 19.4 %all-to-all-start = ((f32[16,4,16,256]{3,2,1,0:T(8,128)}), f32[16,4,16,256]{3,2,1,0:T(8,128)S(1)}, u32[]{:S(2)}, u32[]{:S(2)}) async-start(f32[16,4,16,256]{3,2,1,0:T(8,128)} %get-tuple-element.30), calls=%async_computation | async-start | bytes 2097152 | tf_op jit(solution)/shard_map/all_to_all | solution.py:435
  55.0 8.8 %collective-permute-start.4 = (f32[64,256]{1,0:T(8,128)S(1)}, f32[64,256]{1,0:T(8,128)S(1)}, u32[]{:S(2)}, u32[]{:S(2)}) collective-permute-start(f32[64,256]{1,0:T(8,128)S(1)} %collective-permute-done.1.first), channel_id=1, source_target_pairs={{0,160},{1,161},{2,162},{3,163},{4,164},{5,165},{6,166},{7,167},{8... | collective-permute-start | bytes 196616 | tf_op jit(solution)/shard_map/ppermute | solution.py:71
  57.0 6.9 %collective-permute-start.3 = (f32[64,256]{1,0:T(8,128)S(1)}, f32[64,256]{1,0:T(8,128)S(1)}, u32[]{:S(2)}, u32[]{:S(2)}) collective-permute-start(f32[64,256]{1,0:T(8,128)S(1)} %collective-permute-done.1.first), channel_id=1, source_target_pairs={{0,32},{1,33},{2,34},{3,35},{4,36},{5,37},{6,38},{7,39},{8,40},{9,... | collective-permute-start | bytes 196616 | tf_op jit(solution)/shard_map/ppermute | solution.py:71
  58.9 7.3 %collective-permute-start.2 = (f32[64,256]{1,0:T(8,128)S(1)}, f32[64,256]{1,0:T(8,128)S(1)}, u32[]{:S(2)}, u32[]{:S(2)}) collective-permute-start(f32[64,256]{1,0:T(8,128)S(1)} %collective-permute-done.1.first), channel_id=1, source_target_pairs={{0,128},{1,129},{2,130},{3,131},{4,132},{5,133},{6,134},{7,135},{8... | collective-permute-start | bytes 196616 | tf_op jit(solution)/shard_map/ppermute | solution.py:71
  67.0 17.9 %collective-permute-start.6 = (f32[2,2,64,256]{3,2,1,0:T(8,128)S(1)}, f32[2,2,64,256]{3,2,1,0:T(8,128)S(1)}, u32[]{:S(2)}, u32[]{:S(2)}) collective-permute-start(f32[2,2,64,256]{3,2,1,0:T(8,128)S(1)} %get-tuple-element.33.block), channel_id=1, source_target_pairs={{0,64},{1,65},{2,66},{3,67},{4,68},{5,69},{6,70},{7,71},{8,72},{9,... | collective-permute-start | bytes 786440 | tf_op jit(solution)/shard_map/ppermute | solution.py:71
  69.0 33.0 %collective-permute-start.5 = (f32[4,16,256]{2,1,0:T(8,128)S(1)}, f32[4,16,256]{2,1,0:T(8,128)S(1)}, u32[]{:S(2)}, u32[]{:S(2)}) collective-permute-start(f32[4,16,256]{2,1,0:T(8,128)S(1)} %get-tuple-element.32.summed), channel_id=1, source_target_pairs={{0,4},{1,5},{2,6},{3,7},{4,0},{5,1},{6,2},{7,3},{8,12},{9,13},{10,... | collective-permute-start | bytes 196616 | tf_op jit(solution)/shard_map/ppermute | solution.py:71
  84.9 31.9 %copy-start.2 = (f32[2,2,512,256]{3,2,1,0:T(8,128)S(1)}, f32[2,2,512,256]{3,2,1,0:T(8,128)}, u32[]{:S(2)}) copy-start(f32[2,2,512,256]{3,2,1,0:T(8,128)} %get-tuple-element.38.far_own_hbm) | copy-start | bytes 6291460
  92.4 24.4 %copy-start = (bf16[2,2,2,256,256]{4,3,2,1,0:T(8,128)(2,1)S(1)}, bf16[2,2,2,256,256]{4,3,2,1,0:T(8,128)(2,1)}, u32[]{:S(2)}) copy-start(bf16[2,2,2,256,256]{4,3,2,1,0:T(8,128)(2,1)} %constant.51.clone.table_hbm) | copy-start | bytes 3145732
  92.4 24.4 %copy-start.1 = (f32[1,2,256,256]{3,2,1,0:T(8,128)S(1)}, f32[1,2,256,256]{3,2,1,0:T(8,128)}, u32[]{:S(2)}) copy-start(f32[1,2,256,256]{3,2,1,0:T(8,128)} %param.6) | copy-start | bytes 1572868
  124.8 9.8 %collective-permute-start.7 = (f32[16,2,8,512]{3,2,1,0:T(8,128)S(1)}, f32[16,2,8,512]{3,2,1,0:T(8,128)S(1)}, u32[]{:S(2)}, u32[]{:S(2)}) collective-permute-start(f32[16,2,8,512]{3,2,1,0:T(8,128)S(1)} %get-tuple-element.42), channel_id=1, source_target_pairs={{0,32},{1,33},{2,34},{3,35},{4,36},{5,37},{6,38},{7,39},{8,40},{9,... | collective-permute-start | bytes 1572872 | tf_op jit(solution)/shard_map/ppermute | solution.py:71

commit v10 on v9

--- a/solution.py
+++ b/solution.py
@@ -201,16 +201,17 @@
 
 
 def own_kernel(
-    pos, own_hbm, halo_hbm, probe_hbm, table_hbm,
+    pos, halo, own_hbm, probe_hbm, table_hbm,
     far_hbm, intensity_hbm, ext, probe, table, far, intensity, sems, out_sems,
 ):
     pairs = (
         (own_hbm, ext.at[:, pl.ds(0, SIDE)]),
-        (halo_hbm, ext.at[:, pl.ds(SIDE, SIDE)]),
         (probe_hbm, probe),
         (table_hbm, table),
     )
-    for copy in started(pairs, sems):
+    copies = started(pairs, sems)
+    ext[:, SIDE:] = halo[...]
+    for copy in copies:
         copy.wait()
 
     def out_copies(q):
@@ -360,7 +361,7 @@
 SMEM = pl.BlockSpec(memory_space=pltpu.SMEM)
 HBM = pl.BlockSpec(memory_space=pltpu.HBM)
 PAIRS = COUNT // 2
-ALL_VMEM, OTHER_VMEM, INVERSE_VMEM, SOME_VMEM = 60, 52, 46, 32
+ALL_VMEM, OTHER_VMEM, INVERSE_VMEM, SOME_VMEM = 50, 52, 46, 32
 FAR = (PAIRS, 2, 2 * SIDE, SIDE)
 SHARES = (PLANE_SIZE, COUNT, ROWS, SIDE)
 DMA = pltpu.SemaphoreType.DMA
@@ -417,7 +418,7 @@
     far_own, intensity = call(
         own_kernel,
         "own",
-        [SMEM] + [HBM] * 4,
+        [SMEM, VMEM] + [HBM] * 3,
         [(floats(*FAR), HBM), (floats(*SHARES), HBM)],
         [
             scratch(2, WIDTH, WIDTH),
@@ -425,10 +426,10 @@
             TABLE,
             scratch(*FAR),
             scratch(*SHARES),
-            DMA((4,)),
+            DMA((3,)),
             DMA((2, PAIRS)),
         ],
-        (positions, object_field, halo, probe, table),
+        (positions, halo, object_field, probe, table),
         ALL_VMEM,
     )
     intensity, first = lax.optimization_barrier((intensity, first))

time: 149 us -> 150 us (level)
  the two profiles are of different devices: /device:TPU:2 before, /device:TPU:1 now
where the time goes in v10:
time: 150 us; the launch traced here: 149 us
  starting transfers between devices  75.7 us (50%)
  blocking collectives  33.5 us (22%)
  Pallas kernels  23 us (15%)
  waiting for transfers between devices  10.7 us (7%)
  local copies, waits for them, and re-layouts  5.13 us (3%)
    ppermute x8, starting transfers between devices, moved(): return lax.ppermute(value, AXES, pairs_of(move))  68.9 us
    pallas_call x6, Pallas kernels, call(): pl.pallas_call(kernel, out_shape=[shape for shape, _ in outs], in_specs=i...  23 us
    all_to_all x1, blocking collectives, body(): change = lax.all_to_all(change, PLANE, 0, 0)  19.8 us
    all_to_all x1, blocking collectives, body(): total = jnp.sum(lax.all_to_all(gradient, PLANE, 0, 0), 0)  13.7 us
    ppermute x8, waiting for transfers between devices, moved(): return lax.ppermute(value, AXES, pairs_of(move))  10.7 us
    all_to_all x1, starting transfers between devices, body(): shares = lax.all_to_all(intensity, PLANE, 0, 0)  6.76 us
    unnamed x15, local copies, waits for them, and re-layouts  3.43 us
  transfers between devices with their start and end apart: 9, of which 3 were waited for; matrix products, arithmetic and copies ran while one was open for 2% of the time, Pallas kernels for 10%

profile of v10, /device:TPU:1, one launch (start us, length us, event | category | flops | bytes accessed | tf_op | source)
XLA Modules:
  0.0 148.9 jit_solution(9077315896474280997)
XLA Ops:
  0.0 14.2 %collective-permute-start = (f32[2,256,512]{2,1,0:T(8,128)}, f32[2,256,512]{2,1,0:T(8,128)S(1)}, u32[]{:S(2)}, u32[]{:S(2)}) collective-permute-start(f32[2,256,512]{2,1,0:T(8,128)} %own_hbm.3), channel_id=1, source_target_pairs={{0,996},{1,997},{2,998},{3,999},{4,992},{5,993},{6,994},{7,995},{8... | collective-permute-start | bytes 3145736 | tf_op jit(solution)/shard_map/ppermute | solution.py:71
  14.2 0.1 stack.23.flags
  14.2 1.2 copy-done.6
  15.5 1.0 share.1.measured
  16.5 0.9 dynamic-slice_bitcast_fusion
  17.3 10.1 %collective-permute-start.1 = (f32[64,256]{1,0:T(8,128)S(1)}, f32[64,256]{1,0:T(8,128)S(1)}, u32[]{:S(2)}, u32[]{:S(2)}) collective-permute-start(f32[64,256]{1,0:T(8,128)S(1)} %dynamic-slice_bitcast_fusion), channel_id=1, source_target_pairs={{0,516},{1,517},{2,518},{3,519},{4,512},{5,513},{6,514},{7,515},{8... | collective-permute-start | bytes 196616 | tf_op jit(solution)/shard_map/ppermute | solution.py:71
  27.4 0.8 copy.8.pos
  28.2 0.8 constant_dynamic-slice_fusion
  29.0 0.0 collective-permute-done.halo.halo_hbm
  29.0 0.0 copy-start.3
  29.0 1.4 copy-done.3
  30.4 6.3 %own.1 = (f32[2,2,512,256]{3,2,1,0:T(8,128)}, f32[16,4,16,256]{3,2,1,0:T(8,128)}) custom-call(s32[4,2]{1,0:T(4,128)S(1)} %copy.8.pos, f32[2,256,512]{2,1,0:T(8,128)S(1)} %collective-permute-done.halo.halo_hbm, f32[2,256,512]{2,1,0:T(8,128)S(1)} %copy-done.1, f32[2,256,256]{2,1,0:T(8,128)S(1)} %bitcast.8, bf16[2,2,2,256,256]{4,3,2,1,0:T(8,128)(2,1)} %constant.51.clone.table_hbm), custom_call_target="tpu_custom_call" | custom-call | tf_op jit(solution)/shard_map/own/pallas_call | solution.py:382
  36.7 2.3 %collective-permute-done.1.first = f32[64,256]{1,0:T(8,128)S(1)} collective-permute-done((f32[64,256]{1,0:T(8,128)S(1)}, f32[64,256]{1,0:T(8,128)S(1)}, u32[]{:S(2)}, u32[]{:S(2)}) %collective-permute-start.1) | collective-permute-done | bytes 65568 | tf_op jit(solution)/shard_map/ppermute | solution.py:71
  39.1 6.8 %all-to-all-start = ((f32[16,4,16,256]{3,2,1,0:T(8,128)}), f32[16,4,16,256]{3,2,1,0:T(8,128)S(1)}, u32[]{:S(2)}, u32[]{:S(2)}) async-start(f32[16,4,16,256]{3,2,1,0:T(8,128)} %get-tuple-element.30), calls=%async_computation | async-start | bytes 2097152 | tf_op jit(solution)/shard_map/all_to_all | solution.py:436
  45.8 1.9 %collective-permute-start.4 = (f32[64,256]{1,0:T(8,128)S(1)}, f32[64,256]{1,0:T(8,128)S(1)}, u32[]{:S(2)}, u32[]{:S(2)}) collective-permute-start(f32[64,256]{1,0:T(8,128)S(1)} %collective-permute-done.1.first), channel_id=1, source_target_pairs={{0,160},{1,161},{2,162},{3,163},{4,164},{5,165},{6,166},{7,167},{8... | collective-permute-start | bytes 196616 | tf_op jit(solution)/shard_map/ppermute | solution.py:71
  47.7 11.8 %collective-permute-start.3 = (f32[64,256]{1,0:T(8,128)S(1)}, f32[64,256]{1,0:T(8,128)S(1)}, u32[]{:S(2)}, u32[]{:S(2)}) collective-permute-start(f32[64,256]{1,0:T(8,128)S(1)} %collective-permute-done.1.first), channel_id=1, source_target_pairs={{0,32},{1,33},{2,34},{3,35},{4,36},{5,37},{6,38},{7,39},{8,40},{9,... | collective-permute-start | bytes 196616 | tf_op jit(solution)/shard_map/ppermute | solution.py:71
  59.5 4.2 %collective-permute-start.2 = (f32[64,256]{1,0:T(8,128)S(1)}, f32[64,256]{1,0:T(8,128)S(1)}, u32[]{:S(2)}, u32[]{:S(2)}) collective-permute-start(f32[64,256]{1,0:T(8,128)S(1)} %collective-permute-done.1.first), channel_id=1, source_target_pairs={{0,128},{1,129},{2,130},{3,131},{4,132},{5,133},{6,134},{7,135},{8... | collective-permute-start | bytes 196616 | tf_op jit(solution)/shard_map/ppermute | solution.py:71
  63.7 2.2 %collective-permute-done.2.second = f32[64,256]{1,0:T(8,128)S(1)} collective-permute-done((f32[64,256]{1,0:T(8,128)S(1)}, f32[64,256]{1,0:T(8,128)S(1)}, u32[]{:S(2)}, u32[]{:S(2)}) %collective-permute-start.2) | collective-permute-done | bytes 65568 | tf_op jit(solution)/shard_map/ppermute | solution.py:71
  65.9 0.1 collect.1
  66.0 1.9 %collective-permute-start.6 = (f32[2,2,64,256]{3,2,1,0:T(8,128)S(1)}, f32[2,2,64,256]{3,2,1,0:T(8,128)S(1)}, u32[]{:S(2)}, u32[]{:S(2)}) collective-permute-start(f32[2,2,64,256]{3,2,1,0:T(8,128)S(1)} %get-tuple-element.33.block), channel_id=1, source_target_pairs={{0,64},{1,65},{2,66},{3,67},{4,68},{5,69},{6,70},{7,71},{8,72},{9,... | collective-permute-start | bytes 786440 | tf_op jit(solution)/shard_map/ppermute | solution.py:71
  67.9 18.4 %collective-permute-start.5 = (f32[4,16,256]{2,1,0:T(8,128)S(1)}, f32[4,16,256]{2,1,0:T(8,128)S(1)}, u32[]{:S(2)}, u32[]{:S(2)}) collective-permute-start(f32[4,16,256]{2,1,0:T(8,128)S(1)} %get-tuple-element.32.summed), channel_id=1, source_target_pairs={{0,4},{1,5},{2,6},{3,7},{4,0},{5,1},{6,2},{7,3},{8,12},{9,13},{10,... | collective-permute-start | bytes 196616 | tf_op jit(solution)/shard_map/ppermute | solution.py:71
  86.4 7.5 %other.1 = (f32[2,2,512,256]{3,2,1,0:T(8,128)}, f32[2,256,256]{2,1,0:T(8,128)S(1)}) custom-call(s32[4,2]{1,0:T(4,128)S(1)} %copy.8.pos, s32[5]{0:T(128)S(1)} %stack.23.flags, f32[2,256,512]{2,1,0:T(8,128)} %own_hbm.3, f32[2,256,512]{2,1,0:T(8,128)} %copy-done.2, bf16[2,2,2,256,256]{4,3,2,1,0:T(8,128)(2,1)} %constant.51.clone.table_hbm, ...), custom_call_target="tpu_custom_call" | custom-call | tf_op jit(solution)/shard_map/other/pallas_call | solution.py:382
  93.9 0.0 copy-start
  93.9 0.0 copy-start.4
  93.9 0.1 change.1
  94.0 19.8 %all_to_all.15.change = f32[16,4,16,256]{3,2,1,0:T(8,128)S(1)} all-to-all(f32[16,4,16,256]{3,2,1,0:T(8,128)S(1)} %change.1), channel_id=1, replica_groups=mesh['zlo'=16,'core'=2,'y'=4,'zhi'=2,'x'=4] {'y','x'}, dimensions={0} | all-to-all | bytes 2097152 | tf_op jit(solution)/shard_map/all_to_all | solution.py:475
  113.8 8.0 %inverse.1 = (f32[16,2,8,512]{3,2,1,0:T(8,128)S(1)}, f32[16,2,8,512]{3,2,1,0:T(8,128)S(1)}) custom-call(s32[4,2]{1,0:T(4,128)S(1)} %copy.8.pos, s32[5]{0:T(128)S(1)} %stack.23.flags, f32[16,4,16,256]{3,2,1,0:T(8,128)S(1)} %all_to_all.15.change, f32[2,2,512,256]{3,2,1,0:T(8,128)S(1)} %copy-done.5, f32[2,2,512,256]{3,2,1,0:T(8,128)} %get-tuple-element.39.far_other_hbm, ...), custom_call_target="tpu_custom_call" | custom-call | tf_op jit(solution)/shard_map/inverse/pallas_call | solution.py:382
  121.8 6.5 %collective-permute-start.7 = (f32[16,2,8,512]{3,2,1,0:T(8,128)S(1)}, f32[16,2,8,512]{3,2,1,0:T(8,128)S(1)}, u32[]{:S(2)}, u32[]{:S(2)}) collective-permute-start(f32[16,2,8,512]{3,2,1,0:T(8,128)S(1)} %get-tuple-element.42), channel_id=1, source_target_pairs={{0,32},{1,33},{2,34},{3,35},{4,36},{5,37},{6,38},{7,39},{8,40},{9,... | collective-permute-start | bytes 1572872 | tf_op jit(solution)/shard_map/ppermute | solution.py:71
  128.3 6.1 %collective-permute-done.7 = f32[16,2,8,512]{3,2,1,0:T(8,128)S(1)} collective-permute-done((f32[16,2,8,512]{3,2,1,0:T(8,128)S(1)}, f32[16,2,8,512]{3,2,1,0:T(8,128)S(1)}, u32[]{:S(2)}, u32[]{:S(2)}) %collective-permute-start.7) | collective-permute-done | bytes 524320 | tf_op jit(solution)/shard_map/ppermute | solution.py:71
  134.5 0.1 add.30
  134.6 13.7 %all_to_all.16 = f32[16,2,8,512]{3,2,1,0:T(8,128)S(1)} all-to-all(f32[16,2,8,512]{3,2,1,0:T(8,128)S(1)} %add.30), channel_id=1, replica_groups=mesh['zlo'=16,'core'=2,'y'=4,'zhi'=2,'x'=4] {'y','x'}, dimensions={0} | all-to-all | bytes 1048576 | tf_op jit(solution)/shard_map/all_to_all | solution.py:493
  148.3 0.6 multiply_add_fusion
  (15 shorter events, 0.1 us)
Async XLA Ops:
  0.0 29.0 %copy-start.1 = (f32[2,256,512]{2,1,0:T(8,128)S(1)}, f32[2,256,512]{2,1,0:T(8,128)}, u32[]{:S(2)}) copy-start(f32[2,256,512]{2,1,0:T(8,128)} %own_hbm.3) | copy-start | bytes 3145732
  0.0 29.0 %collective-permute-start = (f32[2,256,512]{2,1,0:T(8,128)}, f32[2,256,512]{2,1,0:T(8,128)S(1)}, u32[]{:S(2)}, u32[]{:S(2)}) collective-permute-start(f32[2,256,512]{2,1,0:T(8,128)} %own_hbm.3), channel_id=1, source_target_pairs={{0,996},{1,997},{2,998},{3,999},{4,992},{5,993},{6,994},{7,995},{8... | collective-permute-start | bytes 3145736 | tf_op jit(solution)/shard_map/ppermute | solution.py:71
  14.2 1.2 copy-start.6
  17.3 21.7 %collective-permute-start.1 = (f32[64,256]{1,0:T(8,128)S(1)}, f32[64,256]{1,0:T(8,128)S(1)}, u32[]{:S(2)}, u32[]{:S(2)}) collective-permute-start(f32[64,256]{1,0:T(8,128)S(1)} %dynamic-slice_bitcast_fusion), channel_id=1, source_target_pairs={{0,516},{1,517},{2,518},{3,519},{4,512},{5,513},{6,514},{7,515},{8... | collective-permute-start | bytes 196616 | tf_op jit(solution)/shard_map/ppermute | solution.py:71
  29.0 10.1 %copy-start.2 = (f32[2,256,512]{2,1,0:T(8,128)}, f32[2,256,512]{2,1,0:T(8,128)S(1)}, u32[]{:S(2)}) copy-start(f32[2,256,512]{2,1,0:T(8,128)S(1)} %collective-permute-done.halo.halo_hbm) | copy-start | bytes 3145732
  29.0 1.4 copy-start.3
  39.1 26.9 %all-to-all-start = ((f32[16,4,16,256]{3,2,1,0:T(8,128)}), f32[16,4,16,256]{3,2,1,0:T(8,128)S(1)}, u32[]{:S(2)}, u32[]{:S(2)}) async-start(f32[16,4,16,256]{3,2,1,0:T(8,128)} %get-tuple-element.30), calls=%async_computation | async-start | bytes 2097152 | tf_op jit(solution)/shard_map/all_to_all | solution.py:436
  45.8 17.9 %collective-permute-start.4 = (f32[64,256]{1,0:T(8,128)S(1)}, f32[64,256]{1,0:T(8,128)S(1)}, u32[]{:S(2)}, u32[]{:S(2)}) collective-permute-start(f32[64,256]{1,0:T(8,128)S(1)} %collective-permute-done.1.first), channel_id=1, source_target_pairs={{0,160},{1,161},{2,162},{3,163},{4,164},{5,165},{6,166},{7,167},{8... | collective-permute-start | bytes 196616 | tf_op jit(solution)/shard_map/ppermute | solution.py:71
  47.7 16.0 %collective-permute-start.3 = (f32[64,256]{1,0:T(8,128)S(1)}, f32[64,256]{1,0:T(8,128)S(1)}, u32[]{:S(2)}, u32[]{:S(2)}) collective-permute-start(f32[64,256]{1,0:T(8,128)S(1)} %collective-permute-done.1.first), channel_id=1, source_target_pairs={{0,32},{1,33},{2,34},{3,35},{4,36},{5,37},{6,38},{7,39},{8,40},{9,... | collective-permute-start | bytes 196616 | tf_op jit(solution)/shard_map/ppermute | solution.py:71
  59.5 6.4 %collective-permute-start.2 = (f32[64,256]{1,0:T(8,128)S(1)}, f32[64,256]{1,0:T(8,128)S(1)}, u32[]{:S(2)}, u32[]{:S(2)}) collective-permute-start(f32[64,256]{1,0:T(8,128)S(1)} %collective-permute-done.1.first), channel_id=1, source_target_pairs={{0,128},{1,129},{2,130},{3,131},{4,132},{5,133},{6,134},{7,135},{8... | collective-permute-start | bytes 196616 | tf_op jit(solution)/shard_map/ppermute | solution.py:71
  66.0 20.4 %collective-permute-start.6 = (f32[2,2,64,256]{3,2,1,0:T(8,128)S(1)}, f32[2,2,64,256]{3,2,1,0:T(8,128)S(1)}, u32[]{:S(2)}, u32[]{:S(2)}) collective-permute-start(f32[2,2,64,256]{3,2,1,0:T(8,128)S(1)} %get-tuple-element.33.block), channel_id=1, source_target_pairs={{0,64},{1,65},{2,66},{3,67},{4,68},{5,69},{6,70},{7,71},{8,72},{9,... | collective-permute-start | bytes 786440 | tf_op jit(solution)/shard_map/ppermute | solution.py:71
  67.9 26.0 %collective-permute-start.5 = (f32[4,16,256]{2,1,0:T(8,128)S(1)}, f32[4,16,256]{2,1,0:T(8,128)S(1)}, u32[]{:S(2)}, u32[]{:S(2)}) collective-permute-start(f32[4,16,256]{2,1,0:T(8,128)S(1)} %get-tuple-element.32.summed), channel_id=1, source_target_pairs={{0,4},{1,5},{2,6},{3,7},{4,0},{5,1},{6,2},{7,3},{8,12},{9,13},{10,... | collective-permute-start | bytes 196616 | tf_op jit(solution)/shard_map/ppermute | solution.py:71
  86.4 27.5 %copy-start.5 = (f32[2,2,512,256]{3,2,1,0:T(8,128)S(1)}, f32[2,2,512,256]{3,2,1,0:T(8,128)}, u32[]{:S(2)}) copy-start(f32[2,2,512,256]{3,2,1,0:T(8,128)} %get-tuple-element.38.far_own_hbm) | copy-start | bytes 6291460
  93.9 20.0 %copy-start = (bf16[2,2,2,256,256]{4,3,2,1,0:T(8,128)(2,1)S(1)}, bf16[2,2,2,256,256]{4,3,2,1,0:T(8,128)(2,1)}, u32[]{:S(2)}) copy-start(bf16[2,2,2,256,256]{4,3,2,1,0:T(8,128)(2,1)} %constant.51.clone.table_hbm) | copy-start | bytes 3145732
  93.9 19.9 %copy-start.4 = (f32[1,2,256,256]{3,2,1,0:T(8,128)S(1)}, f32[1,2,256,256]{3,2,1,0:T(8,128)}, u32[]{:S(2)}) copy-start(f32[1,2,256,256]{3,2,1,0:T(8,128)} %param.6) | copy-start | bytes 1572868
  121.8 12.6 %collective-permute-start.7 = (f32[16,2,8,512]{3,2,1,0:T(8,128)S(1)}, f32[16,2,8,512]{3,2,1,0:T(8,128)S(1)}, u32[]{:S(2)}, u32[]{:S(2)}) collective-permute-start(f32[16,2,8,512]{3,2,1,0:T(8,128)S(1)} %get-tuple-element.42), channel_id=1, source_target_pairs={{0,32},{1,33},{2,34},{3,35},{4,36},{5,37},{6,38},{7,39},{8,40},{9,... | collective-permute-start | bytes 1572872 | tf_op jit(solution)/shard_map/ppermute | solution.py:71

commit v11 on v10

--- a/solution.py
+++ b/solution.py
@@ -411,7 +411,6 @@
         SOME_VMEM,
     )
     piece = lax.dynamic_slice(probe, (core, quarter * QUARTER, 0), (1, QUARTER, SIDE))[0]
-    piece, measured = lax.optimization_barrier((piece, measured))
     first = moved(piece, across)
     own = lax.dynamic_slice_in_dim(object_field, ((y * 2 + zhi) * 4 + x) * 8, 8, 1)
     halo, measured, flags, own = lax.optimization_barrier((halo, measured, flags, own))

time: 150 us -> 150 us (level)
  the two profiles are of different devices: /device:TPU:1 before, /device:TPU:2 now
where the time goes in v11:
time: 150 us; the launch traced here: 149 us
  starting transfers between devices  58.7 us (39%)
  blocking collectives  36.9 us (25%)
  waiting for transfers between devices  24.1 us (16%)
  Pallas kernels  23 us (15%)
  local copies, waits for them, and re-layouts  5.11 us (3%)
    ppermute x8, starting transfers between devices, moved(): return lax.ppermute(value, AXES, pairs_of(move))  51.2 us
    all_to_all x1, blocking collectives, body(): change = lax.all_to_all(change, PLANE, 0, 0)  23.9 us
    ppermute x8, waiting for transfers between devices, moved(): return lax.ppermute(value, AXES, pairs_of(move))  23.3 us
    pallas_call x6, Pallas kernels, call(): pl.pallas_call(kernel, out_shape=[shape for shape, _ in outs], in_specs=i...  23 us
    all_to_all x1, blocking collectives, body(): total = jnp.sum(lax.all_to_all(gradient, PLANE, 0, 0), 0)  13 us
    all_to_all x1, starting transfers between devices, body(): shares = lax.all_to_all(intensity, PLANE, 0, 0)  7.49 us
    unnamed x15, local copies, waits for them, and re-layouts  3.41 us
  transfers between devices with their start and end apart: 9, of which 5 were waited for; matrix products, arithmetic and copies ran while one was open for 2% of the time, Pallas kernels for 10%

profile of v11, /device:TPU:2, one launch (start us, length us, event | category | flops | bytes accessed | tf_op | source)
XLA Modules:
  0.0 148.8 jit_solution(1319154742220701857)
XLA Ops:
  0.0 16.2 %collective-permute-start = (f32[2,256,512]{2,1,0:T(8,128)}, f32[2,256,512]{2,1,0:T(8,128)S(1)}, u32[]{:S(2)}, u32[]{:S(2)}) collective-permute-start(f32[2,256,512]{2,1,0:T(8,128)} %own_hbm.3), channel_id=1, source_target_pairs={{0,996},{1,997},{2,998},{3,999},{4,992},{5,993},{6,994},{7,995},{8... | collective-permute-start | bytes 3145736 | tf_op jit(solution)/shard_map/ppermute | solution.py:71
  16.2 0.8 dynamic-slice_bitcast_fusion
  17.1 8.4 %collective-permute-start.1 = (f32[64,256]{1,0:T(8,128)S(1)}, f32[64,256]{1,0:T(8,128)S(1)}, u32[]{:S(2)}, u32[]{:S(2)}) collective-permute-start(f32[64,256]{1,0:T(8,128)S(1)} %dynamic-slice_bitcast_fusion), channel_id=1, source_target_pairs={{0,516},{1,517},{2,518},{3,519},{4,512},{5,513},{6,514},{7,515},{8... | collective-permute-start | bytes 196616 | tf_op jit(solution)/shard_map/ppermute | solution.py:71
  25.5 0.8 copy.8.pos
  26.3 0.1 stack.23.flags
  26.4 1.2 copy-done.6
  27.6 1.0 share.1.measured
  28.6 0.8 constant_dynamic-slice_fusion
  29.4 10.0 %collective-permute-done.halo.halo_hbm = f32[2,256,512]{2,1,0:T(8,128)S(1)} collective-permute-done((f32[2,256,512]{2,1,0:T(8,128)}, f32[2,256,512]{2,1,0:T(8,128)S(1)}, u32[]{:S(2)}, u32[]{:S(2)}) %collective-permute-start) | collective-permute-done | bytes 1048608 | tf_op jit(solution)/shard_map/ppermute | solution.py:71
  39.4 1.4 copy-done.3
  40.8 6.3 %own.1 = (f32[2,2,512,256]{3,2,1,0:T(8,128)}, f32[16,4,16,256]{3,2,1,0:T(8,128)}) custom-call(s32[4,2]{1,0:T(4,128)S(1)} %copy.8.pos, f32[2,256,512]{2,1,0:T(8,128)S(1)} %collective-permute-done.halo.halo_hbm, f32[2,256,512]{2,1,0:T(8,128)S(1)} %copy-done.1, f32[2,256,256]{2,1,0:T(8,128)S(1)} %bitcast.8, bf16[2,2,2,256,256]{4,3,2,1,0:T(8,128)(2,1)} %constant.51.clone.table_hbm), custom_call_target="tpu_custom_call" | custom-call | tf_op jit(solution)/shard_map/own/pallas_call | solution.py:382
  47.2 7.5 %all-to-all-start = ((f32[16,4,16,256]{3,2,1,0:T(8,128)}), f32[16,4,16,256]{3,2,1,0:T(8,128)S(1)}, u32[]{:S(2)}, u32[]{:S(2)}) async-start(f32[16,4,16,256]{3,2,1,0:T(8,128)} %get-tuple-element.26), calls=%async_computation | async-start | bytes 2097152 | tf_op jit(solution)/shard_map/all_to_all | solution.py:435
  54.7 1.9 %collective-permute-start.4 = (f32[64,256]{1,0:T(8,128)S(1)}, f32[64,256]{1,0:T(8,128)S(1)}, u32[]{:S(2)}, u32[]{:S(2)}) collective-permute-start(f32[64,256]{1,0:T(8,128)S(1)} %collective-permute-done.1.first), channel_id=1, source_target_pairs={{0,160},{1,161},{2,162},{3,163},{4,164},{5,165},{6,166},{7,167},{8... | collective-permute-start | bytes 196616 | tf_op jit(solution)/shard_map/ppermute | solution.py:71
  56.6 1.9 %collective-permute-start.3 = (f32[64,256]{1,0:T(8,128)S(1)}, f32[64,256]{1,0:T(8,128)S(1)}, u32[]{:S(2)}, u32[]{:S(2)}) collective-permute-start(f32[64,256]{1,0:T(8,128)S(1)} %collective-permute-done.1.first), channel_id=1, source_target_pairs={{0,32},{1,33},{2,34},{3,35},{4,36},{5,37},{6,38},{7,39},{8,40},{9,... | collective-permute-start | bytes 196616 | tf_op jit(solution)/shard_map/ppermute | solution.py:71
  58.5 4.9 %collective-permute-start.2 = (f32[64,256]{1,0:T(8,128)S(1)}, f32[64,256]{1,0:T(8,128)S(1)}, u32[]{:S(2)}, u32[]{:S(2)}) collective-permute-start(f32[64,256]{1,0:T(8,128)S(1)} %collective-permute-done.1.first), channel_id=1, source_target_pairs={{0,128},{1,129},{2,130},{3,131},{4,132},{5,133},{6,134},{7,135},{8... | collective-permute-start | bytes 196616 | tf_op jit(solution)/shard_map/ppermute | solution.py:71
  63.5 2.3 %collective-permute-done.2.second = f32[64,256]{1,0:T(8,128)S(1)} collective-permute-done((f32[64,256]{1,0:T(8,128)S(1)}, f32[64,256]{1,0:T(8,128)S(1)}, u32[]{:S(2)}, u32[]{:S(2)}) %collective-permute-start.2) | collective-permute-done | bytes 65568 | tf_op jit(solution)/shard_map/ppermute | solution.py:71
  65.8 0.8 all-to-all-done.shares
  66.6 0.1 collect.1
  66.7 1.9 %collective-permute-start.6 = (f32[2,2,64,256]{3,2,1,0:T(8,128)S(1)}, f32[2,2,64,256]{3,2,1,0:T(8,128)S(1)}, u32[]{:S(2)}, u32[]{:S(2)}) collective-permute-start(f32[2,2,64,256]{3,2,1,0:T(8,128)S(1)} %get-tuple-element.29.block), channel_id=1, source_target_pairs={{0,64},{1,65},{2,66},{3,67},{4,68},{5,69},{6,70},{7,71},{8,72},{9,... | collective-permute-start | bytes 786440 | tf_op jit(solution)/shard_map/ppermute | solution.py:71
  68.6 15.9 %collective-permute-start.5 = (f32[4,16,256]{2,1,0:T(8,128)S(1)}, f32[4,16,256]{2,1,0:T(8,128)S(1)}, u32[]{:S(2)}, u32[]{:S(2)}) collective-permute-start(f32[4,16,256]{2,1,0:T(8,128)S(1)} %get-tuple-element.28.summed), channel_id=1, source_target_pairs={{0,4},{1,5},{2,6},{3,7},{4,0},{5,1},{6,2},{7,3},{8,12},{9,13},{10,... | collective-permute-start | bytes 196616 | tf_op jit(solution)/shard_map/ppermute | solution.py:71
  84.5 7.5 %other.1 = (f32[2,2,512,256]{3,2,1,0:T(8,128)}, f32[2,256,256]{2,1,0:T(8,128)S(1)}) custom-call(s32[4,2]{1,0:T(4,128)S(1)} %copy.8.pos, s32[5]{0:T(128)S(1)} %stack.23.flags, f32[2,256,512]{2,1,0:T(8,128)} %own_hbm.3, f32[2,256,512]{2,1,0:T(8,128)} %copy-done.2, bf16[2,2,2,256,256]{4,3,2,1,0:T(8,128)(2,1)} %constant.51.clone.table_hbm, ...), custom_call_target="tpu_custom_call" | custom-call | tf_op jit(solution)/shard_map/other/pallas_call | solution.py:382
  92.0 0.0 copy-start
  92.0 0.0 copy-start.4
  92.0 1.1 collective-permute-done.5.arrived
  93.2 0.1 change.1
  93.3 23.9 %all_to_all.15.change = f32[16,4,16,256]{3,2,1,0:T(8,128)S(1)} all-to-all(f32[16,4,16,256]{3,2,1,0:T(8,128)S(1)} %change.1), channel_id=1, replica_groups=mesh['zlo'=16,'core'=2,'y'=4,'zhi'=2,'x'=4] {'y','x'}, dimensions={0} | all-to-all | bytes 2097152 | tf_op jit(solution)/shard_map/all_to_all | solution.py:474
  117.2 8.0 %inverse.1 = (f32[16,2,8,512]{3,2,1,0:T(8,128)S(1)}, f32[16,2,8,512]{3,2,1,0:T(8,128)S(1)}) custom-call(s32[4,2]{1,0:T(4,128)S(1)} %copy.8.pos, s32[5]{0:T(128)S(1)} %stack.23.flags, f32[16,4,16,256]{3,2,1,0:T(8,128)S(1)} %all_to_all.15.change, f32[2,2,512,256]{3,2,1,0:T(8,128)S(1)} %copy-done.5, f32[2,2,512,256]{3,2,1,0:T(8,128)} %get-tuple-element.35.far_other_hbm, ...), custom_call_target="tpu_custom_call" | custom-call | tf_op jit(solution)/shard_map/inverse/pallas_call | solution.py:382
  125.2 0.0 collective-permute-start.7
  125.2 9.8 %collective-permute-done.7 = f32[16,2,8,512]{3,2,1,0:T(8,128)S(1)} collective-permute-done((f32[16,2,8,512]{3,2,1,0:T(8,128)S(1)}, f32[16,2,8,512]{3,2,1,0:T(8,128)S(1)}, u32[]{:S(2)}, u32[]{:S(2)}) %collective-permute-start.7) | collective-permute-done | bytes 524320 | tf_op jit(solution)/shard_map/ppermute | solution.py:71
  135.0 0.1 add.30
  135.1 13.0 %all_to_all.16 = f32[16,2,8,512]{3,2,1,0:T(8,128)S(1)} all-to-all(f32[16,2,8,512]{3,2,1,0:T(8,128)S(1)} %add.30), channel_id=1, replica_groups=mesh['zlo'=16,'core'=2,'y'=4,'zhi'=2,'x'=4] {'y','x'}, dimensions={0} | all-to-all | bytes 1048576 | tf_op jit(solution)/shard_map/all_to_all | solution.py:492
  148.2 0.6 multiply_add_fusion
  (15 shorter events, 0.1 us)
Async XLA Ops:
  0.0 39.4 %copy-start.1 = (f32[2,256,512]{2,1,0:T(8,128)S(1)}, f32[2,256,512]{2,1,0:T(8,128)}, u32[]{:S(2)}) copy-start(f32[2,256,512]{2,1,0:T(8,128)} %own_hbm.3) | copy-start | bytes 3145732
  0.0 39.4 %collective-permute-start = (f32[2,256,512]{2,1,0:T(8,128)}, f32[2,256,512]{2,1,0:T(8,128)S(1)}, u32[]{:S(2)}, u32[]{:S(2)}) collective-permute-start(f32[2,256,512]{2,1,0:T(8,128)} %own_hbm.3), channel_id=1, source_target_pairs={{0,996},{1,997},{2,998},{3,999},{4,992},{5,993},{6,994},{7,995},{8... | collective-permute-start | bytes 3145736 | tf_op jit(solution)/shard_map/ppermute | solution.py:71
  17.1 30.1 %collective-permute-start.1 = (f32[64,256]{1,0:T(8,128)S(1)}, f32[64,256]{1,0:T(8,128)S(1)}, u32[]{:S(2)}, u32[]{:S(2)}) collective-permute-start(f32[64,256]{1,0:T(8,128)S(1)} %dynamic-slice_bitcast_fusion), channel_id=1, source_target_pairs={{0,516},{1,517},{2,518},{3,519},{4,512},{5,513},{6,514},{7,515},{8... | collective-permute-start | bytes 196616 | tf_op jit(solution)/shard_map/ppermute | solution.py:71
  26.4 1.2 copy-start.6
  39.4 7.7 %copy-start.2 = (f32[2,256,512]{2,1,0:T(8,128)}, f32[2,256,512]{2,1,0:T(8,128)S(1)}, u32[]{:S(2)}) copy-start(f32[2,256,512]{2,1,0:T(8,128)S(1)} %collective-permute-done.halo.halo_hbm) | copy-start | bytes 3145732
  39.4 1.4 copy-start.3
  47.2 19.4 %all-to-all-start = ((f32[16,4,16,256]{3,2,1,0:T(8,128)}), f32[16,4,16,256]{3,2,1,0:T(8,128)S(1)}, u32[]{:S(2)}, u32[]{:S(2)}) async-start(f32[16,4,16,256]{3,2,1,0:T(8,128)} %get-tuple-element.26), calls=%async_computation | async-start | bytes 2097152 | tf_op jit(solution)/shard_map/all_to_all | solution.py:435
  54.7 8.8 %collective-permute-start.4 = (f32[64,256]{1,0:T(8,128)S(1)}, f32[64,256]{1,0:T(8,128)S(1)}, u32[]{:S(2)}, u32[]{:S(2)}) collective-permute-start(f32[64,256]{1,0:T(8,128)S(1)} %collective-permute-done.1.first), channel_id=1, source_target_pairs={{0,160},{1,161},{2,162},{3,163},{4,164},{5,165},{6,166},{7,167},{8... | collective-permute-start | bytes 196616 | tf_op jit(solution)/shard_map/ppermute | solution.py:71
  56.6 6.9 %collective-permute-start.3 = (f32[64,256]{1,0:T(8,128)S(1)}, f32[64,256]{1,0:T(8,128)S(1)}, u32[]{:S(2)}, u32[]{:S(2)}) collective-permute-start(f32[64,256]{1,0:T(8,128)S(1)} %collective-permute-done.1.first), channel_id=1, source_target_pairs={{0,32},{1,33},{2,34},{3,35},{4,36},{5,37},{6,38},{7,39},{8,40},{9,... | collective-permute-start | bytes 196616 | tf_op jit(solution)/shard_map/ppermute | solution.py:71
  58.5 7.3 %collective-permute-start.2 = (f32[64,256]{1,0:T(8,128)S(1)}, f32[64,256]{1,0:T(8,128)S(1)}, u32[]{:S(2)}, u32[]{:S(2)}) collective-permute-start(f32[64,256]{1,0:T(8,128)S(1)} %collective-permute-done.1.first), channel_id=1, source_target_pairs={{0,128},{1,129},{2,130},{3,131},{4,132},{5,133},{6,134},{7,135},{8... | collective-permute-start | bytes 196616 | tf_op jit(solution)/shard_map/ppermute | solution.py:71
  66.7 17.8 %collective-permute-start.6 = (f32[2,2,64,256]{3,2,1,0:T(8,128)S(1)}, f32[2,2,64,256]{3,2,1,0:T(8,128)S(1)}, u32[]{:S(2)}, u32[]{:S(2)}) collective-permute-start(f32[2,2,64,256]{3,2,1,0:T(8,128)S(1)} %get-tuple-element.29.block), channel_id=1, source_target_pairs={{0,64},{1,65},{2,66},{3,67},{4,68},{5,69},{6,70},{7,71},{8,72},{9,... | collective-permute-start | bytes 786440 | tf_op jit(solution)/shard_map/ppermute | solution.py:71
  68.6 24.6 %collective-permute-start.5 = (f32[4,16,256]{2,1,0:T(8,128)S(1)}, f32[4,16,256]{2,1,0:T(8,128)S(1)}, u32[]{:S(2)}, u32[]{:S(2)}) collective-permute-start(f32[4,16,256]{2,1,0:T(8,128)S(1)} %get-tuple-element.28.summed), channel_id=1, source_target_pairs={{0,4},{1,5},{2,6},{3,7},{4,0},{5,1},{6,2},{7,3},{8,12},{9,13},{10,... | collective-permute-start | bytes 196616 | tf_op jit(solution)/shard_map/ppermute | solution.py:71
  84.5 32.7 %copy-start.5 = (f32[2,2,512,256]{3,2,1,0:T(8,128)S(1)}, f32[2,2,512,256]{3,2,1,0:T(8,128)}, u32[]{:S(2)}) copy-start(f32[2,2,512,256]{3,2,1,0:T(8,128)} %get-tuple-element.34.far_own_hbm) | copy-start | bytes 6291460
  92.0 25.2 %copy-start = (bf16[2,2,2,256,256]{4,3,2,1,0:T(8,128)(2,1)S(1)}, bf16[2,2,2,256,256]{4,3,2,1,0:T(8,128)(2,1)}, u32[]{:S(2)}) copy-start(bf16[2,2,2,256,256]{4,3,2,1,0:T(8,128)(2,1)} %constant.51.clone.table_hbm) | copy-start | bytes 3145732
  92.0 25.2 %copy-start.4 = (f32[1,2,256,256]{3,2,1,0:T(8,128)S(1)}, f32[1,2,256,256]{3,2,1,0:T(8,128)}, u32[]{:S(2)}) copy-start(f32[1,2,256,256]{3,2,1,0:T(8,128)} %param.6) | copy-start | bytes 1572868
  125.2 9.8 %collective-permute-start.7 = (f32[16,2,8,512]{3,2,1,0:T(8,128)S(1)}, f32[16,2,8,512]{3,2,1,0:T(8,128)S(1)}, u32[]{:S(2)}, u32[]{:S(2)}) collective-permute-start(f32[16,2,8,512]{3,2,1,0:T(8,128)S(1)} %get-tuple-element.38), channel_id=1, source_target_pairs={{0,32},{1,33},{2,34},{3,35},{4,36},{5,37},{6,38},{7,39},{8,40},{9,... | collective-permute-start | bytes 1572872 | tf_op jit(solution)/shard_map/ppermute | solution.py:71
